TPU v7x, 32 devices: a whole 2x2x4 slice. The times are simulated.
32 devices in a mesh: ctx: 16 (over z, y, core), mp: 2 (over x).
Axes of the slice: x: 2, y: 2, z: 4, core: 2. Of those that a mesh axis runs over, the one named last changes fastest.
Arguments:
- stream: bfloat16 [4, 65536, 1024], P(None, 'ctx', 'mp'), may hold values from -40 to 40
- gain_mix: bfloat16 [1024], P('mp'), may hold values from 0.25 to 1.75
- proj_in: bfloat16 [8, 128, 384], P('mp'), may hold values from -0.5 to 0.5
- short_taps: float32 [3, 8, 384], P(None, 'mp'), may hold values from -3 to 3
- fwd_inner: bfloat16 [256, 256], replicated, may hold values from -0.375 to 0.375
- twid_inner: float32 [256, 256], P('ctx'), may hold values from -1.5 to 1.5
- fwd_outer: bfloat16 [256, 256], replicated, may hold values from -0.375 to 0.375
- kernel: bfloat16 [256, 256, 1024], P(None, 'ctx', 'mp'), may hold values from -4 to 4
- inv_outer: bfloat16 [256, 256], replicated, may hold values from -0.375 to 0.375
- backward_twiddle: float32 [256, 256], P(None, 'ctx'), may hold values from -1.5 to 1.5
- inv_inner: bfloat16 [256, 256], replicated, may hold values from -0.375 to 0.375
- proj_out: bfloat16 [8, 128, 128], P('mp'), may hold values from -0.5 to 0.5
- gain_mlp: bfloat16 [1024], P('mp'), may hold values from 0.25 to 1.75
- up_blocks: bfloat16 [8, 128, 512], P('mp'), may hold values from -0.5 to 0.5
- down_blocks: bfloat16 [8, 512, 128], P('mp'), may hold values from -0.25 to 0.25
Outputs:
- stream_out: bfloat16 [4, 65536, 1024], P(None, 'ctx', 'mp')
All inputs are finite; a program needn't handle non-finite values.
Results may differ from a plain program's by a relative error of at most 0.0085.
Values may be sent and summed in bfloat16 or wider, within the bound.
No kernel may reach another device: no remote copies, remote signals or barrier semaphores. Data moves between devices by JAX's collectives and lax.ppermute only.
A program may use at most 320 MiB of HBM per device.

v0:
```python
import jax
import jax.numpy as jnp
from jax import lax
from jax.sharding import PartitionSpec as P

D = 1024
NB = 8


epsilon = 1e-05


def from_behind(array, axis, by):
    length = lax.axis_size(axis)
    pairs = [(i, i + by) for i in range(length) if 0 <= i + by < length]
    return lax.ppermute(array, axis, pairs)


def body(
    stream,
    gain_mix,
    proj_in,
    short_taps,
    fwd_inner,
    twid_inner,
    fwd_outer,
    kernel,
    inv_outer,
    backward_twiddle,
    inv_inner,
    proj_out,
    gain_mlp,
    up_blocks,
    down_blocks,
):
    seq_count, tok_count, width_here = stream.shape
    blocks_here, block_width = (proj_in.shape[0], proj_in.shape[1])
    root_len = fwd_inner.shape[0]
    rows_here = twid_inner.shape[0]
    sub_width = block_width // NB
    hid_block = up_blocks.shape[2]
    hid_sub = hid_block // NB
    x_float = stream.astype(jnp.float32)
    sumsq_mix = lax.psum(jnp.sum(x_float * x_float, axis=2), "mp")
    normed = (
        x_float * lax.rsqrt(sumsq_mix[..., None] / D + epsilon) * gain_mix.astype(jnp.float32)
    ).astype(jnp.bfloat16)
    u_blocks = normed.reshape(seq_count, tok_count, blocks_here, block_width)
    projected = jnp.einsum(
        "xtlc,lcd->xtld", u_blocks, proj_in, preferred_element_type=jnp.float32
    ).astype(jnp.bfloat16)
    rim_rows = projected[:, tok_count - 2 :]
    earlier = from_behind(rim_rows, "ctx", 1)
    padded = jnp.concatenate([earlier, projected], axis=1).astype(jnp.float32)
    mixed_all = (
        short_taps[0] * padded[:, 2:]
        + short_taps[1] * padded[:, 1 : tok_count + 1]
        + short_taps[2] * padded[:, :tok_count]
    )
    query_part = mixed_all[..., :block_width].astype(jnp.bfloat16)
    source = (
        mixed_all[..., block_width : 2 * block_width] * mixed_all[..., 2 * block_width :]
    ).astype(jnp.bfloat16)
    lattice = source.reshape(seq_count, rows_here, root_len, blocks_here, block_width)
    opening_segment = (
        jnp.einsum("xablc,bf->xaflc", lattice, fwd_inner, preferred_element_type=jnp.float32)
        * twid_inner[None, :, :, None, None]
    ).astype(jnp.bfloat16)
    kernel_blocks = kernel.reshape(root_len, kernel.shape[1], blocks_here, block_width)
    middle_segment = (
        jnp.einsum(
            "xaflc,ag->xgflc",
            lax.all_to_all(opening_segment, "ctx", split_axis=2, concat_axis=1, tiled=True),
            fwd_outer,
            preferred_element_type=jnp.float32,
        )
        * kernel_blocks[None]
    ).astype(jnp.bfloat16)
    closing_segment = (
        jnp.einsum("xgflc,gh->xhflc", middle_segment, inv_outer, preferred_element_type=jnp.float32)
        * backward_twiddle[None, :, :, None, None]
    ).astype(jnp.bfloat16)
    returned = lax.all_to_all(closing_segment, "ctx", split_axis=1, concat_axis=2, tiled=True)
    convolved = jnp.einsum(
        "xhflc,fe->lcxhe", returned, inv_inner, preferred_element_type=jnp.float32
    ).reshape(blocks_here, block_width, seq_count, tok_count)
    gated_out = (jnp.transpose(query_part, (2, 3, 0, 1)).astype(jnp.float32) * convolved).astype(
        jnp.bfloat16
    )
    spread = gated_out.reshape(blocks_here, NB, sub_width, seq_count, tok_count)
    out_table = proj_out.reshape(blocks_here, NB, sub_width, block_width)
    mix_out = jnp.einsum(
        "ijtxs,jitd->xsjd",
        lax.all_to_all(spread, "mp", split_axis=1, concat_axis=0, tiled=True),
        out_table,
        preferred_element_type=jnp.float32,
    )
    residual = (x_float.reshape(seq_count, tok_count, blocks_here, block_width) + mix_out).astype(
        jnp.bfloat16
    )
    resid_float = residual.astype(jnp.float32)
    sumsq_mlp = lax.psum(jnp.sum(resid_float * resid_float, axis=(2, 3)), "mp")
    gain_here = gain_mlp.astype(jnp.float32).reshape(blocks_here, block_width)
    normed_mlp = (
        resid_float * lax.rsqrt(sumsq_mlp[..., None, None] / D + epsilon) * gain_here
    ).astype(jnp.bfloat16)
    upper_part = jnp.einsum(
        "xslc,lch->lhxs", normed_mlp, up_blocks, preferred_element_type=jnp.float32
    )
    active = (
        jax.nn.gelu(upper_part)
        .astype(jnp.bfloat16)
        .reshape(blocks_here, NB, hid_sub, seq_count, tok_count)
    )
    down_table = down_blocks.reshape(blocks_here, NB, hid_sub, block_width)
    lower_part = jnp.einsum(
        "ijtxs,jitd->xsjd",
        lax.all_to_all(active, "mp", split_axis=1, concat_axis=0, tiled=True),
        down_table,
        preferred_element_type=jnp.float32,
    )
    output = (
        (resid_float + lower_part).astype(jnp.bfloat16).reshape(seq_count, tok_count, width_here)
    )
    return output


def solution(mesh):
    placed = (
        P(None, "ctx", "mp"),
        P("mp"),
        P("mp", None, None),
        P(None, "mp", None),
        P(),
        P("ctx", None),
        P(),
        P(None, "ctx", "mp"),
        P(),
        P(None, "ctx"),
        P(),
        P("mp", None, None),
        P("mp"),
        P("mp", None, None),
        P("mp", None, None),
    )
    return jax.shard_map(
        body, mesh=mesh, in_specs=placed, out_specs=P(None, "ctx", "mp"), check_vma=False
    )
```

profile of v0, /device:TPU:0, one launch (start us, length us, event | category | flops | bytes accessed | tf_op | source)
XLA Modules:
  0.0 2520.5 jit_solution(3733382519255560345)
XLA Ops:
  6.5 21.3 copy.43
  27.8 7.8 multiply_reduce_fusion
  35.6 0.0 all-reduce.3.cloned.1.call-update
  35.6 23.6 all-reduce.3.cloned.1.call-done
  59.2 0.9 add_rsqrt_fusion.1
  60.1 15.7 multiply_convert_fusion.1
  75.8 0.0 copy-done.3
  75.8 24.9 convert_bitcast_fusion
  100.7 0.9 slice.41
  101.6 1.3 collective-permute-start
  102.9 0.0 copy-done.10
  102.9 0.8 collective-permute-done
  103.7 47.6 %maximum_convert_fusion = f32[4,4098,4,384]{3,1,0,2:T(8,128)} fusion(bf16[4,4096,4,384]{3,1,0,2:T(8,128)(2,1)} %convert_bitcast_fusion, bf16[4,2,4,384]{3,1,0,2:T(2,128)(2,1)S(1)} %collective-permute-done), kind=kLoop, calls=%fused_computation.14 | loop fusion | flops 100712448 | bytes 151068672 | tf_op jit(solution)/shard_map/convert_element_type | solution.py:54
  151.3 126.8 %fusion.8 = f32[4,4096,4,384]{3,1,0,2:T(8,128)} fusion(f32[4,4098,4,384]{3,1,0,2:T(8,128)} %maximum_convert_fusion, f32[4,384]{1,0:T(4,128)S(1)} %get-tuple-element.6, f32[4,384]{1,0:T(4,128)S(1)} %get-tuple-element.7, f32[4,384]{1,0:T(4,128)S(1)} %get-tuple-element.5), kind=kLoop, calls=%fused_computation.10 | loop fusion | flops 125829120 | bytes 402671616 | tf_op jit(solution)/shard_map/add | solution.py:56
  278.1 27.7 %fusion.14 = bf16[4,4096,4,128]{3,1,0,2:T(8,128)(2,1)} fusion(f32[4,4096,4,384]{3,1,0,2:T(8,128)} %fusion.8), kind=kLoop, calls=%fused_computation.24 | loop fusion | flops 16777216 | bytes 83886080 | tf_op jit(solution)/shard_map/convert_element_type | solution.py:63
  305.8 0.0 copy-done.6
  305.8 11.5 fusion.19
  317.3 28.0 %copy.46 = bf16[4,16,256,4,128]{4,3,1,0,2:T(4,128)(2,1)} copy(bf16[4,16,256,4,128]{2,4,3,1,0:T(8,128)(2,1)} %fusion.19) | data formatting | bytes 33554432 | tf_op jit(solution)/shard_map/convert_element_type | solution.py:68
  345.2 8.7 all-to-all-start
  353.9 0.2 all-reduce.5.cloned.1.call-start
  354.1 8.6 copy.82
  362.8 287.9 %all-to-all-done = bf16[4,16,256,4,128]{4,3,1,0,2:T(4,128)(2,1)} async-done(((bf16[4,16,256,4,128]{4,3,1,0,2:T(4,128)(2,1)}), bf16[4,16,256,4,128]{4,3,1,0,2:T(4,128)(2,1)}, u32[]{:S(2)}, u32[]{:S(2)}) %all-to-all-start) | async-done | bytes 16777248 | tf_op jit(solution)/shard_map/all_to_all | solution.py:73
  650.7 12.9 copy.47
  663.6 8.5 copy.48
  672.1 19.5 fusion.17
  691.6 28.0 %copy.51 = bf16[4,256,16,4,128]{4,3,2,0,1:T(4,128)(2,1)} copy(bf16[4,256,16,4,128]{1,4,3,2,0:T(8,128)(2,1)} %fusion.17) | data formatting | bytes 33554432 | tf_op jit(solution)/shard_map/convert_element_type | solution.py:82
  719.5 432.1 %all_to_all.72 = bf16[4,256,16,4,128]{4,3,2,0,1:T(4,128)(2,1)S(1)} all-to-all(bf16[4,256,16,4,128]{4,3,2,0,1:T(4,128)(2,1)} %copy.51), channel_id=1, replica_groups=mesh['ctx'=16,'mp'=2] {'ctx'}, dimensions={1} | all-to-all | bytes 33554432 | tf_op jit(solution)/shard_map/all_to_all | solution.py:83
  1151.7 4.2 copy.52
  1155.9 8.1 copy.53
  1164.0 21.4 convolution_bitcast_fusion
  1185.4 32.0 %copy.55 = f32[4,128,4,16,256]{1,4,3,2,0:T(8,128)} copy(f32[4,128,4,16,256]{4,1,0,3,2:T(8,128)} %convolution_bitcast_fusion) | data formatting | bytes 67108864 | tf_op jit(solution)/shard_map/xhflc,fe->lcxhe/transpose | solution.py:84
  1217.4 27.5 %fusion.16 = bf16[4,128,4,4096]{1,3,2,0:T(8,128)(2,1)} fusion(f32[4,128,4,16,256]{1,4,3,2,0:T(8,128)} %copy.55, f32[4,4096,4,384]{3,1,0,2:T(8,128)} %fusion.8), kind=kLoop, calls=%fused_computation.29 | loop fusion | flops 25165824 | bytes 67108864 | tf_op jit(solution)/shard_map/convert_element_type | solution.py:87
  1244.9 21.4 copy.56
  1266.3 8.1 copy.57
  1274.5 0.0 copy-start.9
  1274.5 187.3 %all_to_all.73 = bf16[4,8,16,4,4096]{4,2,3,0,1:T(8,128)(2,1)S(1)} all-to-all(bf16[4,8,16,4,4096]{4,2,3,0,1:T(8,128)(2,1)S(1)} %copy.57), channel_id=1, replica_groups=mesh['ctx'=16,'mp'=2] {'mp'}, dimensions={1} | all-to-all | bytes 33554432 | tf_op jit(solution)/shard_map/all_to_all | solution.py:94
  1461.8 6.5 copy.58
  1468.3 20.7 fusion.10
  1489.0 0.0 all-reduce.5.cloned.1.call-update
  1489.0 21.3 all-reduce.5.cloned.1.call-done
  1510.3 0.9 add_rsqrt_fusion
  1511.2 60.6 %fusion.7 = bf16[4,512,4,4096]{3,1,2,0:T(8,128)(2,1)} fusion(bf16[4,4096,4,128]{1,3,0,2:T(8,128)(2,1)} %get-tuple-element.9, f32[4,128]{1,0:T(4,128)S(1)} %bitcast_convert_fusion, f32[4,4096]{1,0:T(4,128)S(1)} %add_rsqrt_fusion, bf16[4,128,512]{2,1,0:T(8,128)(2,1)S(1)} %copy-done), kind=kOutput, calls=%fused_computation.8 | convolution fusion | flops 8925478912 | bytes 84477952 | tf_op jit(solution)/shard_map/xslc,lch->lhxs/dot_general | solution.py:107
  1571.7 44.3 %copy.62 = bf16[4,8,64,4,4096]{4,2,3,0,1:T(8,128)(2,1)} copy(bf16[4,8,64,4,4096]{4,2,1,3,0:T(8,128)(2,1)} %bitcast.43) | data formatting | bytes 134217728 | tf_op jit(solution)/shard_map/reshape | solution.py:113
  1616.1 782.0 %all_to_all.74 = bf16[4,8,64,4,4096]{4,2,3,0,1:T(8,128)(2,1)} all-to-all(bf16[4,8,64,4,4096]{4,2,3,0,1:T(8,128)(2,1)} %copy.62), channel_id=1, replica_groups=mesh['ctx'=16,'mp'=2] {'mp'}, dimensions={1} | all-to-all | bytes 134217728 | tf_op jit(solution)/shard_map/all_to_all | solution.py:118
  2398.1 44.4 %copy.63 = bf16[4,2,4,64,4,4096]{5,3,0,1,4,2:T(8,128)(2,1)} copy(bf16[4,2,4,64,4,4096]{5,3,4,0,2,1:T(8,128)(2,1)} %bitcast.44) | data formatting | bytes 134217728 | tf_op jit(solution)/shard_map/all_to_all | solution.py:118
  2442.5 36.0 %fusion.13 = bf16[4,4096,4,128]{1,3,0,2:T(8,128)(2,1)} fusion(bf16[4,4096,4,128]{1,3,0,2:T(8,128)(2,1)} %get-tuple-element.9, bf16[8,4,64,4,4096]{4,2,0,3,1:T(8,128)(2,1)} %bitcast.46, bf16[4,8,64,128,1]{3,2,1,4,0:T(8,128)(2,1)S(1)} %bitcast.131), kind=kOutput, calls=%fused_computation.22 | convolution fusion | flops 8615100416 | bytes 101187584 | tf_op jit(solution)/shard_map/ijtxs,jitd->xsjd/dot_general | solution.py:116
  2478.5 14.0 copy.64
  2492.5 21.2 copy.65
  (26 shorter events, 0.1 us)
Async XLA Ops:
  6.5 1504.6 %copy-start = (bf16[4,128,512]{2,1,0:T(8,128)(2,1)S(1)}, bf16[4,128,512]{2,1,0:T(8,128)(2,1)}, u32[]{:S(2)}) copy-start(bf16[4,128,512]{2,1,0:T(8,128)(2,1)} %param.28) | copy-start | bytes 1572868
  6.5 29.1 %copy-start.11 = (bf16[512]{0:T(512)(128)(2,1)S(1)}, bf16[512]{0:T(512)(128)(2,1)}, u32[]{:S(2)}) copy-start(bf16[512]{0:T(512)(128)(2,1)} %param.16) | copy-start | bytes 3076
  6.5 52.7 %all-reduce.3.cloned.1.call-start = ((), (), s32[]{:S(2)}) async-start(), calls=%async_computation.4 | async-start | bytes 131072 | tf_op jit(solution)/shard_map/psum | solution.py:44
  27.8 48.0 %copy-start.3 = (bf16[4,128,384]{2,1,0:T(8,128)(2,1)S(1)}, bf16[4,128,384]{2,1,0:T(8,128)(2,1)}, u32[]{:S(2)}) copy-start(bf16[4,128,384]{2,1,0:T(8,128)(2,1)} %param.17) | copy-start | bytes 1179652
  75.8 27.1 %copy-start.10 = (f32[3,4,384]{2,1,0:T(4,128)S(1)}, f32[3,4,384]{2,1,0:T(4,128)}, u32[]{:S(2)}) copy-start(f32[3,4,384]{2,1,0:T(4,128)} %param.18) | copy-start | bytes 55300
  101.6 2.2 collective-permute-start
  278.1 27.7 %copy-start.4 = (f32[16,256]{1,0:T(8,128)S(1)}, f32[16,256]{1,0:T(8,128)}, u32[]{:S(2)}) copy-start(f32[16,256]{1,0:T(8,128)} %param.20) | copy-start | bytes 49156
  278.1 27.7 %copy-start.6 = (bf16[256,256]{1,0:T(8,128)(2,1)S(1)}, bf16[256,256]{1,0:T(8,128)(2,1)}, u32[]{:S(2)}) copy-start(bf16[256,256]{1,0:T(8,128)(2,1)} %param.19) | copy-start | bytes 393220
  345.2 305.4 %all-to-all-start = ((bf16[4,16,256,4,128]{4,3,1,0,2:T(4,128)(2,1)}), bf16[4,16,256,4,128]{4,3,1,0,2:T(4,128)(2,1)}, u32[]{:S(2)}, u32[]{:S(2)}) async-start(bf16[4,16,256,4,128]{4,3,1,0,2:T(4,128)(2,1)} %copy.46), calls=%async_computation | async-start | bytes 33554432 | tf_op jit(solution)/shard_map/all_to_all | solution.py:73
  353.9 1156.4 %all-reduce.5.cloned.1.call-start = ((), (), s32[]{:S(2)}) async-start(), calls=%async_computation.5 | async-start | bytes 131072 | tf_op jit(solution)/shard_map/psum | solution.py:102
  362.8 309.3 %copy-start.1 = (bf16[256,256]{1,0:T(8,128)(2,1)S(1)}, bf16[256,256]{1,0:T(8,128)(2,1)}, u32[]{:S(2)}) copy-start(bf16[256,256]{1,0:T(8,128)(2,1)} %param.21) | copy-start | bytes 393220
  362.8 309.3 %copy-start.5 = (f32[256,16]{0,1:T(8,128)S(1)}, f32[256,16]{0,1:T(8,128)}, u32[]{:S(2)}) copy-start(f32[256,16]{0,1:T(8,128)} %param.24) | copy-start | bytes 49156
  362.8 309.3 %copy-start.7 = (bf16[256,256]{1,0:T(8,128)(2,1)S(1)}, bf16[256,256]{1,0:T(8,128)(2,1)}, u32[]{:S(2)}) copy-start(bf16[256,256]{1,0:T(8,128)(2,1)} %param.23) | copy-start | bytes 393220
  1151.7 12.4 copy-start.8
  1274.5 193.8 %copy-start.9 = (bf16[4,128,128]{2,1,0:T(8,128)(2,1)S(1)}, bf16[4,128,128]{2,1,0:T(8,128)(2,1)}, u32[]{:S(2)}) copy-start(bf16[4,128,128]{2,1,0:T(8,128)(2,1)} %param.26) | copy-start | bytes 393220
  1468.3 20.7 copy-start.12
  2398.1 44.4 %copy-start.2 = (bf16[4,512,128]{2,1,0:T(8,128)(2,1)S(1)}, bf16[4,512,128]{2,1,0:T(8,128)(2,1)}, u32[]{:S(2)}) copy-start(bf16[4,512,128]{2,1,0:T(8,128)(2,1)} %param.29) | copy-start | bytes 1572868
Sparse Core Ops, SparseCore 0:
  35.7 23.4 all-reduce.2
  1489.1 21.1 all-reduce.4
where the time goes:
time: 2530 us; the launch traced here: 2520 us
  blocking collectives  1400 us (55%)
  waiting for transfers between devices  334 us (13%)
  local copies, waits for them, and re-layouts  312 us (12%)
  other arithmetic  255 us (10%)
  matrix products  195 us (8%)
    all_to_all x1, blocking collectives, body(): lax.all_to_all(active, 'mp', split_axis=1, concat_axis=0, tiled=True)  782 us
    all_to_all x1, blocking collectives, body(): lax.all_to_all(closing_segment, 'ctx', split_axis=1, concat_axis=2, tiled...  432 us
    all_to_all x1, waiting for transfers between devices, body(): lax.all_to_all(opening_segment, 'ctx', split_axis=2, concat_axis=1, tiled...  288 us
    all_to_all x1, blocking collectives, body(): lax.all_to_all(spread, 'mp', split_axis=1, concat_axis=0, tiled=True)  187 us
    add x1, other arithmetic, body(): short_taps[0] * padded[:, 2:] + short_taps[1] * padded[:, 1:tok_count + 1]  127 us
    dot_general x1, matrix products, body(): jnp.einsum('xslc,lch->lhxs', normed_mlp, up_blocks, preferred_element_typ...  60.6 us
  transfers between devices with their start and end apart: 4, of which 4 were waited for; matrix products, arithmetic and copies ran while one was open for 0% of the time, Pallas kernels for 0%

commit v1 on v0

--- a/solution.py
+++ b/solution.py
@@ -1,13 +1,378 @@
+import functools
+
 import jax
 import jax.numpy as jnp
 from jax import lax
+from jax.experimental import pallas as pl
+from jax.experimental.pallas import tpu as pltpu
 from jax.sharding import PartitionSpec as P
 
 D = 1024
 NB = 8
-
-
+ROOT = 256
 epsilon = 1e-05
+
+f32 = jnp.float32
+bf16 = jnp.bfloat16
+VMEM_LIMIT = 56 * 1024 * 1024
+
+
+def params():
+    return pltpu.CompilerParams(vmem_limit_bytes=VMEM_LIMIT)
+
+
+def column(row, width=128):
+    return jnp.broadcast_to(row, (width, row.shape[1])).T
+
+
+def wide(col, width):
+    return jnp.concatenate([col] * (width // 128), axis=1)
+
+
+def mixer_front(x_ref, sums_ref, rim_ref, gain_ref, proj_ref, taps_ref, fwd_ref, twid_ref, *rest):
+    query_ref, *out_refs = rest[:-1]
+    hist = rest[-1]
+    step = pl.program_id(0)
+    blocks, width, triple = proj_ref.shape
+    rows = x_ref.shape[1]
+
+    @pl.when(step == 0)
+    def _():
+        hist[:, 0:8, :] = rim_ref[0]
+
+    scale = wide(column(lax.rsqrt(sums_ref[0] / D + epsilon)), blocks * width)
+    normed = (x_ref[0].astype(f32) * scale * gain_ref[...]).astype(bf16)
+    parts = []
+    for b in range(blocks):
+        proj = jnp.dot(normed[:, b * width : (b + 1) * width], proj_ref[b], preferred_element_type=f32)
+        proj = proj.astype(bf16).astype(f32)
+        hist[b, 8 : 8 + rows, :] = proj
+        mixed = (
+            taps_ref[0, b : b + 1] * proj
+            + taps_ref[1, b : b + 1] * hist[b, 7 : 7 + rows, :]
+            + taps_ref[2, b : b + 1] * hist[b, 6 : 6 + rows, :]
+        )
+        hist[b, 0:8, :] = hist[b, rows : rows + 8, :]
+        query_ref[0, :, b * width : (b + 1) * width] = mixed[:, :width].astype(bf16)
+        parts.append((mixed[:, width : 2 * width] * mixed[:, 2 * width :]).astype(bf16))
+    source = jnp.concatenate(parts, axis=1)
+    first = jnp.dot(fwd_ref[...], source, preferred_element_type=f32)
+    first = (first * wide(column(twid_ref[0]), blocks * width)).astype(bf16)
+    cols = out_refs[0].shape[1]
+    for k, ref in enumerate(out_refs):
+        ref[0] = first[k * cols : (k + 1) * cols]
+
+
+def mixer_middle(count, *refs):
+    ins = refs[:count]
+    fwd_ref, kernel_ref, inv_ref, twid_ref = refs[count : count + 4]
+    outs = refs[count + 4 : 2 * count + 4]
+    held, done = refs[2 * count + 4 :]
+    step = pl.program_id(0)
+    rows, cols, width = ins[0].shape
+    lanes = width // 128
+    root = rows * count
+
+    @pl.when(step == 0)
+    def _():
+        for k in range(count):
+            for l in range(lanes):
+                held[l, k * rows * cols : (k + 1) * rows * cols, :] = (
+                    ins[k][:, :, l * 128 : (l + 1) * 128].astype(f32).reshape(rows * cols, 128)
+                )
+
+    table = jnp.concatenate(
+        [held[l, pl.ds(step, root, stride=cols), :] for l in range(lanes)], axis=1
+    ).astype(bf16)
+    second = jnp.dot(fwd_ref[...], table, preferred_element_type=f32)
+    second = (second * kernel_ref[0].astype(f32)).astype(bf16)
+    third = jnp.dot(inv_ref[...], second, preferred_element_type=f32)
+    third = third * wide(column(twid_ref[0]), width)
+    for l in range(lanes):
+        done[l, pl.ds(step, root, stride=cols), :] = third[:, l * 128 : (l + 1) * 128]
+
+    @pl.when(step == cols - 1)
+    def _():
+        for k in range(count):
+            for l in range(lanes):
+                outs[k][:, :, l * 128 : (l + 1) * 128] = (
+                    done[l, k * rows * cols : (k + 1) * rows * cols, :]
+                    .astype(bf16)
+                    .reshape(rows, cols, 128)
+                )
+
+
+def mixer_back(count, half, pos_ref, *refs):
+    ins = refs[:count]
+    inv_ref, query_ref, send_ref, own_ref = refs[count:]
+    step = pl.program_id(0)
+    table = jnp.concatenate([r[0] for r in ins], axis=0)
+    conv = jnp.dot(inv_ref[...], table, preferred_element_type=f32)
+    gated = (query_ref[0].astype(f32) * conv).astype(bf16)
+
+    @pl.when(step < half)
+    def _():
+        send_ref[...] = gated
+
+    @pl.when(step >= half)
+    def _():
+        own_ref[...] = gated
+
+
+def mlp(pos_ref, own_ref, got_ref, x_own_ref, x_got_ref, mix_ref, gain_ref, up_ref, down_ref, *rest):
+    out_ref, send_ref = rest[-2:]
+    gated = jnp.concatenate([own_ref[...], got_ref[...]], axis=1)
+    width = own_ref.shape[1]
+    mix = jnp.dot(gated, mix_ref[...], preferred_element_type=f32)
+    x = jnp.concatenate([x_own_ref[0], x_got_ref[...]], axis=1).astype(f32)
+    resid = (x + mix).astype(bf16).astype(f32)
+    sums = jnp.sum(resid * resid, axis=1, keepdims=True)
+    normed = (resid * lax.rsqrt(sums / D + epsilon) * gain_ref[...]).astype(bf16)
+    blocks, block, hidden = up_ref.shape
+    acts = []
+    for i in range(blocks):
+        upper = jnp.dot(normed[:, i * block : (i + 1) * block], up_ref[i], preferred_element_type=f32)
+        acts.append(jax.nn.gelu(upper).astype(bf16))
+    pairs, _, span = down_ref.shape
+    for p in range(pairs):
+        act = jnp.concatenate([a[:, p * 128 : (p + 1) * 128] for a in acts], axis=1)
+        low = jnp.dot(act, down_ref[p], preferred_element_type=f32)
+        res = (resid[:, p * span : (p + 1) * span] + low).astype(bf16)
+        if (p + 1) * span <= width:
+            out_ref[0, :, p * span : (p + 1) * span] = res
+        else:
+            send_ref[:, p * span - width : (p + 1) * span - width] = res
+
+
+def place(pos_ref, got_ref, _, out_ref):
+    out_ref[0] = got_ref[...]
+
+
+def body(
+    stream,
+    gain_mix,
+    proj_in,
+    short_taps,
+    fwd_inner,
+    twid_inner,
+    fwd_outer,
+    kernel,
+    inv_outer,
+    backward_twiddle,
+    inv_inner,
+    proj_out,
+    gain_mlp,
+    up_blocks,
+    down_blocks,
+):
+    seqs, toks, width = stream.shape
+    blocks, block = proj_in.shape[:2]
+    root = fwd_inner.shape[0]
+    rows = twid_inner.shape[0]
+    cols = kernel.shape[1]
+    count = lax.axis_size("ctx")
+    sub = block // NB
+    hidden = up_blocks.shape[2]
+    hsub = hidden // NB
+    half = rows // 2
+    me = lax.axis_index("ctx")
+    mp = lax.axis_index("mp")
+    pos = jnp.stack([me, mp]).astype(jnp.int32)
+    swap = [(0, 1), (1, 0)]
+
+    order = me ^ jnp.arange(count)
+
+    def relative(table):
+        return jnp.take(
+            table.reshape(count, root // count, -1), order, axis=0, mode="clip"
+        ).reshape(root, -1)
+
+    fwd_in = relative(fwd_inner.T)
+    twid_in = relative(twid_inner.T).T.reshape(rows, 1, root)
+    fwd_out = relative(fwd_outer).T
+    inv_out = relative(inv_outer.T)
+    twid_out = relative(backward_twiddle).T.reshape(cols, 1, root)
+    inv_in = relative(inv_inner).T
+    kernel_t = jnp.transpose(kernel, (1, 0, 2))
+
+    def sumsq(x):
+        x = x.astype(f32)
+        part = jnp.sum(x * x, axis=-1)
+        return part + lax.ppermute(part, "mp", swap)
+
+    rim = lax.ppermute(stream[:, toks - 2 :], "ctx", [(i, i + 1) for i in range(count - 1)])
+    sums = sumsq(stream).reshape(seqs, rows, 1, root)
+    rim_norm = (
+        rim.astype(f32) * lax.rsqrt(sumsq(rim)[..., None] / D + epsilon) * gain_mix.astype(f32)
+    ).astype(bf16)
+    rim_proj = jnp.einsum(
+        "xtlc,lcd->xltd", rim_norm.reshape(seqs, 2, blocks, block), proj_in, preferred_element_type=f32
+    )
+    rim_proj = jnp.pad(rim_proj.astype(bf16).astype(f32), ((0, 0), (0, 0), (6, 0), (0, 0)))
+    gain_in = gain_mix.astype(f32).reshape(1, width)
+
+    def both(w):
+        got = lax.ppermute(w, "mp", swap)
+        return jnp.concatenate([w, got], axis=0)
+
+    def by_source(w):
+        n = w.shape[1] // 2
+        return jnp.where(mp == 0, w, jnp.roll(w, n, axis=1))
+
+    eye = jnp.eye(NB, dtype=bf16)
+    out_tab = by_source(both(proj_out).reshape(NB, NB, sub, block))
+    place_of = jnp.where(mp == 0, jnp.eye(NB, dtype=bf16), jnp.roll(jnp.eye(NB, dtype=bf16), NB // 2, axis=1))
+    mix_tab = jnp.einsum("rj,ritd->ijtrd", place_of, out_tab).reshape(NB * block, NB * block)
+    gain_out = both(gain_mlp).astype(f32).reshape(1, NB * block)
+    up_tab = both(up_blocks)
+    pair = 2
+    pairs = NB // pair
+    down_tab = by_source(both(down_blocks).reshape(NB, NB, hsub, block))
+    down_tab = jnp.einsum(
+        "pjitd,jk->pijtkd",
+        down_tab.reshape(pairs, pair, NB, hsub, block),
+        jnp.eye(pair, dtype=bf16),
+    ).reshape(pairs, NB * pair * hsub, pair * block)
+    up_tab = jnp.where(mp == 0, up_tab, jnp.roll(up_tab, hidden // 2, axis=2))
+
+    def whole(array):
+        return pl.BlockSpec(array.shape, lambda *_: (0,) * array.ndim)
+
+    def swapped(parts):
+        return [parts[0]] + [
+            lax.ppermute(p, "ctx", [(i, i ^ k) for i in range(count)])
+            for k, p in enumerate(parts)
+            if k > 0
+        ]
+
+    piece = jax.ShapeDtypeStruct((rows, cols, width), bf16)
+
+    def front(s):
+        row_block = pl.BlockSpec((1, root, width), lambda i: (s, i, 0))
+        return pl.pallas_call(
+            mixer_front,
+            grid=(rows,),
+            in_specs=[
+                row_block,
+                pl.BlockSpec((1, 1, root), lambda i: (i, 0, 0)),
+                pl.BlockSpec((1,) + rim_proj.shape[1:], lambda i: (s, 0, 0, 0)),
+                whole(gain_in),
+                whole(proj_in),
+                whole(short_taps),
+                whole(fwd_in),
+                pl.BlockSpec((1, 1, root), lambda i: (i, 0, 0)),
+            ],
+            out_specs=[pl.BlockSpec((1, root, width), lambda i: (0, i, 0))]
+            + [pl.BlockSpec((1, cols, width), lambda i: (i, 0, 0))] * count,
+            out_shape=[jax.ShapeDtypeStruct((1, toks, width), bf16)] + [piece] * count,
+            scratch_shapes=[pltpu.VMEM((blocks, root + 8, 3 * block), f32)],
+            compiler_params=params(),
+            name="mixer_front",
+        )(stream, sums[s], rim_proj, gain_in, proj_in, short_taps, fwd_in, twid_in)
+
+    def middle(parts):
+        full = pl.BlockSpec((rows, cols, width), lambda i: (0, 0, 0))
+        return pl.pallas_call(
+            functools.partial(mixer_middle, count),
+            grid=(cols,),
+            in_specs=[full] * count
+            + [
+                whole(fwd_out),
+                pl.BlockSpec((1, root, width), lambda i: (i, 0, 0)),
+                whole(inv_out),
+                pl.BlockSpec((1, 1, root), lambda i: (i, 0, 0)),
+            ],
+            out_specs=[full] * count,
+            out_shape=[piece] * count,
+            scratch_shapes=[pltpu.VMEM((width // 128, root * cols, 128), f32)] * 2,
+            compiler_params=params(),
+            name="mixer_middle",
+        )(*parts, fwd_out, kernel_t, inv_out, twid_out)
+
+    def back(parts, query):
+        def row(i, pos):
+            return lax.rem(i + half * (1 - pos[1]), rows)
+
+        half_shape = jax.ShapeDtypeStruct((half * root, width), bf16)
+        return pl.pallas_call(
+            functools.partial(mixer_back, count, half),
+            grid_spec=pltpu.PrefetchScalarGridSpec(
+                num_scalar_prefetch=1,
+                grid=(rows,),
+                in_specs=[pl.BlockSpec((1, cols, width), lambda i, pos: (row(i, pos), 0, 0))] * count
+                + [
+                    whole(inv_in),
+                    pl.BlockSpec((1, root, width), lambda i, pos: (0, row(i, pos), 0)),
+                ],
+                out_specs=[
+                    pl.BlockSpec((root, width), lambda i, pos: (jnp.minimum(i, half - 1), 0)),
+                    pl.BlockSpec((root, width), lambda i, pos: (jnp.maximum(i - half, 0), 0)),
+                ],
+            ),
+            out_shape=[half_shape] * 2,
+            compiler_params=params(),
+            name="mixer_back",
+        )(pos, *parts, inv_in, query)
+
+    out_shape = jax.ShapeDtypeStruct(stream.shape, bf16)
+
+    def channels(s, own, got, x_got, out):
+        flat = pl.BlockSpec((root, width), lambda i, pos: (i, 0))
+        mine = pl.BlockSpec((1, root, width), lambda i, pos: (s, pos[1] * half + i, 0))
+        args = [pos, own, got, stream, x_got, mix_tab, gain_out, up_tab, down_tab]
+        specs = [flat, flat, mine, flat, whole(mix_tab), whole(gain_out), whole(up_tab), whole(down_tab)]
+        if out is not None:
+            args.append(out)
+            specs.append(pl.BlockSpec(memory_space=pl.ANY))
+        return pl.pallas_call(
+            mlp,
+            grid_spec=pltpu.PrefetchScalarGridSpec(
+                num_scalar_prefetch=1, grid=(half,), in_specs=specs, out_specs=[mine, flat]
+            ),
+            out_shape=[out_shape, jax.ShapeDtypeStruct((half * root, width), bf16)],
+            input_output_aliases={} if out is None else {9: 0},
+            compiler_params=params(),
+            name="mlp",
+        )(*args)
+
+    def placed(s, got, out):
+        return pl.pallas_call(
+            place,
+            grid_spec=pltpu.PrefetchScalarGridSpec(
+                num_scalar_prefetch=1,
+                grid=(2,),
+                in_specs=[
+                    pl.BlockSpec((half * root // 2, width), lambda i, pos: (i, 0)),
+                    pl.BlockSpec(memory_space=pl.ANY),
+                ],
+                out_specs=pl.BlockSpec(
+                    (1, half * root // 2, width), lambda i, pos: (s, (1 - pos[1]) * 2 + i, 0)
+                ),
+            ),
+            out_shape=out_shape,
+            input_output_aliases={2: 0},
+            compiler_params=params(),
+            name="place",
+        )(pos, got, out)
+
+    queries, firsts, x_gots = [], [], []
+    for s in range(seqs):
+        query, *parts = front(s)
+        queries.append(query)
+        firsts.append(swapped(parts))
+        x_send = lax.dynamic_slice(stream, (s, (1 - mp) * (toks // 2), 0), (1, toks // 2, width))
+        x_gots.append(lax.ppermute(x_send[0], "mp", swap))
+    thirds = [swapped(middle(parts)) for parts in firsts]
+    out = None
+    waiting = []
+    for s in range(seqs):
+        send, own = back(thirds[s], queries[s])
+        got = lax.ppermute(send, "mp", swap)
+        out, send = channels(s, own, got, x_gots[s], out)
+        waiting.append(lax.ppermute(send, "mp", swap))
+        if s >= 1:
+            out = placed(s - 1, waiting[s - 1], out)
+    return placed(seqs - 1, waiting[seqs - 1], out)
 
 
 def from_behind(array, axis, by):
@@ -16,7 +381,7 @@
     return lax.ppermute(array, axis, pairs)
 
 
-def body(
+def plain_body(
     stream,
     gain_mix,
     proj_in,
@@ -143,6 +508,8 @@
         P("mp", None, None),
         P("mp", None, None),
     )
+    sizes = dict(mesh.shape)
+    tiled = ROOT // sizes["ctx"] % 16 == 0 and sizes["mp"] == 2
     return jax.shard_map(
-        body, mesh=mesh, in_specs=placed, out_specs=P(None, "ctx", "mp"), check_vma=False
-    )
+        body if tiled else plain_body, mesh=mesh, in_specs=placed, out_specs=P(None, "ctx", "mp"), check_vma=False
+    )

time: 2530 us -> 1330 us (0.53)
  blocking collectives: 1400 us -> 0 us
  Pallas kernels: 0 us -> 343 us
  starting transfers between devices: 10.2 us -> 353 us
  local copies, waits for them, and re-layouts: 312 us -> 36.3 us
  other arithmetic: 255 us -> 15.7 us
  waiting for transfers between devices: 334 us -> 569 us
  matrix products: 195 us -> 0.24 us
    all_to_all x3 -> x0, blocking collectives: 1400 us -> none  [the longest x1 782 us: body(): lax.all_to_all(active, 'mp', split_axis=1, concat_axis=0, tiled=True)]
    ppermute x1 -> x139, waiting for transfers between devices: 0.81 us -> 569 us  [the longest x120 337 us: swapped(): lax.ppermute(p, 'ctx', [(i, i ^ k) for i in range(count)])]
    ppermute x1 -> x139, starting transfers between devices: 1.32 us -> 353 us  [the longest x120 330 us: swapped(): lax.ppermute(p, 'ctx', [(i, i ^ k) for i in range(count)])]
    pallas_call x0 -> x20, Pallas kernels: none -> 343 us  [the longest x4 106 us: channels(): pl.pallas_call(mlp, grid_spec=pltpu.PrefetchScalarGridSpec(num_scalar_pre...]
    all_to_all x1 -> x0, waiting for transfers between devices: 288 us -> none  [body(): lax.all_to_all(opening_segment, 'ctx', split_axis=2, concat_axis=1, tiled...]
    dot_general x7 -> x1, matrix products: 195 us -> 0.24 us  [body(): jnp.einsum('xtlc,lcd->xltd', rim_norm.reshape(seqs, 2, blocks, block), pr...]
    add x1, other arithmetic: 127 us -> 0.02 us  [sumsq(): return part + lax.ppermute(part, 'mp', swap)]
    convert_element_type x5 -> x3, other arithmetic: 118 us -> 0.61 us  [the longest x1 0.6 us: body(): gain_out = both(gain_mlp).astype(f32).reshape(1, NB * block)]
  transfers between devices with their start and end apart: 4 -> 139, of which waited for: 4 -> 49; matrix products, arithmetic and copies ran while one was open for 0% -> 3% of each run, Pallas kernels for 0% -> 26%
where the time goes in v1:
time: 1330 us; the launch traced here: 1320 us
  waiting for transfers between devices  569 us (43%)
  starting transfers between devices  353 us (27%)
  Pallas kernels  343 us (26%)
  local copies, waits for them, and re-layouts  36.3 us (3%)
  other arithmetic  15.7 us (1%)
    ppermute x120, waiting for transfers between devices, swapped(): lax.ppermute(p, 'ctx', [(i, i ^ k) for i in range(count)])  337 us
    ppermute x120, starting transfers between devices, swapped(): lax.ppermute(p, 'ctx', [(i, i ^ k) for i in range(count)])  330 us
    ppermute x4, waiting for transfers between devices, body(): got = lax.ppermute(send, 'mp', swap)  132 us
    pallas_call x4, Pallas kernels, channels(): pl.pallas_call(mlp, grid_spec=pltpu.PrefetchScalarGridSpec(num_scalar_pre...  106 us
    pallas_call x4, Pallas kernels, middle(): pl.pallas_call(functools.partial(mixer_middle, count), grid=(cols,), in_s...  84.1 us
    pallas_call x4, Pallas kernels, front(): pl.pallas_call(mixer_front, grid=(rows,), in_specs=[row_block, pl.BlockSp...  80.1 us
    ppermute x4, waiting for transfers between devices, body(): waiting.append(lax.ppermute(send, 'mp', swap))  73.8 us
    pallas_call x4, Pallas kernels, back(): pl.pallas_call(functools.partial(mixer_back, count, half), grid_spec=pltp...  59.9 us
  transfers between devices with their start and end apart: 139, of which 49 were waited for; matrix products, arithmetic and copies ran while one was open for 3% of the time, Pallas kernels for 26%

profile of v1, /device:TPU:0, one launch (start us, length us, event | category | flops | bytes accessed | tf_op | source)
XLA Modules:
  0.0 1320.0 jit_solution(1011443807707082778)
XLA Ops:
  3.4 7.2 multiply_reduce_fusion
  23.1 19.9 %mixer_front.6 = (bf16[1,4096,512]{2,1,0:T(8,128)(2,1)}, bf16[16,16,512]{2,1,0:T(8,128)(2,1)}, bf16[16,16,512]{2,1,0:T(8,128)(2,1)}, bf16[16,16,512]{2,1,0:T(8,1...) custom-call(bf16[4,4096,512]{2,1,0:T(8,128)(2,1)} %x_own_ref.7, ...), custom_call_target="tpu_custom_call" | custom-call | tf_op jit(solution)/shard_map/mixer_front/pallas_call | solution.py:252
  63.9 14.0 %collective-permute-done.76.refs_6_ = bf16[16,16,512]{2,1,0:T(8,128)(2,1)} collective-permute-done((bf16[16,16,512]{2,1,0:T(8,128)(2,1)}, bf16[16,16,512]{2,1,0:T(8,128)(2,1)}, u32[]{:S(2)}, u32[]{:S(2)}) %collective-permute-start.76) | collective-permute-done | bytes 262176 | tf_op jit(solution)/shard_map/ppermute | solution.py:243
  85.9 25.2 %collective-permute-start.84 = (bf16[16,16,512]{2,1,0:T(8,128)(2,1)}, bf16[16,16,512]{2,1,0:T(8,128)(2,1)S(1)}, u32[]{:S(2)}, u32[]{:S(2)}) collective-permute-start(bf16[16,16,512]{2,1,0:T(8,128)(2,1)} %get-tuple-element.237), channel_id=1, source_target_pairs={{0,28},{2,30},{4,24},{6,26},{8,20},{10,22},{12,16},{14,18},{16,12}... | collective-permute-start | bytes 786440 | tf_op jit(solution)/shard_map/ppermute | solution.py:243
  111.1 8.3 collective-permute-done.80.refs_10_
  119.4 20.0 %mixer_front.5 = (bf16[1,4096,512]{2,1,0:T(8,128)(2,1)}, bf16[16,16,512]{2,1,0:T(8,128)(2,1)}, bf16[16,16,512]{2,1,0:T(8,128)(2,1)}, bf16[16,16,512]{2,1,0:T(8,1...) custom-call(bf16[4,4096,512]{2,1,0:T(8,128)(2,1)} %x_own_ref.7, ...), custom_call_target="tpu_custom_call" | custom-call | tf_op jit(solution)/shard_map/mixer_front/pallas_call | solution.py:252
  158.5 19.3 %collective-permute-start.46 = (bf16[16,16,512]{2,1,0:T(8,128)(2,1)}, bf16[16,16,512]{2,1,0:T(8,128)(2,1)}, u32[]{:S(2)}, u32[]{:S(2)}) collective-permute-start(bf16[16,16,512]{2,1,0:T(8,128)(2,1)} %get-tuple-element.196), channel_id=1, source_target_pairs={{0,16},{2,18},{4,20},{6,22},{8,24},{10,26},{12,28},{14,30},{16,0},... | collective-permute-start | bytes 786440 | tf_op jit(solution)/shard_map/ppermute | solution.py:243
  181.4 31.4 %collective-permute-done.46.refs_8_ = bf16[16,16,512]{2,1,0:T(8,128)(2,1)} collective-permute-done((bf16[16,16,512]{2,1,0:T(8,128)(2,1)}, bf16[16,16,512]{2,1,0:T(8,128)(2,1)}, u32[]{:S(2)}, u32[]{:S(2)}) %collective-permute-start.46) | collective-permute-done | bytes 262176 | tf_op jit(solution)/shard_map/ppermute | solution.py:243
  212.8 11.1 collective-permute-done.47.refs_9_
  235.6 20.0 %mixer_front.7 = (bf16[1,4096,512]{2,1,0:T(8,128)(2,1)}, bf16[16,16,512]{2,1,0:T(8,128)(2,1)}, bf16[16,16,512]{2,1,0:T(8,128)(2,1)}, bf16[16,16,512]{2,1,0:T(8,1...) custom-call(bf16[4,4096,512]{2,1,0:T(8,128)(2,1)} %x_own_ref.7, ...), custom_call_target="tpu_custom_call" | custom-call | tf_op jit(solution)/shard_map/mixer_front/pallas_call | solution.py:252
  275.6 15.0 %collective-permute-start.111 = (bf16[16,16,512]{2,1,0:T(8,128)(2,1)}, bf16[16,16,512]{2,1,0:T(8,128)(2,1)S(1)}, u32[]{:S(2)}, u32[]{:S(2)}) collective-permute-start(bf16[16,16,512]{2,1,0:T(8,128)(2,1)} %get-tuple-element.268), channel_id=1, source_target_pairs={{0,16},{2,18},{4,20},{6,22},{8,24},{10,26},{12,28},{14,30},{16,0},... | collective-permute-start | bytes 786440 | tf_op jit(solution)/shard_map/ppermute | solution.py:243
  297.8 28.2 %collective-permute-done.111.refs_8_ = bf16[16,16,512]{2,1,0:T(8,128)(2,1)S(1)} collective-permute-done((bf16[16,16,512]{2,1,0:T(8,128)(2,1)}, bf16[16,16,512]{2,1,0:T(8,128)(2,1)S(1)}, u32[]{:S(2)}, u32[]{:S(2)}) %collective-permute-start.111) | collective-permute-done | bytes 262176 | tf_op jit(solution)/shard_map/ppermute | solution.py:243
  330.6 10.5 collective-permute-start.117
  341.1 8.3 collective-permute-done.113.refs_10_
  350.1 20.2 %mixer_front.4 = (bf16[1,4096,512]{2,1,0:T(8,128)(2,1)}, bf16[16,16,512]{2,1,0:T(8,128)(2,1)}, bf16[16,16,512]{2,1,0:T(8,128)(2,1)}, bf16[16,16,512]{2,1,0:T(8,1...) custom-call(bf16[4,4096,512]{2,1,0:T(8,128)(2,1)} %x_own_ref.7, ...), custom_call_target="tpu_custom_call" | custom-call | tf_op jit(solution)/shard_map/mixer_front/pallas_call | solution.py:252
  378.0 18.0 %collective-permute-start.13 = (bf16[16,16,512]{2,1,0:T(8,128)(2,1)}, bf16[16,16,512]{2,1,0:T(8,128)(2,1)S(1)}, u32[]{:S(2)}, u32[]{:S(2)}) collective-permute-start(bf16[16,16,512]{2,1,0:T(8,128)(2,1)} %get-tuple-element.164), channel_id=1, source_target_pairs={{0,22},{2,20},{4,18},{6,16},{8,30},{10,28},{12,26},{14,24},{16,6},... | collective-permute-start | bytes 786440 | tf_op jit(solution)/shard_map/ppermute | solution.py:243
  396.7 19.2 %collective-permute-done.10.refs_8_ = bf16[16,16,512]{2,1,0:T(8,128)(2,1)S(1)} collective-permute-done((bf16[16,16,512]{2,1,0:T(8,128)(2,1)}, bf16[16,16,512]{2,1,0:T(8,128)(2,1)S(1)}, u32[]{:S(2)}, u32[]{:S(2)}) %collective-permute-start.10) | collective-permute-done | bytes 262176 | tf_op jit(solution)/shard_map/ppermute | solution.py:243
  420.5 10.5 collective-permute-start.16
  431.0 8.3 collective-permute-done.12.refs_10_
  451.8 16.2 %collective-permute-start.6 = (bf16[16,16,512]{2,1,0:T(8,128)(2,1)}, bf16[16,16,512]{2,1,0:T(8,128)(2,1)}, u32[]{:S(2)}, u32[]{:S(2)}) collective-permute-start(bf16[16,16,512]{2,1,0:T(8,128)(2,1)} %get-tuple-element.157), channel_id=1, source_target_pairs={{0,8},{2,10},{4,12},{6,14},{8,0},{10,2},{12,4},{14,6},{16,24},{18,... | collective-permute-start | bytes 786440 | tf_op jit(solution)/shard_map/ppermute | solution.py:243
  491.2 21.0 %mixer_middle.6 = (bf16[16,16,512]{2,1,0:T(8,128)(2,1)}, bf16[16,16,512]{2,1,0:T(8,128)(2,1)}, bf16[16,16,512]{2,1,0:T(8,128)(2,1)}, bf16[16,16,512]{2,1,0:T(8,1...) custom-call(bf16[16,16,512]{2,1,0:T(8,128)(2,1)} %get-tuple-element., ...), custom_call_target="tpu_custom_call" | custom-call | tf_op jit(solution)/shard_map/mixer_middle/pallas_call | solution.py:275
  537.9 7.0 dynamic-slice_bitcast_fusion
  545.0 21.0 %mixer_middle.5 = (bf16[16,16,512]{2,1,0:T(8,128)(2,1)}, bf16[16,16,512]{2,1,0:T(8,128)(2,1)}, bf16[16,16,512]{2,1,0:T(8,128)(2,1)}, bf16[16,16,512]{2,1,0:T(8,1...) custom-call(bf16[16,16,512]{2,1,0:T(8,128)(2,1)} %get-tuple-element., ...), custom_call_target="tpu_custom_call" | custom-call | tf_op jit(solution)/shard_map/mixer_middle/pallas_call | solution.py:275
  574.7 21.2 %collective-permute-done.95.refs_10_ = bf16[16,16,512]{2,1,0:T(8,128)(2,1)} collective-permute-done((bf16[16,16,512]{2,1,0:T(8,128)(2,1)}, bf16[16,16,512]{2,1,0:T(8,128)(2,1)}, u32[]{:S(2)}, u32[]{:S(2)}) %collective-permute-start.95) | collective-permute-done | bytes 262176 | tf_op jit(solution)/shard_map/ppermute | solution.py:243
  602.6 9.1 collective-permute-start.57
  624.0 13.9 %collective-permute-start.63 = (bf16[16,16,512]{2,1,0:T(8,128)(2,1)}, bf16[16,16,512]{2,1,0:T(8,128)(2,1)}, u32[]{:S(2)}, u32[]{:S(2)}) collective-permute-start(bf16[16,16,512]{2,1,0:T(8,128)(2,1)} %get-tuple-element.214), channel_id=1, source_target_pairs={{0,20},{2,22},{4,16},{6,18},{8,28},{10,30},{12,24},{14,26},{16,4},... | collective-permute-start | bytes 786440 | tf_op jit(solution)/shard_map/ppermute | solution.py:243
  648.2 15.2 %mixer_back.6 = (bf16[2048,512]{1,0:T(8,128)(2,1)}, bf16[2048,512]{1,0:T(8,128)(2,1)}) custom-call(s32[2]{0:T(128)} %pad_add_fusion.pos_ref, bf16[16,16,512]{2,1,0:T(8,128)(2,1)} %get-tuple-element.239.refs_0_, bf16[16,16,512]{2,1,0:T(8,128)(2,1)} %copy-done.68, bf16[16,16,512]{2,1,0:T(8,128)(2,1)} %copy-done.71, bf16[16,16,512]{2,1,0:T(8,128)(2,1)} %copy-done.72, ...), custom_call_target="tpu_custom_call" | custom-call | tf_op jit(solution)/shard_map/mixer_back/pallas_call | solution.py:297
  669.0 20.9 %collective-permute-done.64.refs_11_ = bf16[16,16,512]{2,1,0:T(8,128)(2,1)} collective-permute-done((bf16[16,16,512]{2,1,0:T(8,128)(2,1)}, bf16[16,16,512]{2,1,0:T(8,128)(2,1)}, u32[]{:S(2)}, u32[]{:S(2)}) %collective-permute-start.64) | collective-permute-done | bytes 262176 | tf_op jit(solution)/shard_map/ppermute | solution.py:243
  690.7 20.9 %mixer_middle.7 = (bf16[16,16,512]{2,1,0:T(8,128)(2,1)}, bf16[16,16,512]{2,1,0:T(8,128)(2,1)}, bf16[16,16,512]{2,1,0:T(8,128)(2,1)}, bf16[16,16,512]{2,1,0:T(8,1...) custom-call(bf16[16,16,512]{2,1,0:T(8,128)(2,1)} %get-tuple-element., ...), custom_call_target="tpu_custom_call" | custom-call | tf_op jit(solution)/shard_map/mixer_middle/pallas_call | solution.py:275
  758.8 14.9 %mixer_back.5 = (bf16[2048,512]{1,0:T(8,128)(2,1)}, bf16[2048,512]{1,0:T(8,128)(2,1)}) custom-call(s32[2]{0:T(128)} %pad_add_fusion.pos_ref, bf16[16,16,512]{2,1,0:T(8,128)(2,1)} %get-tuple-element.204.refs_0_, bf16[16,16,512]{2,1,0:T(8,128)(2,1)} %copy-done.54, bf16[16,16,512]{2,1,0:T(8,128)(2,1)} %copy-done.57, bf16[16,16,512]{2,1,0:T(8,128)(2,1)} %copy-done.58, ...), custom_call_target="tpu_custom_call" | custom-call | tf_op jit(solution)/shard_map/mixer_back/pallas_call | solution.py:297
  792.0 14.3 %collective-permute-start.132 = (bf16[16,16,512]{2,1,0:T(8,128)(2,1)}, bf16[16,16,512]{2,1,0:T(8,128)(2,1)}, u32[]{:S(2)}, u32[]{:S(2)}) collective-permute-start(bf16[16,16,512]{2,1,0:T(8,128)(2,1)} %get-tuple-element.290), channel_id=1, source_target_pairs={{0,28},{2,30},{4,24},{6,26},{8,20},{10,22},{12,16},{14,18},{16,12}... | collective-permute-start | bytes 786440 | tf_op jit(solution)/shard_map/ppermute | solution.py:243
  811.7 26.3 %mlp.4 = (bf16[4,4096,512]{2,1,0:T(8,128)(2,1)}, bf16[2048,512]{1,0:T(8,128)(2,1)}) custom-call(s32[2]{0:T(128)} %pad_add_fusion.pos_ref, bf16[2048,512]{1,0:T(8,128)(2,1)} %get-tuple-element.256.own_ref, bf16[2048,512]{1,0:T(8,128)(2,1)} %collective-permute-done.101.got_ref, bf16[4,4096,512]{2,1,0:T(8,128)(2,1)} %x_own_ref.7, ...), custom_call_target="tpu_custom_call" | custom-call | tf_op jit(solution)/shard_map/mlp/pallas_call | solution.py:327
  838.6 21.2 %mixer_middle.4 = (bf16[16,16,512]{2,1,0:T(8,128)(2,1)}, bf16[16,16,512]{2,1,0:T(8,128)(2,1)}, bf16[16,16,512]{2,1,0:T(8,128)(2,1)}, bf16[16,16,512]{2,1,0:T(8,1...) custom-call(bf16[16,16,512]{2,1,0:T(8,128)(2,1)} %get-tuple-element., ...), custom_call_target="tpu_custom_call" | custom-call | tf_op jit(solution)/shard_map/mixer_middle/pallas_call | solution.py:275
  860.1 10.9 collective-permute-done.133.refs_15_
  872.2 8.2 collective-permute-done.19.refs_2_
  906.5 14.1 %collective-permute-done.25.refs_8_ = bf16[16,16,512]{2,1,0:T(8,128)(2,1)S(1)} collective-permute-done((bf16[16,16,512]{2,1,0:T(8,128)(2,1)}, bf16[16,16,512]{2,1,0:T(8,128)(2,1)S(1)}, u32[]{:S(2)}, u32[]{:S(2)}) %collective-permute-start.25) | collective-permute-done | bytes 262176 | tf_op jit(solution)/shard_map/ppermute | solution.py:243
  921.5 24.4 %collective-permute-done.27.refs_10_ = bf16[16,16,512]{2,1,0:T(8,128)(2,1)S(1)} collective-permute-done((bf16[16,16,512]{2,1,0:T(8,128)(2,1)}, bf16[16,16,512]{2,1,0:T(8,128)(2,1)S(1)}, u32[]{:S(2)}, u32[]{:S(2)}) %collective-permute-start.27) | collective-permute-done | bytes 262176 | tf_op jit(solution)/shard_map/ppermute | solution.py:243
  956.1 14.9 %mixer_back.7 = (bf16[2048,512]{1,0:T(8,128)(2,1)}, bf16[2048,512]{1,0:T(8,128)(2,1)}) custom-call(s32[2]{0:T(128)} %pad_add_fusion.pos_ref, bf16[16,16,512]{2,1,0:T(8,128)(2,1)} %get-tuple-element.276.refs_0_, bf16[16,16,512]{2,1,0:T(8,128)(2,1)} %copy-done.51, bf16[16,16,512]{2,1,0:T(8,128)(2,1)} %copy-done.52, bf16[16,16,512]{2,1,0:T(8,128)(2,1)} %copy-done.53, ...), custom_call_target="tpu_custom_call" | custom-call | tf_op jit(solution)/shard_map/mixer_back/pallas_call | solution.py:297
  971.1 26.8 %mlp.5 = (bf16[4,4096,512]{2,1,0:T(8,128)(2,1)}, bf16[2048,512]{1,0:T(8,128)(2,1)}) custom-call(s32[2]{0:T(128)} %pad_add_fusion.pos_ref, bf16[2048,512]{1,0:T(8,128)(2,1)} %get-tuple-element.221.own_ref, bf16[2048,512]{1,0:T(8,128)(2,1)} %collective-permute-done.69.got_ref, bf16[4,4096,512]{2,1,0:T(8,128)(2,1)} %x_own_ref.7, ...), custom_call_target="tpu_custom_call", output_to_operand_aliasing={{0}: (9, {})} | custom-call | tf_op jit(solution)/shard_map/mlp/pallas_call | solution.py:327
  1002.0 14.9 %mixer_back.4 = (bf16[2048,512]{1,0:T(8,128)(2,1)}, bf16[2048,512]{1,0:T(8,128)(2,1)}) custom-call(s32[2]{0:T(128)} %pad_add_fusion.pos_ref, bf16[16,16,512]{2,1,0:T(8,128)(2,1)} %get-tuple-element.169.refs_0_, bf16[16,16,512]{2,1,0:T(8,128)(2,1)} %copy-done.78, bf16[16,16,512]{2,1,0:T(8,128)(2,1)} %copy-done.79, bf16[16,16,512]{2,1,0:T(8,128)(2,1)} %copy-done.80, ...), custom_call_target="tpu_custom_call" | custom-call | tf_op jit(solution)/shard_map/mixer_back/pallas_call | solution.py:297
  1022.0 23.2 %collective-permute-done.135.x_got_ref = bf16[2048,512]{1,0:T(8,128)(2,1)} collective-permute-done((bf16[2048,512]{1,0:T(8,128)(2,1)S(1)}, bf16[2048,512]{1,0:T(8,128)(2,1)}, u32[]{:S(2)}, u32[]{:S(2)}) %collective-permute-start.135) | collective-permute-done | bytes 2097184 | tf_op jit(solution)/shard_map/ppermute | solution.py:364
  1045.2 89.9 %collective-permute-done.134.got_ref = bf16[2048,512]{1,0:T(8,128)(2,1)} collective-permute-done((bf16[2048,512]{1,0:T(8,128)(2,1)}, bf16[2048,512]{1,0:T(8,128)(2,1)}, u32[]{:S(2)}, u32[]{:S(2)}) %collective-permute-start.134) | collective-permute-done | bytes 2097184 | tf_op jit(solution)/shard_map/ppermute | solution.py:370
  1135.1 26.3 %mlp.6 = (bf16[4,4096,512]{2,1,0:T(8,128)(2,1)}, bf16[2048,512]{1,0:T(8,128)(2,1)}) custom-call(s32[2]{0:T(128)} %pad_add_fusion.pos_ref, bf16[2048,512]{1,0:T(8,128)(2,1)} %get-tuple-element.293.own_ref, bf16[2048,512]{1,0:T(8,128)(2,1)} %collective-permute-done.134.got_ref, bf16[4,4096,512]{2,1,0:T(8,128)(2,1)} %x_own_ref.7, ...), custom_call_target="tpu_custom_call", output_to_operand_aliasing={{0}: (9, {})} | custom-call | tf_op jit(solution)/shard_map/mlp/pallas_call | solution.py:327
  1163.1 16.9 %collective-permute-done.103.got_ref = bf16[2048,512]{1,0:T(8,128)(2,1)} collective-permute-done((bf16[2048,512]{1,0:T(8,128)(2,1)}, bf16[2048,512]{1,0:T(8,128)(2,1)}, u32[]{:S(2)}, u32[]{:S(2)}) %collective-permute-start.103) | collective-permute-done | bytes 2097184 | tf_op jit(solution)/shard_map/ppermute | solution.py:372
  1183.3 41.7 %collective-permute-done.33.got_ref = bf16[2048,512]{1,0:T(8,128)(2,1)} collective-permute-done((bf16[2048,512]{1,0:T(8,128)(2,1)}, bf16[2048,512]{1,0:T(8,128)(2,1)}, u32[]{:S(2)}, u32[]{:S(2)}) %collective-permute-start.33) | collective-permute-done | bytes 2097184 | tf_op jit(solution)/shard_map/ppermute | solution.py:370
  1224.9 26.6 %mlp.7 = (bf16[4,4096,512]{2,1,0:T(8,128)(2,1)}, bf16[2048,512]{1,0:T(8,128)(2,1)}) custom-call(s32[2]{0:T(128)} %pad_add_fusion.pos_ref, bf16[2048,512]{1,0:T(8,128)(2,1)} %get-tuple-element.186.own_ref, bf16[2048,512]{1,0:T(8,128)(2,1)} %collective-permute-done.33.got_ref, bf16[4,4096,512]{2,1,0:T(8,128)(2,1)} %x_own_ref.7, ...), custom_call_target="tpu_custom_call", output_to_operand_aliasing={{0}: (9, {})} | custom-call | tf_op jit(solution)/shard_map/mlp/pallas_call | solution.py:327
  1253.2 16.5 %collective-permute-done.138.got_ref = bf16[2048,512]{1,0:T(8,128)(2,1)S(1)} collective-permute-done((bf16[2048,512]{1,0:T(8,128)(2,1)}, bf16[2048,512]{1,0:T(8,128)(2,1)S(1)}, u32[]{:S(2)}, u32[]{:S(2)}) %collective-permute-start.138) | collective-permute-done | bytes 2097184 | tf_op jit(solution)/shard_map/ppermute | solution.py:372
  1274.4 40.3 %collective-permute-done.137.got_ref = bf16[2048,512]{1,0:T(8,128)(2,1)S(1)} collective-permute-done((bf16[2048,512]{1,0:T(8,128)(2,1)}, bf16[2048,512]{1,0:T(8,128)(2,1)S(1)}, u32[]{:S(2)}, u32[]{:S(2)}) %collective-permute-start.137) | collective-permute-done | bytes 2097184 | tf_op jit(solution)/shard_map/ppermute | solution.py:372
  (546 shorter events, 364.7 us)
Async XLA Ops:
  60.3 59.1 %collective-permute-start.80 = (bf16[16,16,512]{2,1,0:T(8,128)(2,1)}, bf16[16,16,512]{2,1,0:T(8,128)(2,1)}, u32[]{:S(2)}, u32[]{:S(2)}) collective-permute-start(bf16[16,16,512]{2,1,0:T(8,128)(2,1)} %get-tuple-element.233), channel_id=1, source_target_pairs={{0,20},{2,22},{4,16},{6,18},{8,28},{10,30},{12,24},{14,26},{16,4},... | collective-permute-start | bytes 786440 | tf_op jit(solution)/shard_map/ppermute | solution.py:243
  77.9 61.4 %collective-permute-start.81 = (bf16[16,16,512]{2,1,0:T(8,128)(2,1)}, bf16[16,16,512]{2,1,0:T(8,128)(2,1)S(1)}, u32[]{:S(2)}, u32[]{:S(2)}) collective-permute-start(bf16[16,16,512]{2,1,0:T(8,128)(2,1)} %get-tuple-element.234), channel_id=1, source_target_pairs={{0,22},{2,20},{4,18},{6,16},{8,30},{10,28},{12,26},{14,24},{16,6},... | collective-permute-start | bytes 786440 | tf_op jit(solution)/shard_map/ppermute | solution.py:243
  82.4 57.1 %collective-permute-start.82 = (bf16[16,16,512]{2,1,0:T(8,128)(2,1)}, bf16[16,16,512]{2,1,0:T(8,128)(2,1)S(1)}, u32[]{:S(2)}, u32[]{:S(2)}) collective-permute-start(bf16[16,16,512]{2,1,0:T(8,128)(2,1)} %get-tuple-element.235), channel_id=1, source_target_pairs={{0,24},{2,26},{4,28},{6,30},{8,16},{10,18},{12,20},{14,22},{16,8},... | collective-permute-start | bytes 786440 | tf_op jit(solution)/shard_map/ppermute | solution.py:243
  83.7 60.9 %collective-permute-start.83 = (bf16[16,16,512]{2,1,0:T(8,128)(2,1)}, bf16[16,16,512]{2,1,0:T(8,128)(2,1)S(1)}, u32[]{:S(2)}, u32[]{:S(2)}) collective-permute-start(bf16[16,16,512]{2,1,0:T(8,128)(2,1)} %get-tuple-element.236), channel_id=1, source_target_pairs={{0,26},{2,24},{4,30},{6,28},{8,18},{10,16},{12,22},{14,20},{16,10}... | collective-permute-start | bytes 786440 | tf_op jit(solution)/shard_map/ppermute | solution.py:243
  85.9 58.7 %collective-permute-start.84 = (bf16[16,16,512]{2,1,0:T(8,128)(2,1)}, bf16[16,16,512]{2,1,0:T(8,128)(2,1)S(1)}, u32[]{:S(2)}, u32[]{:S(2)}) collective-permute-start(bf16[16,16,512]{2,1,0:T(8,128)(2,1)} %get-tuple-element.237), channel_id=1, source_target_pairs={{0,28},{2,30},{4,24},{6,26},{8,20},{10,22},{12,16},{14,18},{16,12}... | collective-permute-start | bytes 786440 | tf_op jit(solution)/shard_map/ppermute | solution.py:243
  158.5 54.3 %collective-permute-start.46 = (bf16[16,16,512]{2,1,0:T(8,128)(2,1)}, bf16[16,16,512]{2,1,0:T(8,128)(2,1)}, u32[]{:S(2)}, u32[]{:S(2)}) collective-permute-start(bf16[16,16,512]{2,1,0:T(8,128)(2,1)} %get-tuple-element.196), channel_id=1, source_target_pairs={{0,16},{2,18},{4,20},{6,22},{8,24},{10,26},{12,28},{14,30},{16,0},... | collective-permute-start | bytes 786440 | tf_op jit(solution)/shard_map/ppermute | solution.py:243
  177.9 46.1 %collective-permute-start.47 = (bf16[16,16,512]{2,1,0:T(8,128)(2,1)}, bf16[16,16,512]{2,1,0:T(8,128)(2,1)}, u32[]{:S(2)}, u32[]{:S(2)}) collective-permute-start(bf16[16,16,512]{2,1,0:T(8,128)(2,1)} %get-tuple-element.197), channel_id=1, source_target_pairs={{0,18},{2,16},{4,22},{6,20},{8,26},{10,24},{12,30},{14,28},{16,2},... | collective-permute-start | bytes 786440 | tf_op jit(solution)/shard_map/ppermute | solution.py:243
  177.9 51.7 %collective-permute-start.48 = (bf16[16,16,512]{2,1,0:T(8,128)(2,1)}, bf16[16,16,512]{2,1,0:T(8,128)(2,1)}, u32[]{:S(2)}, u32[]{:S(2)}) collective-permute-start(bf16[16,16,512]{2,1,0:T(8,128)(2,1)} %get-tuple-element.198), channel_id=1, source_target_pairs={{0,20},{2,22},{4,16},{6,18},{8,28},{10,30},{12,24},{14,26},{16,4},... | collective-permute-start | bytes 786440 | tf_op jit(solution)/shard_map/ppermute | solution.py:243
  180.2 75.5 %collective-permute-start.49 = (bf16[16,16,512]{2,1,0:T(8,128)(2,1)}, bf16[16,16,512]{2,1,0:T(8,128)(2,1)S(1)}, u32[]{:S(2)}, u32[]{:S(2)}) collective-permute-start(bf16[16,16,512]{2,1,0:T(8,128)(2,1)} %get-tuple-element.199), channel_id=1, source_target_pairs={{0,22},{2,20},{4,18},{6,16},{8,30},{10,28},{12,26},{14,24},{16,6},... | collective-permute-start | bytes 786440 | tf_op jit(solution)/shard_map/ppermute | solution.py:243
  181.2 76.0 %collective-permute-start.50 = (bf16[16,16,512]{2,1,0:T(8,128)(2,1)}, bf16[16,16,512]{2,1,0:T(8,128)(2,1)S(1)}, u32[]{:S(2)}, u32[]{:S(2)}) collective-permute-start(bf16[16,16,512]{2,1,0:T(8,128)(2,1)} %get-tuple-element.200), channel_id=1, source_target_pairs={{0,24},{2,26},{4,28},{6,30},{8,16},{10,18},{12,20},{14,22},{16,8},... | collective-permute-start | bytes 786440 | tf_op jit(solution)/shard_map/ppermute | solution.py:243
  275.6 50.4 %collective-permute-start.111 = (bf16[16,16,512]{2,1,0:T(8,128)(2,1)}, bf16[16,16,512]{2,1,0:T(8,128)(2,1)S(1)}, u32[]{:S(2)}, u32[]{:S(2)}) collective-permute-start(bf16[16,16,512]{2,1,0:T(8,128)(2,1)} %get-tuple-element.268), channel_id=1, source_target_pairs={{0,16},{2,18},{4,20},{6,22},{8,24},{10,26},{12,28},{14,30},{16,0},... | collective-permute-start | bytes 786440 | tf_op jit(solution)/shard_map/ppermute | solution.py:243
  290.6 58.8 %collective-permute-start.113 = (bf16[16,16,512]{2,1,0:T(8,128)(2,1)}, bf16[16,16,512]{2,1,0:T(8,128)(2,1)S(1)}, u32[]{:S(2)}, u32[]{:S(2)}) collective-permute-start(bf16[16,16,512]{2,1,0:T(8,128)(2,1)} %get-tuple-element.270), channel_id=1, source_target_pairs={{0,20},{2,22},{4,16},{6,18},{8,28},{10,30},{12,24},{14,26},{16,4},... | collective-permute-start | bytes 786440 | tf_op jit(solution)/shard_map/ppermute | solution.py:243
  293.9 76.5 %collective-permute-start.114 = (bf16[16,16,512]{2,1,0:T(8,128)(2,1)}, bf16[16,16,512]{2,1,0:T(8,128)(2,1)S(1)}, u32[]{:S(2)}, u32[]{:S(2)}) collective-permute-start(bf16[16,16,512]{2,1,0:T(8,128)(2,1)} %get-tuple-element.271), channel_id=1, source_target_pairs={{0,22},{2,20},{4,18},{6,16},{8,30},{10,28},{12,26},{14,24},{16,6},... | collective-permute-start | bytes 786440 | tf_op jit(solution)/shard_map/ppermute | solution.py:243
  294.3 77.0 %collective-permute-start.115 = (bf16[16,16,512]{2,1,0:T(8,128)(2,1)}, bf16[16,16,512]{2,1,0:T(8,128)(2,1)S(1)}, u32[]{:S(2)}, u32[]{:S(2)}) collective-permute-start(bf16[16,16,512]{2,1,0:T(8,128)(2,1)} %get-tuple-element.272), channel_id=1, source_target_pairs={{0,24},{2,26},{4,28},{6,30},{8,16},{10,18},{12,20},{14,22},{16,8},... | collective-permute-start | bytes 786440 | tf_op jit(solution)/shard_map/ppermute | solution.py:243
  326.0 46.5 %collective-permute-start.116 = (bf16[16,16,512]{2,1,0:T(8,128)(2,1)}, bf16[16,16,512]{2,1,0:T(8,128)(2,1)S(1)}, u32[]{:S(2)}, u32[]{:S(2)}) collective-permute-start(bf16[16,16,512]{2,1,0:T(8,128)(2,1)} %get-tuple-element.273), channel_id=1, source_target_pairs={{0,26},{2,24},{4,30},{6,28},{8,18},{10,16},{12,22},{14,20},{16,10}... | collective-permute-start | bytes 786440 | tf_op jit(solution)/shard_map/ppermute | solution.py:243
  330.6 47.4 %collective-permute-start.117 = (bf16[16,16,512]{2,1,0:T(8,128)(2,1)}, bf16[16,16,512]{2,1,0:T(8,128)(2,1)S(1)}, u32[]{:S(2)}, u32[]{:S(2)}) collective-permute-start(bf16[16,16,512]{2,1,0:T(8,128)(2,1)} %get-tuple-element.274), channel_id=1, source_target_pairs={{0,28},{2,30},{4,24},{6,26},{8,20},{10,22},{12,16},{14,18},{16,12}... | collective-permute-start | bytes 786440 | tf_op jit(solution)/shard_map/ppermute | solution.py:243
  349.4 46.6 %collective-permute-start.118 = (bf16[16,16,512]{2,1,0:T(8,128)(2,1)}, bf16[16,16,512]{2,1,0:T(8,128)(2,1)S(1)}, u32[]{:S(2)}, u32[]{:S(2)}) collective-permute-start(bf16[16,16,512]{2,1,0:T(8,128)(2,1)} %get-tuple-element.275), channel_id=1, source_target_pairs={{0,30},{2,28},{4,26},{6,24},{8,22},{10,20},{12,18},{14,16},{16,14}... | collective-permute-start | bytes 786440 | tf_op jit(solution)/shard_map/ppermute | solution.py:243
  370.4 45.5 %collective-permute-start.10 = (bf16[16,16,512]{2,1,0:T(8,128)(2,1)}, bf16[16,16,512]{2,1,0:T(8,128)(2,1)S(1)}, u32[]{:S(2)}, u32[]{:S(2)}) collective-permute-start(bf16[16,16,512]{2,1,0:T(8,128)(2,1)} %get-tuple-element.161), channel_id=1, source_target_pairs={{0,16},{2,18},{4,20},{6,22},{8,24},{10,26},{12,28},{14,30},{16,0},... | collective-permute-start | bytes 786440 | tf_op jit(solution)/shard_map/ppermute | solution.py:243
  372.0 48.5 %collective-permute-start.11 = (bf16[16,16,512]{2,1,0:T(8,128)(2,1)}, bf16[16,16,512]{2,1,0:T(8,128)(2,1)S(1)}, u32[]{:S(2)}, u32[]{:S(2)}) collective-permute-start(bf16[16,16,512]{2,1,0:T(8,128)(2,1)} %get-tuple-element.162), channel_id=1, source_target_pairs={{0,18},{2,16},{4,22},{6,20},{8,26},{10,24},{12,30},{14,28},{16,2},... | collective-permute-start | bytes 786440 | tf_op jit(solution)/shard_map/ppermute | solution.py:243
  373.2 66.1 %collective-permute-start.12 = (bf16[16,16,512]{2,1,0:T(8,128)(2,1)}, bf16[16,16,512]{2,1,0:T(8,128)(2,1)S(1)}, u32[]{:S(2)}, u32[]{:S(2)}) collective-permute-start(bf16[16,16,512]{2,1,0:T(8,128)(2,1)} %get-tuple-element.163), channel_id=1, source_target_pairs={{0,20},{2,22},{4,16},{6,18},{8,28},{10,30},{12,24},{14,26},{16,4},... | collective-permute-start | bytes 786440 | tf_op jit(solution)/shard_map/ppermute | solution.py:243
  378.0 65.9 %collective-permute-start.13 = (bf16[16,16,512]{2,1,0:T(8,128)(2,1)}, bf16[16,16,512]{2,1,0:T(8,128)(2,1)S(1)}, u32[]{:S(2)}, u32[]{:S(2)}) collective-permute-start(bf16[16,16,512]{2,1,0:T(8,128)(2,1)} %get-tuple-element.164), channel_id=1, source_target_pairs={{0,22},{2,20},{4,18},{6,16},{8,30},{10,28},{12,26},{14,24},{16,6},... | collective-permute-start | bytes 786440 | tf_op jit(solution)/shard_map/ppermute | solution.py:243
  396.0 54.3 %collective-permute-start.14 = (bf16[16,16,512]{2,1,0:T(8,128)(2,1)}, bf16[16,16,512]{2,1,0:T(8,128)(2,1)S(1)}, u32[]{:S(2)}, u32[]{:S(2)}) collective-permute-start(bf16[16,16,512]{2,1,0:T(8,128)(2,1)} %get-tuple-element.165), channel_id=1, source_target_pairs={{0,24},{2,26},{4,28},{6,30},{8,16},{10,18},{12,20},{14,22},{16,8},... | collective-permute-start | bytes 786440 | tf_op jit(solution)/shard_map/ppermute | solution.py:243
  468.1 48.9 %collective-permute-start.38 = (bf16[4,512,128]{2,1,0:T(8,128)(2,1)S(1)}, bf16[4,512,128]{2,1,0:T(8,128)(2,1)S(1)}, u32[]{:S(2)}, u32[]{:S(2)}) collective-permute-start(bf16[4,512,128]{2,1,0:T(8,128)(2,1)S(1)} %copy-done.10), channel_id=1, source_target_pairs={{0,1},{1,0},{2,3},{3,2},{4,5},{5,4},{6,7},{7,6},{8,9},{9,8},{10,11... | collective-permute-start | bytes 1572872 | tf_op jit(solution)/shard_map/ppermute | solution.py:215
  468.7 49.2 %collective-permute-start.37 = (bf16[4,128,512]{2,1,0:T(8,128)(2,1)S(1)}, bf16[4,128,512]{2,1,0:T(8,128)(2,1)S(1)}, u32[]{:S(2)}, u32[]{:S(2)}) collective-permute-start(bf16[4,128,512]{2,1,0:T(8,128)(2,1)S(1)} %copy-done.11), channel_id=1, source_target_pairs={{0,1},{1,0},{2,3},{3,2},{4,5},{5,4},{6,7},{7,6},{8,9},{9,8},{10,11... | collective-permute-start | bytes 1572872 | tf_op jit(solution)/shard_map/ppermute | solution.py:215
  537.5 58.4 %collective-permute-start.95 = (bf16[16,16,512]{2,1,0:T(8,128)(2,1)}, bf16[16,16,512]{2,1,0:T(8,128)(2,1)}, u32[]{:S(2)}, u32[]{:S(2)}) collective-permute-start(bf16[16,16,512]{2,1,0:T(8,128)(2,1)} %get-tuple-element.249), channel_id=1, source_target_pairs={{0,20},{2,22},{4,16},{6,18},{8,28},{10,30},{12,24},{14,26},{16,4},... | collective-permute-start | bytes 786440 | tf_op jit(solution)/shard_map/ppermute | solution.py:243
  643.5 46.3 %collective-permute-start.64 = (bf16[16,16,512]{2,1,0:T(8,128)(2,1)}, bf16[16,16,512]{2,1,0:T(8,128)(2,1)}, u32[]{:S(2)}, u32[]{:S(2)}) collective-permute-start(bf16[16,16,512]{2,1,0:T(8,128)(2,1)} %get-tuple-element.215), channel_id=1, source_target_pairs={{0,22},{2,20},{4,18},{6,16},{8,30},{10,28},{12,26},{14,24},{16,6},... | collective-permute-start | bytes 786440 | tf_op jit(solution)/shard_map/ppermute | solution.py:243
  663.5 128.5 %collective-permute-start.102 = (bf16[2048,512]{1,0:T(8,128)(2,1)S(1)}, bf16[2048,512]{1,0:T(8,128)(2,1)}, u32[]{:S(2)}, u32[]{:S(2)}) collective-permute-start(bf16[2048,512]{1,0:T(8,128)(2,1)S(1)} %copy-done.6), channel_id=1, source_target_pairs={{0,1},{1,0},{2,3},{3,2},{4,5},{5,4},{6,7},{7,6},{8,9},{9,8},{10,11... | collective-permute-start | bytes 6291464 | tf_op jit(solution)/shard_map/ppermute | solution.py:364
  664.1 47.5 %collective-permute-start.65 = (bf16[16,16,512]{2,1,0:T(8,128)(2,1)S(1)}, bf16[16,16,512]{2,1,0:T(8,128)(2,1)S(1)}, u32[]{:S(2)}, u32[]{:S(2)}) collective-permute-start(bf16[16,16,512]{2,1,0:T(8,128)(2,1)S(1)} %copy-done.111), channel_id=1, source_target_pairs={{0,24},{2,26},{4,28},{6,30},{8,16},{10,18},{12,20},{14,22},{16,8},... | collective-permute-start | bytes 786440 | tf_op jit(solution)/shard_map/ppermute | solution.py:243
  666.0 46.5 %collective-permute-start.66 = (bf16[16,16,512]{2,1,0:T(8,128)(2,1)S(1)}, bf16[16,16,512]{2,1,0:T(8,128)(2,1)S(1)}, u32[]{:S(2)}, u32[]{:S(2)}) collective-permute-start(bf16[16,16,512]{2,1,0:T(8,128)(2,1)S(1)} %copy-done.109), channel_id=1, source_target_pairs={{0,26},{2,24},{4,30},{6,28},{8,18},{10,16},{12,22},{14,20},{16,10}... | collective-permute-start | bytes 786440 | tf_op jit(solution)/shard_map/ppermute | solution.py:243
  667.2 46.2 %collective-permute-start.67 = (bf16[16,16,512]{2,1,0:T(8,128)(2,1)S(1)}, bf16[16,16,512]{2,1,0:T(8,128)(2,1)S(1)}, u32[]{:S(2)}, u32[]{:S(2)}) collective-permute-start(bf16[16,16,512]{2,1,0:T(8,128)(2,1)S(1)} %copy-done.108), channel_id=1, source_target_pairs={{0,28},{2,30},{4,24},{6,26},{8,20},{10,22},{12,16},{14,18},{16,12}... | collective-permute-start | bytes 786440 | tf_op jit(solution)/shard_map/ppermute | solution.py:243
  689.9 116.5 %collective-permute-start.101 = (bf16[2048,512]{1,0:T(8,128)(2,1)}, bf16[2048,512]{1,0:T(8,128)(2,1)}, u32[]{:S(2)}, u32[]{:S(2)}) collective-permute-start(bf16[2048,512]{1,0:T(8,128)(2,1)} %get-tuple-element.257), channel_id=1, source_target_pairs={{0,1},{1,0},{2,3},{3,2},{4,5},{5,4},{6,7},{7,6},{8,9},{9,8},{10,11... | collective-permute-start | bytes 6291464 | tf_op jit(solution)/shard_map/ppermute | solution.py:370
  779.4 174.1 %collective-permute-start.70 = (bf16[2048,512]{1,0:T(8,128)(2,1)}, bf16[2048,512]{1,0:T(8,128)(2,1)}, u32[]{:S(2)}, u32[]{:S(2)}) collective-permute-start(bf16[2048,512]{1,0:T(8,128)(2,1)} %get-tuple-element.303), channel_id=1, source_target_pairs={{0,1},{1,0},{2,3},{3,2},{4,5},{5,4},{6,7},{7,6},{8,9},{9,8},{10,11... | collective-permute-start | bytes 6291464 | tf_op jit(solution)/shard_map/ppermute | solution.py:364
  784.9 53.1 %collective-permute-start.130 = (bf16[16,16,512]{2,1,0:T(8,128)(2,1)}, bf16[16,16,512]{2,1,0:T(8,128)(2,1)}, u32[]{:S(2)}, u32[]{:S(2)}) collective-permute-start(bf16[16,16,512]{2,1,0:T(8,128)(2,1)} %get-tuple-element.288), channel_id=1, source_target_pairs={{0,24},{2,26},{4,28},{6,30},{8,16},{10,18},{12,20},{14,22},{16,8},... | collective-permute-start | bytes 786440 | tf_op jit(solution)/shard_map/ppermute | solution.py:243
  790.5 69.4 %collective-permute-start.131 = (bf16[16,16,512]{2,1,0:T(8,128)(2,1)}, bf16[16,16,512]{2,1,0:T(8,128)(2,1)}, u32[]{:S(2)}, u32[]{:S(2)}) collective-permute-start(bf16[16,16,512]{2,1,0:T(8,128)(2,1)} %get-tuple-element.289), channel_id=1, source_target_pairs={{0,26},{2,24},{4,30},{6,28},{8,18},{10,16},{12,22},{14,20},{16,10}... | collective-permute-start | bytes 786440 | tf_op jit(solution)/shard_map/ppermute | solution.py:243
  792.0 68.0 %collective-permute-start.132 = (bf16[16,16,512]{2,1,0:T(8,128)(2,1)}, bf16[16,16,512]{2,1,0:T(8,128)(2,1)}, u32[]{:S(2)}, u32[]{:S(2)}) collective-permute-start(bf16[16,16,512]{2,1,0:T(8,128)(2,1)} %get-tuple-element.290), channel_id=1, source_target_pairs={{0,28},{2,30},{4,24},{6,26},{8,20},{10,22},{12,16},{14,18},{16,12}... | collective-permute-start | bytes 786440 | tf_op jit(solution)/shard_map/ppermute | solution.py:243
  806.4 149.7 %collective-permute-start.69 = (bf16[2048,512]{1,0:T(8,128)(2,1)}, bf16[2048,512]{1,0:T(8,128)(2,1)}, u32[]{:S(2)}, u32[]{:S(2)}) collective-permute-start(bf16[2048,512]{1,0:T(8,128)(2,1)} %get-tuple-element.222), channel_id=1, source_target_pairs={{0,1},{1,0},{2,3},{3,2},{4,5},{5,4},{6,7},{7,6},{8,9},{9,8},{10,11... | collective-permute-start | bytes 6291464 | tf_op jit(solution)/shard_map/ppermute | solution.py:370
  838.0 178.9 %collective-permute-start.136 = (bf16[2048,512]{1,0:T(8,128)(2,1)}, bf16[2048,512]{1,0:T(8,128)(2,1)S(1)}, u32[]{:S(2)}, u32[]{:S(2)}) collective-permute-start(bf16[2048,512]{1,0:T(8,128)(2,1)} %get-tuple-element.295), channel_id=1, source_target_pairs={{0,1},{1,0},{2,3},{3,2},{4,5},{5,4},{6,7},{7,6},{8,9},{9,8},{10,11... | collective-permute-start | bytes 6291464 | tf_op jit(solution)/shard_map/ppermute | solution.py:372
  945.9 51.9 %collective-permute-start.29 = (bf16[16,16,512]{2,1,0:T(8,128)(2,1)}, bf16[16,16,512]{2,1,0:T(8,128)(2,1)}, u32[]{:S(2)}, u32[]{:S(2)}) collective-permute-start(bf16[16,16,512]{2,1,0:T(8,128)(2,1)} %get-tuple-element.181), channel_id=1, source_target_pairs={{0,24},{2,26},{4,28},{6,30},{8,16},{10,18},{12,20},{14,22},{16,8},... | collective-permute-start | bytes 786440 | tf_op jit(solution)/shard_map/ppermute | solution.py:243
  948.1 51.6 %collective-permute-start.30 = (bf16[16,16,512]{2,1,0:T(8,128)(2,1)}, bf16[16,16,512]{2,1,0:T(8,128)(2,1)}, u32[]{:S(2)}, u32[]{:S(2)}) collective-permute-start(bf16[16,16,512]{2,1,0:T(8,128)(2,1)} %get-tuple-element.182), channel_id=1, source_target_pairs={{0,26},{2,24},{4,30},{6,28},{8,18},{10,16},{12,22},{14,20},{16,10}... | collective-permute-start | bytes 786440 | tf_op jit(solution)/shard_map/ppermute | solution.py:243
  953.5 46.4 %collective-permute-start.31 = (bf16[16,16,512]{2,1,0:T(8,128)(2,1)}, bf16[16,16,512]{2,1,0:T(8,128)(2,1)}, u32[]{:S(2)}, u32[]{:S(2)}) collective-permute-start(bf16[16,16,512]{2,1,0:T(8,128)(2,1)} %get-tuple-element.183), channel_id=1, source_target_pairs={{0,28},{2,30},{4,24},{6,26},{8,20},{10,22},{12,16},{14,18},{16,12}... | collective-permute-start | bytes 786440 | tf_op jit(solution)/shard_map/ppermute | solution.py:243
  956.1 45.6 %collective-permute-start.32 = (bf16[16,16,512]{2,1,0:T(8,128)(2,1)}, bf16[16,16,512]{2,1,0:T(8,128)(2,1)}, u32[]{:S(2)}, u32[]{:S(2)}) collective-permute-start(bf16[16,16,512]{2,1,0:T(8,128)(2,1)} %get-tuple-element.184), channel_id=1, source_target_pairs={{0,30},{2,28},{4,26},{6,24},{8,22},{10,20},{12,18},{14,16},{16,14}... | collective-permute-start | bytes 786440 | tf_op jit(solution)/shard_map/ppermute | solution.py:243
  997.9 47.3 %collective-permute-start.135 = (bf16[2048,512]{1,0:T(8,128)(2,1)S(1)}, bf16[2048,512]{1,0:T(8,128)(2,1)}, u32[]{:S(2)}, u32[]{:S(2)}) collective-permute-start(bf16[2048,512]{1,0:T(8,128)(2,1)S(1)} %copy-done.5), channel_id=1, source_target_pairs={{0,1},{1,0},{2,3},{3,2},{4,5},{5,4},{6,7},{7,6},{8,9},{9,8},{10,11... | collective-permute-start | bytes 6291464 | tf_op jit(solution)/shard_map/ppermute | solution.py:364
  999.6 183.6 %collective-permute-start.34 = (bf16[2048,512]{1,0:T(8,128)(2,1)S(1)}, bf16[2048,512]{1,0:T(8,128)(2,1)}, u32[]{:S(2)}, u32[]{:S(2)}) collective-permute-start(bf16[2048,512]{1,0:T(8,128)(2,1)S(1)} %copy-done.4), channel_id=1, source_target_pairs={{0,1},{1,0},{2,3},{3,2},{4,5},{5,4},{6,7},{7,6},{8,9},{9,8},{10,11... | collective-permute-start | bytes 6291464 | tf_op jit(solution)/shard_map/ppermute | solution.py:364
  1000.0 135.1 %collective-permute-start.134 = (bf16[2048,512]{1,0:T(8,128)(2,1)}, bf16[2048,512]{1,0:T(8,128)(2,1)}, u32[]{:S(2)}, u32[]{:S(2)}) collective-permute-start(bf16[2048,512]{1,0:T(8,128)(2,1)} %get-tuple-element.294), channel_id=1, source_target_pairs={{0,1},{1,0},{2,3},{3,2},{4,5},{5,4},{6,7},{7,6},{8,9},{9,8},{10,11... | collective-permute-start | bytes 6291464 | tf_op jit(solution)/shard_map/ppermute | solution.py:370
  1001.7 178.3 %collective-permute-start.103 = (bf16[2048,512]{1,0:T(8,128)(2,1)}, bf16[2048,512]{1,0:T(8,128)(2,1)}, u32[]{:S(2)}, u32[]{:S(2)}) collective-permute-start(bf16[2048,512]{1,0:T(8,128)(2,1)} %get-tuple-element.259), channel_id=1, source_target_pairs={{0,1},{1,0},{2,3},{3,2},{4,5},{5,4},{6,7},{7,6},{8,9},{9,8},{10,11... | collective-permute-start | bytes 6291464 | tf_op jit(solution)/shard_map/ppermute | solution.py:372
  1016.9 208.0 %collective-permute-start.33 = (bf16[2048,512]{1,0:T(8,128)(2,1)}, bf16[2048,512]{1,0:T(8,128)(2,1)}, u32[]{:S(2)}, u32[]{:S(2)}) collective-permute-start(bf16[2048,512]{1,0:T(8,128)(2,1)} %get-tuple-element.187), channel_id=1, source_target_pairs={{0,1},{1,0},{2,3},{3,2},{4,5},{5,4},{6,7},{7,6},{8,9},{9,8},{10,11... | collective-permute-start | bytes 6291464 | tf_op jit(solution)/shard_map/ppermute | solution.py:370
  1161.3 108.5 %collective-permute-start.138 = (bf16[2048,512]{1,0:T(8,128)(2,1)}, bf16[2048,512]{1,0:T(8,128)(2,1)S(1)}, u32[]{:S(2)}, u32[]{:S(2)}) collective-permute-start(bf16[2048,512]{1,0:T(8,128)(2,1)} %get-tuple-element.299), channel_id=1, source_target_pairs={{0,1},{1,0},{2,3},{3,2},{4,5},{5,4},{6,7},{7,6},{8,9},{9,8},{10,11... | collective-permute-start | bytes 6291464 | tf_op jit(solution)/shard_map/ppermute | solution.py:372
  1251.5 63.2 %collective-permute-start.137 = (bf16[2048,512]{1,0:T(8,128)(2,1)}, bf16[2048,512]{1,0:T(8,128)(2,1)S(1)}, u32[]{:S(2)}, u32[]{:S(2)}) collective-permute-start(bf16[2048,512]{1,0:T(8,128)(2,1)} %get-tuple-element.298), channel_id=1, source_target_pairs={{0,1},{1,0},{2,3},{3,2},{4,5},{5,4},{6,7},{7,6},{8,9},{9,8},{10,11... | collective-permute-start | bytes 6291464 | tf_op jit(solution)/shard_map/ppermute | solution.py:372
  (213 other events, 6919.8 us)

commit v2 on v1

--- a/solution.py
+++ b/solution.py
@@ -21,6 +21,10 @@
     return pltpu.CompilerParams(vmem_limit_bytes=VMEM_LIMIT)
 
 
+def cost(us):
+    return pl.CostEstimate(flops=0, bytes_accessed=int(us * 3.6e6), transcendentals=0)
+
+
 def column(row, width=128):
     return jnp.broadcast_to(row, (width, row.shape[1])).T
 
@@ -29,8 +33,8 @@
     return jnp.concatenate([col] * (width // 128), axis=1)
 
 
-def mixer_front(x_ref, sums_ref, rim_ref, gain_ref, proj_ref, taps_ref, fwd_ref, twid_ref, *rest):
-    query_ref, *out_refs = rest[:-1]
+def mixer_front(extra, pos_ref, x_ref, sums_ref, rim_ref, gain_ref, proj_ref, taps_ref, fwd_ref, twid_ref, *rest):
+    query_ref, across_ref, tail_ref, *out_refs = rest[extra:-1]
     hist = rest[-1]
     step = pl.program_id(0)
     blocks, width, triple = proj_ref.shape
@@ -38,7 +42,7 @@
 
     @pl.when(step == 0)
     def _():
-        hist[:, 0:8, :] = rim_ref[0]
+        hist[:, 0:8, :] = rim_ref[...]
 
     scale = wide(column(lax.rsqrt(sums_ref[0] / D + epsilon)), blocks * width)
     normed = (x_ref[0].astype(f32) * scale * gain_ref[...]).astype(bf16)
@@ -55,31 +59,54 @@
         hist[b, 0:8, :] = hist[b, rows : rows + 8, :]
         query_ref[0, :, b * width : (b + 1) * width] = mixed[:, :width].astype(bf16)
         parts.append((mixed[:, width : 2 * width] * mixed[:, 2 * width :]).astype(bf16))
+    tail_ref[...] = hist[:, 0:8, :]
+
+    @pl.when(lax.rem(step, 2) != pos_ref[1])
+    def _():
+        across_ref[...] = x_ref[0]
+
     source = jnp.concatenate(parts, axis=1)
     first = jnp.dot(fwd_ref[...], source, preferred_element_type=f32)
     first = (first * wide(column(twid_ref[0]), blocks * width)).astype(bf16)
-    cols = out_refs[0].shape[1]
+    inner, _, cols, _ = out_refs[0].shape
     for k, ref in enumerate(out_refs):
-        ref[0] = first[k * cols : (k + 1) * cols]
-
-
-def mixer_middle(count, *refs):
+        for j in range(inner):
+            at = (k * inner + j) * cols
+            ref[j, 0] = first[at : at + cols]
+
+
+def regroup(count, *refs):
     ins = refs[:count]
-    fwd_ref, kernel_ref, inv_ref, twid_ref = refs[count : count + 4]
-    outs = refs[count + 4 : 2 * count + 4]
-    held, done = refs[2 * count + 4 :]
+    outs = refs[-(ins[0].shape[0] - 1) :]
+    for q, out in enumerate(outs):
+        for p in range(count):
+            out[p] = ins[p][q + 1]
+
+
+def mixer_middle(outer, inner, into, outof, *refs):
+    count = outer * inner
+    per = outer + inner - 1
+    ins, refs = refs[: per * len(into)], refs[per * len(into) :]
+    fwd_ref, kernel_ref, inv_ref, twid_ref = refs[:4]
+    outs = refs[-2 - inner * len(outof) : -2]
+    held, done = refs[-2:]
     step = pl.program_id(0)
-    rows, cols, width = ins[0].shape
+    cols, width = ins[0].shape[-2:]
     lanes = width // 128
-    root = rows * count
+    root = fwd_ref.shape[0]
+    rows = root // count
 
     @pl.when(step == 0)
     def _():
-        for k in range(count):
-            for l in range(lanes):
-                held[l, k * rows * cols : (k + 1) * rows * cols, :] = (
-                    ins[k][:, :, l * 128 : (l + 1) * 128].astype(f32).reshape(rows * cols, 128)
-                )
+        for c, (start, size) in enumerate(into):
+            for k in range(outer):
+                for j in range(inner):
+                    ref = ins[c * per + k].at[0] if j == 0 else ins[c * per + outer + j - 1].at[k]
+                    at = ((k * inner + j) * rows + start) * cols
+                    for l in range(lanes):
+                        held[l, at : at + size * cols, :] = (
+                            ref[:, :, l * 128 : (l + 1) * 128].astype(f32).reshape(size * cols, 128)
+                        )
 
     table = jnp.concatenate(
         [held[l, pl.ds(step, root, stride=cols), :] for l in range(lanes)], axis=1
@@ -93,20 +120,25 @@
 
     @pl.when(step == cols - 1)
     def _():
-        for k in range(count):
-            for l in range(lanes):
-                outs[k][:, :, l * 128 : (l + 1) * 128] = (
-                    done[l, k * rows * cols : (k + 1) * rows * cols, :]
-                    .astype(bf16)
-                    .reshape(rows, cols, 128)
-                )
-
-
-def mixer_back(count, half, pos_ref, *refs):
-    ins = refs[:count]
-    inv_ref, query_ref, send_ref, own_ref = refs[count:]
+        for c, (start, size) in enumerate(outof):
+            for k in range(outer):
+                for j in range(inner):
+                    at = ((k * inner + j) * rows + 2 * start) * cols
+                    for l in range(lanes):
+                        outs[c * inner + j][k, :, :, l * 128 : (l + 1) * 128] = (
+                            done[l, at : at + 2 * size * cols, :]
+                            .astype(bf16)
+                            .reshape(2 * size, cols, 128)
+                        )
+
+
+def mixer_back(outer, inner, half, pos_ref, *refs):
+    ins = refs[: outer + inner - 1]
+    inv_ref, query_ref = refs[outer + inner - 1 : outer + inner + 1]
+    send_ref, own_ref = refs[-2:]
     step = pl.program_id(0)
-    table = jnp.concatenate([r[0] for r in ins], axis=0)
+    table = [r[0, 0] for r in ins[:inner]] + [r[j, 0] for r in ins[inner:] for j in range(inner)]
+    table = jnp.concatenate(table, axis=0)
     conv = jnp.dot(inv_ref[...], table, preferred_element_type=f32)
     gated = (query_ref[0].astype(f32) * conv).astype(bf16)
 
@@ -144,8 +176,8 @@
             send_ref[:, p * span - width : (p + 1) * span - width] = res
 
 
-def place(pos_ref, got_ref, _, out_ref):
-    out_ref[0] = got_ref[...]
+def place(pos_ref, got_ref, *rest):
+    rest[-1][0] = got_ref[...]
 
 
 def body(
@@ -180,7 +212,11 @@
     pos = jnp.stack([me, mp]).astype(jnp.int32)
     swap = [(0, 1), (1, 0)]
 
-    order = me ^ jnp.arange(count)
+    inner = 4
+    outer = count // inner
+    legs = [0] + list(range(outer // 2, outer)) + list(range(1, outer // 2))
+    turns = [k * inner + j for k in legs for j in range(inner)]
+    order = me ^ jnp.array(turns, jnp.int32)
 
     def relative(table):
         return jnp.take(
@@ -201,7 +237,8 @@
         return part + lax.ppermute(part, "mp", swap)
 
     rim = lax.ppermute(stream[:, toks - 2 :], "ctx", [(i, i + 1) for i in range(count - 1)])
-    sums = sumsq(stream).reshape(seqs, rows, 1, root)
+    early, later = sumsq(stream[:1]), sumsq(stream[1:])
+    sums = [(early[0] if s == 0 else later[s - 1]).reshape(rows, 1, root) for s in range(seqs)]
     rim_norm = (
         rim.astype(f32) * lax.rsqrt(sumsq(rim)[..., None] / D + epsilon) * gain_mix.astype(f32)
     ).astype(bf16)
@@ -211,8 +248,13 @@
     rim_proj = jnp.pad(rim_proj.astype(bf16).astype(f32), ((0, 0), (0, 0), (6, 0), (0, 0)))
     gain_in = gain_mix.astype(f32).reshape(1, width)
 
+    small = [proj_out, up_blocks, down_blocks, gain_mlp]
+    packed = jnp.concatenate([w.reshape(-1, block) for w in small], axis=0)
+    packed_got = lax.ppermute(packed, "mp", swap)
+
     def both(w):
-        got = lax.ppermute(w, "mp", swap)
+        at = sum(v.size for v in small[: [v is w for v in small].index(True)]) // block
+        got = packed_got[at : at + w.size // block].reshape(w.shape)
         return jnp.concatenate([w, got], axis=0)
 
     def by_source(w):
@@ -238,141 +280,334 @@
     def whole(array):
         return pl.BlockSpec(array.shape, lambda *_: (0,) * array.ndim)
 
-    def swapped(parts):
-        return [parts[0]] + [
-            lax.ppermute(p, "ctx", [(i, i ^ k) for i in range(count)])
-            for k, p in enumerate(parts)
-            if k > 0
+    hbm = pl.BlockSpec(memory_space=pltpu.HBM)
+    line = []
+
+    def over(parts, shifts, note=False):
+        got = [
+            p if k == 0 else lax.ppermute(p, "ctx", [(i, i ^ k) for i in range(count)])
+            for p, k in zip(parts, shifts)
         ]
-
-    piece = jax.ShapeDtypeStruct((rows, cols, width), bf16)
-
-    def front(s):
-        row_block = pl.BlockSpec((1, root, width), lambda i: (s, i, 0))
+        if note:
+            line.extend(got[1:])
+        return got
+
+    def over_outer(parts):
+        return over(parts, [k * inner for k in legs], True)
+
+    def over_inner(parts):
+        return over(parts, range(inner))
+
+    def regrouped(parts, after):
+        size = parts[0].shape[1]
+        step = max(size // 4, 1)
+        many = parts[0].shape[0] - 1
+        shape = jax.ShapeDtypeStruct((len(parts),) + parts[0].shape[1:], bf16)
+
+        def spec(n):
+            return pl.BlockSpec((n, step, cols, width), lambda i: (0, i, 0, 0))
+
         return pl.pallas_call(
-            mixer_front,
-            grid=(rows,),
-            in_specs=[
-                row_block,
-                pl.BlockSpec((1, 1, root), lambda i: (i, 0, 0)),
-                pl.BlockSpec((1,) + rim_proj.shape[1:], lambda i: (s, 0, 0, 0)),
-                whole(gain_in),
-                whole(proj_in),
-                whole(short_taps),
-                whole(fwd_in),
-                pl.BlockSpec((1, 1, root), lambda i: (i, 0, 0)),
-            ],
-            out_specs=[pl.BlockSpec((1, root, width), lambda i: (0, i, 0))]
-            + [pl.BlockSpec((1, cols, width), lambda i: (i, 0, 0))] * count,
-            out_shape=[jax.ShapeDtypeStruct((1, toks, width), bf16)] + [piece] * count,
-            scratch_shapes=[pltpu.VMEM((blocks, root + 8, 3 * block), f32)],
+            functools.partial(regroup, len(parts)),
+            grid=(size // step,),
+            in_specs=[spec(many + 1)] * len(parts) + [hbm] * len(after),
+            out_specs=[spec(len(parts))] * many,
+            out_shape=[shape] * many,
             compiler_params=params(),
+            cost_estimate=cost(4),
+            name="regroup",
+        )(*parts, *after)
+
+    def front(s, start, size, rim, held, after):
+        piece = jax.ShapeDtypeStruct((inner, size, cols, width), bf16)
+        extra = list(after) + list(held)
+        args = [pos, stream, sums[s], rim, gain_in, proj_in, short_taps, fwd_in, twid_in] + extra
+        first = len(args) - 2
+        query, across, tail, *parts = pl.pallas_call(
+            functools.partial(mixer_front, len(extra)),
+            grid_spec=pltpu.PrefetchScalarGridSpec(
+                num_scalar_prefetch=1,
+                grid=(size,),
+                in_specs=[
+                    pl.BlockSpec((1, root, width), lambda i, pos: (s, start + i, 0)),
+                    pl.BlockSpec((1, 1, root), lambda i, pos: (start + i, 0, 0)),
+                    whole(rim),
+                    whole(gain_in),
+                    whole(proj_in),
+                    whole(short_taps),
+                    whole(fwd_in),
+                    pl.BlockSpec((1, 1, root), lambda i, pos: (start + i, 0, 0)),
+                ]
+                + [hbm] * len(extra),
+                out_specs=[
+                    pl.BlockSpec((1, root, width), lambda i, pos: (0, start + i, 0)),
+                    pl.BlockSpec((root, width), lambda i, pos: ((start + i) // 2, 0)),
+                    whole(rim),
+                ]
+                + [pl.BlockSpec((inner, 1, cols, width), lambda i, pos: (0, i, 0, 0))] * outer,
+                scratch_shapes=[pltpu.VMEM((blocks, root + 8, 3 * block), f32)],
+            ),
+            out_shape=[
+                jax.ShapeDtypeStruct((1, toks, width), bf16),
+                jax.ShapeDtypeStruct((toks // 2, width), bf16),
+                jax.ShapeDtypeStruct(rim.shape, f32),
+            ]
+            + [piece] * outer,
+            input_output_aliases={first: 0, first + 1: 1} if held else {},
+            compiler_params=params(),
+            cost_estimate=cost(1.25 * size),
             name="mixer_front",
-        )(stream, sums[s], rim_proj, gain_in, proj_in, short_taps, fwd_in, twid_in)
-
-    def middle(parts):
-        full = pl.BlockSpec((rows, cols, width), lambda i: (0, 0, 0))
-        return pl.pallas_call(
-            functools.partial(mixer_middle, count),
+        )(*args)
+        return (query, across), tail, parts
+
+    def middle(pieces, into, outof, after):
+        def specs(first, sizes):
+            return [
+                pl.BlockSpec((n,) + p, lambda i: (0, 0, 0, 0)) for p in sizes for n in first
+            ]
+
+        flat = [p for piece in pieces for p in piece]
+        shapes = [(2 * n, cols, width) for _, n in outof]
+        res = pl.pallas_call(
+            functools.partial(mixer_middle, outer, inner, into, outof),
             grid=(cols,),
-            in_specs=[full] * count
+            in_specs=specs([1] * outer + [outer] * (inner - 1), [(n, cols, width) for _, n in into])
             + [
                 whole(fwd_out),
                 pl.BlockSpec((1, root, width), lambda i: (i, 0, 0)),
                 whole(inv_out),
                 pl.BlockSpec((1, 1, root), lambda i: (i, 0, 0)),
-            ],
-            out_specs=[full] * count,
-            out_shape=[piece] * count,
+            ]
+            + [hbm] * len(after),
+            out_specs=specs([outer] * inner, shapes),
+            out_shape=[jax.ShapeDtypeStruct((outer,) + p, bf16) for p in shapes for _ in range(inner)],
             scratch_shapes=[pltpu.VMEM((width // 128, root * cols, 128), f32)] * 2,
             compiler_params=params(),
+            cost_estimate=cost(20),
             name="mixer_middle",
-        )(*parts, fwd_out, kernel_t, inv_out, twid_out)
-
-    def back(parts, query):
+        )(*flat, fwd_out, kernel_t, inv_out, twid_out, *after)
+        return [res[c * inner : (c + 1) * inner] for c in range(len(outof))]
+
+    def back(parts, query, start, size, after):
+        def local(i, pos):
+            return jnp.where(i < size, 2 * i + 1 - pos[1], 2 * (i - size) + pos[1])
+
         def row(i, pos):
-            return lax.rem(i + half * (1 - pos[1]), rows)
-
-        half_shape = jax.ShapeDtypeStruct((half * root, width), bf16)
+            return 2 * start + local(i, pos)
+
+        shape = jax.ShapeDtypeStruct((size * root, width), bf16)
         return pl.pallas_call(
-            functools.partial(mixer_back, count, half),
+            functools.partial(mixer_back, outer, inner, size),
             grid_spec=pltpu.PrefetchScalarGridSpec(
                 num_scalar_prefetch=1,
-                grid=(rows,),
-                in_specs=[pl.BlockSpec((1, cols, width), lambda i, pos: (row(i, pos), 0, 0))] * count
+                grid=(2 * size,),
+                in_specs=[pl.BlockSpec((1, 1, cols, width), lambda i, pos: (0, local(i, pos), 0, 0))] * inner
+                + [pl.BlockSpec((inner, 1, cols, width), lambda i, pos: (0, local(i, pos), 0, 0))]
+                * (outer - 1)
                 + [
                     whole(inv_in),
                     pl.BlockSpec((1, root, width), lambda i, pos: (0, row(i, pos), 0)),
-                ],
+                ]
+                + [hbm] * len(after),
                 out_specs=[
-                    pl.BlockSpec((root, width), lambda i, pos: (jnp.minimum(i, half - 1), 0)),
-                    pl.BlockSpec((root, width), lambda i, pos: (jnp.maximum(i - half, 0), 0)),
+                    pl.BlockSpec((root, width), lambda i, pos: (jnp.minimum(i, size - 1), 0)),
+                    pl.BlockSpec((root, width), lambda i, pos: (jnp.maximum(i - size, 0), 0)),
                 ],
             ),
-            out_shape=[half_shape] * 2,
+            out_shape=[shape] * 2,
             compiler_params=params(),
+            cost_estimate=cost(1.8 * size),
             name="mixer_back",
-        )(pos, *parts, inv_in, query)
+        )(pos, *parts, inv_in, query, *after)
 
     out_shape = jax.ShapeDtypeStruct(stream.shape, bf16)
 
-    def channels(s, own, got, x_got, out):
+    def channels(s, start, size, own, got, x_got, out, after):
         flat = pl.BlockSpec((root, width), lambda i, pos: (i, 0))
-        mine = pl.BlockSpec((1, root, width), lambda i, pos: (s, pos[1] * half + i, 0))
+        mine = pl.BlockSpec((1, root, width), lambda i, pos: (s, 2 * (start + i) + pos[1], 0))
+        theirs = pl.BlockSpec((root, width), lambda i, pos: (start + i, 0))
         args = [pos, own, got, stream, x_got, mix_tab, gain_out, up_tab, down_tab]
-        specs = [flat, flat, mine, flat, whole(mix_tab), whole(gain_out), whole(up_tab), whole(down_tab)]
-        if out is not None:
-            args.append(out)
-            specs.append(pl.BlockSpec(memory_space=pl.ANY))
+        specs = [flat, flat, mine, theirs, whole(mix_tab), whole(gain_out), whole(up_tab), whole(down_tab)]
+        extra = list(after) + ([] if out is None else [out])
+        args, specs = args + extra, specs + [hbm] * len(extra)
         return pl.pallas_call(
             mlp,
             grid_spec=pltpu.PrefetchScalarGridSpec(
-                num_scalar_prefetch=1, grid=(half,), in_specs=specs, out_specs=[mine, flat]
+                num_scalar_prefetch=1, grid=(size,), in_specs=specs, out_specs=[mine, flat]
             ),
-            out_shape=[out_shape, jax.ShapeDtypeStruct((half * root, width), bf16)],
-            input_output_aliases={} if out is None else {9: 0},
+            out_shape=[out_shape, jax.ShapeDtypeStruct((size * root, width), bf16)],
+            input_output_aliases={} if out is None else {len(args) - 1: 0},
             compiler_params=params(),
+            cost_estimate=cost(3.2 * size),
             name="mlp",
         )(*args)
 
-    def placed(s, got, out):
+    def placed(s, start, size, got, out):
         return pl.pallas_call(
             place,
             grid_spec=pltpu.PrefetchScalarGridSpec(
                 num_scalar_prefetch=1,
-                grid=(2,),
-                in_specs=[
-                    pl.BlockSpec((half * root // 2, width), lambda i, pos: (i, 0)),
-                    pl.BlockSpec(memory_space=pl.ANY),
-                ],
+                grid=(size,),
+                in_specs=[pl.BlockSpec((root, width), lambda i, pos: (i, 0)), hbm],
                 out_specs=pl.BlockSpec(
-                    (1, half * root // 2, width), lambda i, pos: (s, (1 - pos[1]) * 2 + i, 0)
+                    (1, root, width), lambda i, pos: (s, 2 * (start + i) + 1 - pos[1], 0)
                 ),
             ),
             out_shape=out_shape,
             input_output_aliases={2: 0},
             compiler_params=params(),
+            cost_estimate=cost(0.4 * size),
             name="place",
         )(pos, got, out)
 
-    queries, firsts, x_gots = [], [], []
-    for s in range(seqs):
-        query, *parts = front(s)
-        queries.append(query)
-        firsts.append(swapped(parts))
-        x_send = lax.dynamic_slice(stream, (s, (1 - mp) * (toks // 2), 0), (1, toks // 2, width))
-        x_gots.append(lax.ppermute(x_send[0], "mp", swap))
-    thirds = [swapped(middle(parts)) for parts in firsts]
+    def cut(sizes):
+        return [(sum(sizes[:i]), n) for i, n in enumerate(sizes)]
+
+    into = [cut([half, half])] * seqs
+    outof = [cut([half // 2, half // 2])] * seqs
+
+    firsts, queries, thirds, x_gots, gates, sent = {}, {}, {}, {}, {}, {}
     out = None
-    waiting = []
-    for s in range(seqs):
-        send, own = back(thirds[s], queries[s])
-        got = lax.ppermute(send, "mp", swap)
-        out, send = channels(s, own, got, x_gots[s], out)
-        waiting.append(lax.ppermute(send, "mp", swap))
-        if s >= 1:
-            out = placed(s - 1, waiting[s - 1], out)
-    return placed(seqs - 1, waiting[seqs - 1], out)
+    last = None
+
+    def swap_x(a):
+        return lax.ppermute(a, "mp", swap)
+
+    def upto(n):
+        return [] if n is None else line[max(n - 3, 0) : n]
+
+    def do_front(s, c=0, n=None, extra=()):
+        nonlocal last
+        start, size = into[s][c]
+        rim, held = (rim_proj[s], ()) if c == 0 else queries[s]
+        held, rim, parts = front(
+            s, start, size, rim, held, [*upto(n), *extra, *([] if last is None else [last])]
+        )
+        last = rim
+        queries[s] = rim, held
+        firsts[s, c] = parts
+        if c + 1 == len(into[s]):
+            x_gots[s] = swap_x(held[1])
+
+    def do_go(s, c):
+        firsts[s, c] = over_outer(firsts[s, c])
+
+    def do_turn(s, c=0, n=None, extra=()):
+        nonlocal last
+        parts = firsts[s, c]
+        res = regrouped(parts, [*upto(n), last, *extra])
+        last = res[0]
+        firsts[s, c] = parts + over_inner([None] + list(res))[1:]
+
+    def do_middle(s, n=None, extra=()):
+        nonlocal last
+        pieces = [firsts[s, c] for c in range(len(into[s]))]
+        res = middle(pieces, into[s], outof[s], [*upto(n), last, *extra])
+        last = res[0][0]
+        for c, parts in enumerate(res):
+            thirds[s, c] = over_inner(parts)
+
+    def do_return(s, c=0, n=None):
+        nonlocal last
+        parts = thirds[s, c]
+        res = regrouped(parts, [*upto(n), last])
+        last = res[0]
+        thirds[s, c] = parts, res
+
+    def do_send(s, c=0):
+        parts, res = thirds[s, c]
+        thirds[s, c] = parts + over_outer([None] + list(res))[1:]
+
+    def do_back(s, c=0, n=None, extra=()):
+        nonlocal last
+        start, size = outof[s][c]
+        send, own = back(thirds[s, c], queries[s][1][0], start, size, [*upto(n), last, *extra])
+        last = own
+        gates[s, c] = own, swap_x(send)
+
+    def do_mlp(s, c=0, n=None, extra=()):
+        nonlocal last, out
+        start, size = outof[s][c]
+        out, send = channels(s, start, size, *gates[s, c], x_gots[s], out, [*upto(n), last, *extra])
+        last = send
+        sent[s, c] = swap_x(send)
+
+    def do_place(s, c=0):
+        nonlocal out
+        out = placed(s, *outof[s][c], sent[s, c], out)
+
+    def at(groups):
+        return int(groups * (outer - 1))
+
+    do_front(0, 0)
+    do_go(0, 0)
+    do_front(0, 1)
+    do_go(0, 1)
+    do_front(1, 0, n=1)
+    do_go(1, 0)
+    do_front(1, 1, n=2)
+    do_go(1, 1)
+    do_turn(0, 0, n=3)
+    do_front(2, 0, n=4)
+    do_go(2, 0)
+    do_front(2, 1, n=5)
+    do_go(2, 1)
+    do_turn(0, 1, n=6)
+    do_middle(0, n=7, extra=[packed_got])
+    do_front(3, 0, n=8)
+    do_turn(1, 0, n=9)
+    do_front(3, 1, n=10)
+    do_return(0, 0, n=11)
+    do_send(0, 0)
+    do_return(0, 1, n=11)
+    do_send(0, 1)
+    do_go(3, 0)
+    do_go(3, 1)
+    do_turn(1, 1, n=12)
+    do_middle(1, n=14, extra=[x_gots[0]])
+    do_turn(2, 0, n=15)
+    do_return(1, 0, n=16)
+    do_send(1, 0)
+    do_return(1, 1, n=17)
+    do_send(1, 1)
+    do_turn(2, 1, n=18)
+    do_middle(2, n=20, extra=[x_gots[1]])
+    do_back(0, 0, n=21)
+    do_return(2, 0, n=22)
+    do_send(2, 0)
+    do_return(2, 1, n=23)
+    do_send(2, 1)
+    do_back(0, 1, n=24)
+    do_mlp(0, 0, n=26)
+    do_turn(3, 0, n=27, extra=[x_gots[2]])
+    do_mlp(0, 1, n=29)
+    do_turn(3, 1, n=30)
+    do_middle(3, n=32)
+    do_back(1, 0, n=33)
+    do_place(0, 0)
+    do_return(3, 0, n=34)
+    do_send(3, 0)
+    do_return(3, 1, n=35)
+    do_send(3, 1)
+    do_back(1, 1, n=36)
+    do_mlp(1, 0, n=38, extra=[x_gots[3]])
+    do_place(0, 1)
+    do_back(2, 0, n=39)
+    do_mlp(1, 1, n=41)
+    do_place(1, 0)
+    do_back(2, 1, n=42)
+    do_mlp(2, 0, n=44)
+    do_place(1, 1)
+    do_back(3, 0, n=45)
+    do_mlp(2, 1, n=47)
+    do_back(3, 1)
+    do_place(2, 0)
+    do_mlp(3, 0)
+    do_place(2, 1)
+    do_mlp(3, 1)
+    do_place(3, 0)
+    do_place(3, 1)
+    return out
 
 
 def from_behind(array, axis, by):

time: 1330 us -> 1070 us (0.80)
  waiting for transfers between devices: 569 us -> 328 us
  starting transfers between devices: 353 us -> 201 us
  Pallas kernels: 343 us -> 462 us
  local copies, waits for them, and re-layouts: 36.3 us -> 49.7 us
    ppermute x136 -> x117, waiting for transfers between devices: 566 us -> 326 us  [the longest x96 262 us: over(): lax.ppermute(p, 'ctx', [(i, i ^ k) for i in range(count)])]
    ppermute x136 -> x117, starting transfers between devices: 349 us -> 194 us  [the longest x96 175 us: over(): lax.ppermute(p, 'ctx', [(i, i ^ k) for i in range(count)])]
    pallas_call x12 -> x36, Pallas kernels: 224 us -> 306 us  [the longest x8 98.3 us: front(): pl.pallas_call(functools.partial(mixer_front, len(extra)), grid_spec=pltp...]
    pallas_call x4 -> x8, Pallas kernels: 13.3 us -> 32.5 us  [placed(): pl.pallas_call(place, grid_spec=pltpu.PrefetchScalarGridSpec(num_scalar_p...]
    pallas_call x4 -> x8, Pallas kernels: 106 us -> 123 us  [channels(): pl.pallas_call(mlp, grid_spec=pltpu.PrefetchScalarGridSpec(num_scalar_pre...]
    unnamed x251 -> x300, local copies, waits for them, and re-layouts: 15.7 us -> 29.2 us
  transfers between devices with their start and end apart: 139 -> 121, of which waited for: 49 -> 40; matrix products, arithmetic and copies ran while one was open for 3% -> 5% of each run, Pallas kernels for 26% -> 43%
where the time goes in v2:
time: 1070 us; the launch traced here: 1060 us
  Pallas kernels  462 us (43%)
  waiting for transfers between devices  328 us (31%)
  starting transfers between devices  201 us (19%)
  local copies, waits for them, and re-layouts  49.7 us (5%)
  other arithmetic  20 us (2%)
    ppermute x96, waiting for transfers between devices, over(): lax.ppermute(p, 'ctx', [(i, i ^ k) for i in range(count)])  262 us
    ppermute x96, starting transfers between devices, over(): lax.ppermute(p, 'ctx', [(i, i ^ k) for i in range(count)])  175 us
    pallas_call x8, Pallas kernels, channels(): pl.pallas_call(mlp, grid_spec=pltpu.PrefetchScalarGridSpec(num_scalar_pre...  123 us
    pallas_call x8, Pallas kernels, front(): pl.pallas_call(functools.partial(mixer_front, len(extra)), grid_spec=pltp...  98.3 us
    pallas_call x4, Pallas kernels, middle(): pl.pallas_call(functools.partial(mixer_middle, outer, inner, into, outof)...  83 us
    pallas_call x8, Pallas kernels, back(): pl.pallas_call(functools.partial(mixer_back, outer, inner, size), grid_sp...  65.1 us
    ppermute x20, waiting for transfers between devices, swap_x(): return lax.ppermute(a, 'mp', swap)  63.9 us
    pallas_call x16, Pallas kernels, regrouped(): pl.pallas_call(functools.partial(regroup, len(parts)), grid=(size // step...  60 us
  transfers between devices with their start and end apart: 121, of which 40 were waited for; matrix products, arithmetic and copies ran while one was open for 5% of the time, Pallas kernels for 43%

profile of v2, /device:TPU:0, one launch (start us, length us, event | category | flops | bytes accessed | tf_op | source)
XLA Modules:
  0.0 1062.4 jit_solution(16852668692321175607)
XLA Ops:
  25.0 12.5 %mixer_front.8 = (bf16[1,4096,512]{2,1,0:T(8,128)(2,1)}, bf16[2048,512]{1,0:T(8,128)(2,1)}, f32[4,8,384]{2,1,0:T(8,128)}, bf16[4,8,16,512]{3,2,1,0:T(8,128)(2,1)...) custom-call(s32[2]{0:T(128)} %pad_add_fusion.pos_ref, ...), custom_call_target="tpu_custom_call" | custom-call | bytes 36000000 | tf_op jit(solution)/shard_map/mixer_front/pallas_call | solution.py:326
  42.3 12.2 %mixer_front.9 = (bf16[1,4096,512]{2,1,0:T(8,128)(2,1)}, bf16[2048,512]{1,0:T(8,128)(2,1)}, f32[4,8,384]{2,1,0:T(8,128)}, bf16[4,8,16,512]{3,2,1,0:T(8,128)(2,1)...) custom-call(s32[2]{0:T(128)} %pad_add_fusion.pos_ref, ...), custom_call_target="tpu_custom_call", output_to_operand_aliasing={{0}: (10, {}), {1}: (11, {})} | custom-call | bytes 36000000 | tf_op jit(solution)/shard_map/mixer_front/pallas_call | solution.py:326
  58.7 17.4 %collective-permute-done.5.rest_0_.refs_1_.refs_4_ = bf16[4,8,16,512]{3,2,1,0:T(8,128)(2,1)S(1)} collective-permute-done((bf16[4,8,16,512]{3,2,1,0:T(8,128)(2,1)}, bf16[4,8,16,512]{3,2,1,0:T(8,128)(2,1)S(1)}, u32[]{:S(2)}, u32[]{:S(2)}) %collective-permute-start.5) | collective-permute-done | bytes 524320 | tf_op jit(solution)/shard_map/ppermute | solution.py:288
  79.3 12.2 %mixer_front.10 = (bf16[1,4096,512]{2,1,0:T(8,128)(2,1)}, bf16[2048,512]{1,0:T(8,128)(2,1)}, f32[4,8,384]{2,1,0:T(8,128)}, bf16[4,8,16,512]{3,2,1,0:T(8,128)(2,1...) custom-call(s32[2]{0:T(128)} %pad_add_fusion.pos_ref, ...), custom_call_target="tpu_custom_call" | custom-call | bytes 36000000 | tf_op jit(solution)/shard_map/mixer_front/pallas_call | solution.py:326
  92.3 12.4 %mixer_front.11 = (bf16[1,4096,512]{2,1,0:T(8,128)(2,1)}, bf16[2048,512]{1,0:T(8,128)(2,1)}, f32[4,8,384]{2,1,0:T(8,128)}, bf16[4,8,16,512]{3,2,1,0:T(8,128)(2,1...) custom-call(s32[2]{0:T(128)} %pad_add_fusion.pos_ref, ...), custom_call_target="tpu_custom_call", output_to_operand_aliasing={{0}: (12, {}), {1}: (13, {})} | custom-call | bytes 36000000 | tf_op jit(solution)/shard_map/mixer_front/pallas_call | solution.py:326
  109.4 32.6 %collective-permute-start.11 = (bf16[4,8,16,512]{3,2,1,0:T(8,128)(2,1)}, bf16[4,8,16,512]{3,2,1,0:T(8,128)(2,1)S(1)}, u32[]{:S(2)}, u32[]{:S(2)}) collective-permute-start(bf16[4,8,16,512]{3,2,1,0:T(8,128)(2,1)} %get-tuple-element.189), channel_id=1, source_target_pairs={{0,4},{2,6},{4,0},{6,2},{8,12},{10,14},{12,8},{14,10},{16,20},{18,... | collective-permute-start | bytes 1572872 | tf_op jit(solution)/shard_map/ppermute | solution.py:288
  145.3 12.2 %mixer_front.12 = (bf16[1,4096,512]{2,1,0:T(8,128)(2,1)}, bf16[2048,512]{1,0:T(8,128)(2,1)}, f32[4,8,384]{2,1,0:T(8,128)}, bf16[4,8,16,512]{3,2,1,0:T(8,128)(2,1...) custom-call(s32[2]{0:T(128)} %pad_add_fusion.pos_ref, ...), custom_call_target="tpu_custom_call" | custom-call | bytes 36000000 | tf_op jit(solution)/shard_map/mixer_front/pallas_call | solution.py:326
  157.5 12.3 %mixer_front.13 = (bf16[1,4096,512]{2,1,0:T(8,128)(2,1)}, bf16[2048,512]{1,0:T(8,128)(2,1)}, f32[4,8,384]{2,1,0:T(8,128)}, bf16[4,8,16,512]{3,2,1,0:T(8,128)(2,1...) custom-call(s32[2]{0:T(128)} %pad_add_fusion.pos_ref, ...), custom_call_target="tpu_custom_call", output_to_operand_aliasing={{0}: (13, {}), {1}: (14, {})} | custom-call | bytes 36000000 | tf_op jit(solution)/shard_map/mixer_front/pallas_call | solution.py:326
  176.7 11.3 %collective-permute-start.25 = (bf16[4,8,16,512]{3,2,1,0:T(8,128)(2,1)}, bf16[4,8,16,512]{3,2,1,0:T(8,128)(2,1)S(1)}, u32[]{:S(2)}, u32[]{:S(2)}) collective-permute-start(bf16[4,8,16,512]{3,2,1,0:T(8,128)(2,1)} %get-tuple-element.209), channel_id=1, source_target_pairs={{0,8},{2,10},{4,12},{6,14},{8,0},{10,2},{12,4},{14,6},{16,24},{18,... | collective-permute-start | bytes 1572872 | tf_op jit(solution)/shard_map/ppermute | solution.py:288
  188.8 13.3 %collective-permute-start.26 = (bf16[4,8,16,512]{3,2,1,0:T(8,128)(2,1)}, bf16[4,8,16,512]{3,2,1,0:T(8,128)(2,1)S(1)}, u32[]{:S(2)}, u32[]{:S(2)}) collective-permute-start(bf16[4,8,16,512]{3,2,1,0:T(8,128)(2,1)} %get-tuple-element.210), channel_id=1, source_target_pairs={{0,16},{2,18},{4,20},{6,22},{8,24},{10,26},{12,28},{14,30},{16,0},... | collective-permute-start | bytes 1572872 | tf_op jit(solution)/shard_map/ppermute | solution.py:288
  217.4 9.1 collective-permute-start.37
  226.5 21.0 %mixer_middle.4 = (bf16[4,8,16,512]{3,2,1,0:T(8,128)(2,1)}, bf16[4,8,16,512]{3,2,1,0:T(8,128)(2,1)}, bf16[4,8,16,512]{3,2,1,0:T(8,128)(2,1)}, bf16[4,8,16,512]{3...) custom-call(bf16[4,8,16,512]{3,2,1,0:T(8,128)(2,1)} %get-tuple-eleme, ...), custom_call_target="tpu_custom_call" | custom-call | bytes 72000000 | tf_op jit(solution)/shard_map/mixer_middle/pallas_call | solution.py:371
  249.6 23.9 %collective-permute-done.31.refs_19_.refs_1_.refs_4_ = bf16[4,8,16,512]{3,2,1,0:T(8,128)(2,1)S(1)} collective-permute-done((bf16[4,8,16,512]{3,2,1,0:T(8,128)(2,1)S(1)}, bf16[4,8,16,512]{3,2,1,0:T(8,128)(2,1)S(1)}, u32[]{:S(2)}, u32[]{:S(2)}) %collective-permute-start.31) | collective-permute-done | bytes 524320 | tf_op jit(solution)/shard_map/ppermute | solution.py:288
  275.4 12.2 %mixer_front.14 = (bf16[1,4096,512]{2,1,0:T(8,128)(2,1)}, bf16[2048,512]{1,0:T(8,128)(2,1)}, f32[4,8,384]{2,1,0:T(8,128)}, bf16[4,8,16,512]{3,2,1,0:T(8,128)(2,1...) custom-call(s32[2]{0:T(128)} %pad_add_fusion.pos_ref, ...), custom_call_target="tpu_custom_call" | custom-call | bytes 36000000 | tf_op jit(solution)/shard_map/mixer_front/pallas_call | solution.py:326
  299.9 12.3 %mixer_front.15 = (bf16[1,4096,512]{2,1,0:T(8,128)(2,1)}, bf16[2048,512]{1,0:T(8,128)(2,1)}, f32[4,8,384]{2,1,0:T(8,128)}, bf16[4,8,16,512]{3,2,1,0:T(8,128)(2,1...) custom-call(s32[2]{0:T(128)} %pad_add_fusion.pos_ref, ...), custom_call_target="tpu_custom_call", output_to_operand_aliasing={{0}: (13, {}), {1}: (14, {})} | custom-call | bytes 36000000 | tf_op jit(solution)/shard_map/mixer_front/pallas_call | solution.py:326
  326.2 12.3 %collective-permute-done.42.refs_12_ = bf16[4,8,16,512]{3,2,1,0:T(8,128)(2,1)S(1)} collective-permute-done((bf16[4,8,16,512]{3,2,1,0:T(8,128)(2,1)}, bf16[4,8,16,512]{3,2,1,0:T(8,128)(2,1)S(1)}, u32[]{:S(2)}, u32[]{:S(2)}) %collective-permute-start.42) | collective-permute-done | bytes 524320 | tf_op jit(solution)/shard_map/ppermute | solution.py:288
  338.5 9.3 collective-permute-done.43.refs_13_
  350.1 20.6 %mixer_middle.5 = (bf16[4,8,16,512]{3,2,1,0:T(8,128)(2,1)}, bf16[4,8,16,512]{3,2,1,0:T(8,128)(2,1)}, bf16[4,8,16,512]{3,2,1,0:T(8,128)(2,1)}, bf16[4,8,16,512]{3...) custom-call(bf16[4,8,16,512]{3,2,1,0:T(8,128)(2,1)} %get-tuple-eleme, ...), custom_call_target="tpu_custom_call" | custom-call | bytes 72000000 | tf_op jit(solution)/shard_map/mixer_middle/pallas_call | solution.py:371
  375.4 11.1 %collective-permute-done.52.refs_2_ = bf16[4,8,16,512]{3,2,1,0:T(8,128)(2,1)S(1)} collective-permute-done((bf16[4,8,16,512]{3,2,1,0:T(8,128)(2,1)}, bf16[4,8,16,512]{3,2,1,0:T(8,128)(2,1)S(1)}, u32[]{:S(2)}, u32[]{:S(2)}) %collective-permute-start.52) | collective-permute-done | bytes 524320 | tf_op jit(solution)/shard_map/ppermute | solution.py:288
  387.4 10.4 collective-permute-done.55.refs_2_
  430.9 15.0 %collective-permute-done.28.refs_19_.refs_4_.refs_9_ = bf16[4,8,16,512]{3,2,1,0:T(8,128)(2,1)} collective-permute-done((bf16[4,8,16,512]{3,2,1,0:T(8,128)(2,1)}, bf16[4,8,16,512]{3,2,1,0:T(8,128)(2,1)}, u32[]{:S(2)}, u32[]{:S(2)}) %collective-permute-start.28) | collective-permute-done | bytes 524320 | tf_op jit(solution)/shard_map/ppermute | solution.py:288
  452.8 10.2 collective-permute-done.58.refs_12_
  477.2 20.7 %mixer_middle.6 = (bf16[4,8,16,512]{3,2,1,0:T(8,128)(2,1)}, bf16[4,8,16,512]{3,2,1,0:T(8,128)(2,1)}, bf16[4,8,16,512]{3,2,1,0:T(8,128)(2,1)}, bf16[4,8,16,512]{3...) custom-call(bf16[4,8,16,512]{3,2,1,0:T(8,128)(2,1)} %get-tuple-eleme, ...), custom_call_target="tpu_custom_call" | custom-call | bytes 72000000 | tf_op jit(solution)/shard_map/mixer_middle/pallas_call | solution.py:371
  502.8 8.2 mixer_back.8
  513.7 9.6 collective-permute-done.67.refs_3_
  577.4 15.3 %mlp.8 = (bf16[4,4096,512]{2,1,0:T(8,128)(2,1)}, bf16[1024,512]{1,0:T(8,128)(2,1)}) custom-call(s32[2]{0:T(128)} %pad_add_fusion.pos_ref, bf16[1024,512]{1,0:T(8,128)(2,1)} %get-tuple-element.261.refs_7_.own_ref, bf16[1024,512]{1,0:T(8,128)(2,1)} %collective-permute-done.61.got_ref, bf16[4,4096,512]{2,1,0:T(8,128)(2,1)} %x_own_ref.15, ...), custom_call_target="tpu_custom_call" | custom-call | bytes 46080000 | tf_op jit(solution)/shard_map/mlp/pallas_call | solution.py:433
  598.1 11.8 %collective-permute-done.75.rest_1_.refs_1_.refs_4_.refs_8_ = bf16[4,8,16,512]{3,2,1,0:T(8,128)(2,1)S(1)} collective-permute-done((bf16[4,8,16,512]{3,2,1,0:T(8,128)(2,1)S(1)}, bf16[4,8,16,512]{3,2,1,0:T(8,128)(2,1)S(1)}, u32[]{:S(2)}, u32[]{:S(2)}) %collective-permute-start.75) | collective-permute-done | bytes 524320 | tf_op jit(solution)/shard_map/ppermute | solution.py:288
  612.0 21.6 %collective-permute-start.82 = (bf16[4,8,16,512]{3,2,1,0:T(8,128)(2,1)S(1)}, bf16[4,8,16,512]{3,2,1,0:T(8,128)(2,1)S(1)}, u32[]{:S(2)}, u32[]{:S(2)}) collective-permute-start(bf16[4,8,16,512]{3,2,1,0:T(8,128)(2,1)S(1)} %copy-done.112), channel_id=1, source_target_pairs={{0,16},{2,18},{4,20},{6,22},{8,24},{10,26},{12,28},{14,30},{16,0},... | collective-permute-start | bytes 1572872 | tf_op jit(solution)/shard_map/ppermute | solution.py:288
  634.0 15.5 %mlp.9 = (bf16[4,4096,512]{2,1,0:T(8,128)(2,1)}, bf16[1024,512]{1,0:T(8,128)(2,1)}) custom-call(s32[2]{0:T(128)} %pad_add_fusion.pos_ref, bf16[1024,512]{1,0:T(8,128)(2,1)} %get-tuple-element.274.rest_3_.own_ref, bf16[1024,512]{1,0:T(8,128)(2,1)} %collective-permute-done.78.got_ref, ...), custom_call_target="tpu_custom_call", output_to_operand_aliasing={{0}: (13, {})} | custom-call | bytes 46080000 | tf_op jit(solution)/shard_map/mlp/pallas_call | solution.py:433
  655.1 10.3 collective-permute-done.82.refs_19_.refs_4_.refs_9_
  667.6 12.9 %collective-permute-done.80.refs_12_ = bf16[4,8,16,512]{3,2,1,0:T(8,128)(2,1)S(1)} collective-permute-done((bf16[4,8,16,512]{3,2,1,0:T(8,128)(2,1)}, bf16[4,8,16,512]{3,2,1,0:T(8,128)(2,1)S(1)}, u32[]{:S(2)}, u32[]{:S(2)}) %collective-permute-start.80) | collective-permute-done | bytes 524320 | tf_op jit(solution)/shard_map/ppermute | solution.py:288
  692.3 20.6 %mixer_middle.7 = (bf16[4,8,16,512]{3,2,1,0:T(8,128)(2,1)}, bf16[4,8,16,512]{3,2,1,0:T(8,128)(2,1)}, bf16[4,8,16,512]{3,2,1,0:T(8,128)(2,1)}, bf16[4,8,16,512]{3...) custom-call(bf16[4,8,16,512]{3,2,1,0:T(8,128)(2,1)} %get-tuple-eleme, ...), custom_call_target="tpu_custom_call" | custom-call | bytes 72000000 | tf_op jit(solution)/shard_map/mixer_middle/pallas_call | solution.py:371
  714.5 9.7 collective-permute-done.88.refs_6_.refs_5_.refs_4_.refs_9_
  724.6 8.3 mixer_back.10
  765.8 8.2 mixer_back.11
  775.1 11.0 %collective-permute-done.102.rest_1_.refs_4_.refs_9_ = bf16[4,8,16,512]{3,2,1,0:T(8,128)(2,1)S(1)} collective-permute-done((bf16[4,8,16,512]{3,2,1,0:T(8,128)(2,1)S(1)}, bf16[4,8,16,512]{3,2,1,0:T(8,128)(2,1)S(1)}, u32[]{:S(2)}, u32[]{:S(2)}) %collective-permute-start.102) | collective-permute-done | bytes 524320 | tf_op jit(solution)/shard_map/ppermute | solution.py:288
  793.6 15.3 %mlp.10 = (bf16[4,4096,512]{2,1,0:T(8,128)(2,1)}, bf16[1024,512]{1,0:T(8,128)(2,1)}) custom-call(s32[2]{0:T(128)} %pad_add_fusion.pos_ref, bf16[1024,512]{1,0:T(8,128)(2,1)} %get-tuple-element.302.refs_7_.own_ref, bf16[1024,512]{1,0:T(8,128)(2,1)} %collective-permute-done.104.got_ref, ...), custom_call_target="tpu_custom_call", output_to_operand_aliasing={{0}: (14, {})} | custom-call | bytes 46080000 | tf_op jit(solution)/shard_map/mlp/pallas_call | solution.py:433
  825.5 9.8 collective-permute-done.96.rest_1_.refs_4_.refs_9_
  841.5 15.9 %mlp.11 = (bf16[4,4096,512]{2,1,0:T(8,128)(2,1)}, bf16[1024,512]{1,0:T(8,128)(2,1)}) custom-call(s32[2]{0:T(128)} %pad_add_fusion.pos_ref, bf16[1024,512]{1,0:T(8,128)(2,1)} %get-tuple-element.312.rest_3_.own_ref, bf16[1024,512]{1,0:T(8,128)(2,1)} %copy-done.79, bf16[4,4096,512]{2,1,0:T(8,128)(2,1)} %x_own_ref.15, ...), custom_call_target="tpu_custom_call", output_to_operand_aliasing={{0}: (13, {})} | custom-call | bytes 46080000 | tf_op jit(solution)/shard_map/mlp/pallas_call | solution.py:433
  867.7 11.2 %collective-permute-done.110.rest_1_.refs_4_.refs_9_ = bf16[4,8,16,512]{3,2,1,0:T(8,128)(2,1)S(1)} collective-permute-done((bf16[4,8,16,512]{3,2,1,0:T(8,128)(2,1)S(1)}, bf16[4,8,16,512]{3,2,1,0:T(8,128)(2,1)S(1)}, u32[]{:S(2)}, u32[]{:S(2)}) %collective-permute-start.110) | collective-permute-done | bytes 524320 | tf_op jit(solution)/shard_map/ppermute | solution.py:288
  889.1 15.3 %mlp.12 = (bf16[4,4096,512]{2,1,0:T(8,128)(2,1)}, bf16[1024,512]{1,0:T(8,128)(2,1)}) custom-call(s32[2]{0:T(128)} %pad_add_fusion.pos_ref, bf16[1024,512]{1,0:T(8,128)(2,1)} %get-tuple-element.320.rest_3_.own_ref, bf16[1024,512]{1,0:T(8,128)(2,1)} %copy-done.80, bf16[4,4096,512]{2,1,0:T(8,128)(2,1)} %x_own_ref.15, ...), custom_call_target="tpu_custom_call", output_to_operand_aliasing={{0}: (13, {})} | custom-call | bytes 46080000 | tf_op jit(solution)/shard_map/mlp/pallas_call | solution.py:433
  904.4 8.2 mixer_back.14
  930.0 15.3 %mlp.13 = (bf16[4,4096,512]{2,1,0:T(8,128)(2,1)}, bf16[1024,512]{1,0:T(8,128)(2,1)}) custom-call(s32[2]{0:T(128)} %pad_add_fusion.pos_ref, bf16[1024,512]{1,0:T(8,128)(2,1)} %get-tuple-element.323.rest_3_.own_ref, bf16[1024,512]{1,0:T(8,128)(2,1)} %copy-done.82, bf16[4,4096,512]{2,1,0:T(8,128)(2,1)} %x_own_ref.15, ...), custom_call_target="tpu_custom_call", output_to_operand_aliasing={{0}: (13, {})} | custom-call | bytes 46080000 | tf_op jit(solution)/shard_map/mlp/pallas_call | solution.py:433
  961.2 12.7 %collective-permute-done.116.got_ref = bf16[1024,512]{1,0:T(8,128)(2,1)S(1)} collective-permute-done((bf16[1024,512]{1,0:T(8,128)(2,1)S(1)}, bf16[1024,512]{1,0:T(8,128)(2,1)S(1)}, u32[]{:S(2)}, u32[]{:S(2)}) %collective-permute-start.116) | collective-permute-done | bytes 1048608 | tf_op jit(solution)/shard_map/ppermute | solution.py:474
  974.9 15.3 %mlp.14 = (bf16[4,4096,512]{2,1,0:T(8,128)(2,1)}, bf16[1024,512]{1,0:T(8,128)(2,1)}) custom-call(s32[2]{0:T(128)} %pad_add_fusion.pos_ref, bf16[1024,512]{1,0:T(8,128)(2,1)} %get-tuple-element.330.rest_3_.own_ref, bf16[1024,512]{1,0:T(8,128)(2,1)} %copy-done.85, bf16[4,4096,512]{2,1,0:T(8,128)(2,1)} %x_own_ref.15, ...), custom_call_target="tpu_custom_call", output_to_operand_aliasing={{0}: (10, {})} | custom-call | bytes 46080000 | tf_op jit(solution)/shard_map/mlp/pallas_call | solution.py:433
  1001.5 17.4 %collective-permute-done.115.got_ref = bf16[1024,512]{1,0:T(8,128)(2,1)S(1)} collective-permute-done((bf16[1024,512]{1,0:T(8,128)(2,1)}, bf16[1024,512]{1,0:T(8,128)(2,1)S(1)}, u32[]{:S(2)}, u32[]{:S(2)}) %collective-permute-start.115) | collective-permute-done | bytes 1048608 | tf_op jit(solution)/shard_map/ppermute | solution.py:474
  1019.9 15.5 %mlp.15 = (bf16[4,4096,512]{2,1,0:T(8,128)(2,1)}, bf16[1024,512]{1,0:T(8,128)(2,1)}) custom-call(s32[2]{0:T(128)} %pad_add_fusion.pos_ref, bf16[1024,512]{1,0:T(8,128)(2,1)} %get-tuple-element.333.rest_0_.own_ref, bf16[1024,512]{1,0:T(8,128)(2,1)} %copy-done.87, bf16[4,4096,512]{2,1,0:T(8,128)(2,1)} %x_own_ref.15, ...), custom_call_target="tpu_custom_call", output_to_operand_aliasing={{0}: (10, {})} | custom-call | bytes 46080000 | tf_op jit(solution)/shard_map/mlp/pallas_call | solution.py:433
  1046.4 10.6 collective-permute-done.119.got_ref
  (597 shorter events, 398.5 us)
Async XLA Ops:
  15.9 40.5 %collective-permute-start = (f32[3,4096]{1,0:T(4,128)S(1)}, f32[3,4096]{1,0:T(4,128)S(1)}, u32[]{:S(2)}, u32[]{:S(2)}) collective-permute-start(f32[3,4096]{1,0:T(4,128)S(1)} %multiply_reduce_fusion), channel_id=1, source_target_pairs={{0,1},{1,0},{2,3},{3,2},{4,5},{5,4},{6,7},{7,6},{8,9},{9,8},{10,11... | collective-permute-start | bytes 147464 | tf_op jit(solution)/shard_map/ppermute | solution.py:237
  40.7 50.8 %collective-permute-start.8 = (bf16[4,8,16,512]{3,2,1,0:T(8,128)(2,1)}, bf16[4,8,16,512]{3,2,1,0:T(8,128)(2,1)S(1)}, u32[]{:S(2)}, u32[]{:S(2)}) collective-permute-start(bf16[4,8,16,512]{3,2,1,0:T(8,128)(2,1)} %get-tuple-element.182), channel_id=1, source_target_pairs={{0,24},{2,26},{4,28},{6,30},{8,16},{10,18},{12,20},{14,22},{16,8},... | collective-permute-start | bytes 1572872 | tf_op jit(solution)/shard_map/ppermute | solution.py:288
  42.0 62.7 %collective-permute-start.9 = (bf16[4,8,16,512]{3,2,1,0:T(8,128)(2,1)}, bf16[4,8,16,512]{3,2,1,0:T(8,128)(2,1)S(1)}, u32[]{:S(2)}, u32[]{:S(2)}) collective-permute-start(bf16[4,8,16,512]{3,2,1,0:T(8,128)(2,1)} %get-tuple-element.183), channel_id=1, source_target_pairs={{0,8},{2,10},{4,12},{6,14},{8,0},{10,2},{12,4},{14,6},{16,24},{18,... | collective-permute-start | bytes 1572872 | tf_op jit(solution)/shard_map/ppermute | solution.py:288
  54.5 54.8 %collective-permute-start.4 = (bf16[4,8,16,512]{3,2,1,0:T(8,128)(2,1)}, bf16[4,8,16,512]{3,2,1,0:T(8,128)(2,1)S(1)}, u32[]{:S(2)}, u32[]{:S(2)}) collective-permute-start(bf16[4,8,16,512]{3,2,1,0:T(8,128)(2,1)} %get-tuple-element.176), channel_id=1, source_target_pairs={{0,8},{2,10},{4,12},{6,14},{8,0},{10,2},{12,4},{14,6},{16,24},{18,... | collective-permute-start | bytes 1572872 | tf_op jit(solution)/shard_map/ppermute | solution.py:288
  56.4 87.2 %collective-permute-start.13 = (bf16[4,8,16,512]{3,2,1,0:T(8,128)(2,1)}, bf16[4,8,16,512]{3,2,1,0:T(8,128)(2,1)S(1)}, u32[]{:S(2)}, u32[]{:S(2)}) collective-permute-start(bf16[4,8,16,512]{3,2,1,0:T(8,128)(2,1)} %get-tuple-element.192), channel_id=1, source_target_pairs={{0,16},{2,18},{4,20},{6,22},{8,24},{10,26},{12,28},{14,30},{16,0},... | collective-permute-start | bytes 1572872 | tf_op jit(solution)/shard_map/ppermute | solution.py:288
  76.1 69.1 %collective-permute-start.14 = (bf16[4,8,16,512]{3,2,1,0:T(8,128)(2,1)}, bf16[4,8,16,512]{3,2,1,0:T(8,128)(2,1)S(1)}, u32[]{:S(2)}, u32[]{:S(2)}) collective-permute-start(bf16[4,8,16,512]{3,2,1,0:T(8,128)(2,1)} %get-tuple-element.193), channel_id=1, source_target_pairs={{0,24},{2,26},{4,28},{6,30},{8,16},{10,18},{12,20},{14,22},{16,8},... | collective-permute-start | bytes 1572872 | tf_op jit(solution)/shard_map/ppermute | solution.py:288
  91.5 82.2 %collective-permute-start.6 = (bf16[4,8,16,512]{3,2,1,0:T(8,128)(2,1)}, bf16[4,8,16,512]{3,2,1,0:T(8,128)(2,1)S(1)}, u32[]{:S(2)}, u32[]{:S(2)}) collective-permute-start(bf16[4,8,16,512]{3,2,1,0:T(8,128)(2,1)} %get-tuple-element.179), channel_id=1, source_target_pairs={{0,16},{2,18},{4,20},{6,22},{8,24},{10,26},{12,28},{14,30},{16,0},... | collective-permute-start | bytes 1572872 | tf_op jit(solution)/shard_map/ppermute | solution.py:288
  104.8 69.0 %collective-permute-start.7 = (bf16[4,8,16,512]{3,2,1,0:T(8,128)(2,1)S(1)}, bf16[4,8,16,512]{3,2,1,0:T(8,128)(2,1)S(1)}, u32[]{:S(2)}, u32[]{:S(2)}) collective-permute-start(bf16[4,8,16,512]{3,2,1,0:T(8,128)(2,1)S(1)} %copy-done.141), channel_id=1, source_target_pairs={{0,24},{2,26},{4,28},{6,30},{8,16},{10,18},{12,20},{14,22},{16,8},... | collective-permute-start | bytes 1572872 | tf_op jit(solution)/shard_map/ppermute | solution.py:288
  109.4 66.5 %collective-permute-start.11 = (bf16[4,8,16,512]{3,2,1,0:T(8,128)(2,1)}, bf16[4,8,16,512]{3,2,1,0:T(8,128)(2,1)S(1)}, u32[]{:S(2)}, u32[]{:S(2)}) collective-permute-start(bf16[4,8,16,512]{3,2,1,0:T(8,128)(2,1)} %get-tuple-element.189), channel_id=1, source_target_pairs={{0,4},{2,6},{4,0},{6,2},{8,12},{10,14},{12,8},{14,10},{16,20},{18,... | collective-permute-start | bytes 1572872 | tf_op jit(solution)/shard_map/ppermute | solution.py:288
  143.6 73.8 %collective-permute-start.18 = (bf16[4612,128]{1,0:T(8,128)(2,1)}, bf16[4612,128]{1,0:T(8,128)(2,1)}, u32[]{:S(2)}, u32[]{:S(2)}) collective-permute-start(bf16[4612,128]{1,0:T(8,128)(2,1)} %pad_maximum_fusion.1), channel_id=1, source_target_pairs={{0,1},{1,0},{2,3},{3,2},{4,5},{5,4},{6,7},{7,6},{8,9},{9,8},{10,11... | collective-permute-start | bytes 3542024 | tf_op jit(solution)/shard_map/ppermute | solution.py:253
  175.9 39.9 %collective-permute-start.15 = (bf16[4,8,16,512]{3,2,1,0:T(8,128)(2,1)}, bf16[4,8,16,512]{3,2,1,0:T(8,128)(2,1)}, u32[]{:S(2)}, u32[]{:S(2)}) collective-permute-start(bf16[4,8,16,512]{3,2,1,0:T(8,128)(2,1)} %get-tuple-element.198.refs_21_), channel_id=1, source_target_pairs={{0,2},{2,0},{4,6},{6,4},{8,10},{10,8},{12,14},{14,12},{16,18},{18,... | collective-permute-start | bytes 1572872 | tf_op jit(solution)/shard_map/ppermute | solution.py:288
  176.7 70.8 %collective-permute-start.25 = (bf16[4,8,16,512]{3,2,1,0:T(8,128)(2,1)}, bf16[4,8,16,512]{3,2,1,0:T(8,128)(2,1)S(1)}, u32[]{:S(2)}, u32[]{:S(2)}) collective-permute-start(bf16[4,8,16,512]{3,2,1,0:T(8,128)(2,1)} %get-tuple-element.209), channel_id=1, source_target_pairs={{0,8},{2,10},{4,12},{6,14},{8,0},{10,2},{12,4},{14,6},{16,24},{18,... | collective-permute-start | bytes 1572872 | tf_op jit(solution)/shard_map/ppermute | solution.py:288
  188.8 58.8 %collective-permute-start.26 = (bf16[4,8,16,512]{3,2,1,0:T(8,128)(2,1)}, bf16[4,8,16,512]{3,2,1,0:T(8,128)(2,1)S(1)}, u32[]{:S(2)}, u32[]{:S(2)}) collective-permute-start(bf16[4,8,16,512]{3,2,1,0:T(8,128)(2,1)} %get-tuple-element.210), channel_id=1, source_target_pairs={{0,16},{2,18},{4,20},{6,22},{8,24},{10,26},{12,28},{14,30},{16,0},... | collective-permute-start | bytes 1572872 | tf_op jit(solution)/shard_map/ppermute | solution.py:288
  202.9 44.9 %collective-permute-start.27 = (bf16[4,8,16,512]{3,2,1,0:T(8,128)(2,1)}, bf16[4,8,16,512]{3,2,1,0:T(8,128)(2,1)S(1)}, u32[]{:S(2)}, u32[]{:S(2)}) collective-permute-start(bf16[4,8,16,512]{3,2,1,0:T(8,128)(2,1)} %get-tuple-element.211), channel_id=1, source_target_pairs={{0,24},{2,26},{4,28},{6,30},{8,16},{10,18},{12,20},{14,22},{16,8},... | collective-permute-start | bytes 1572872 | tf_op jit(solution)/shard_map/ppermute | solution.py:288
  215.8 110.4 %collective-permute-start.44 = (bf16[2048,512]{1,0:T(8,128)(2,1)}, bf16[2048,512]{1,0:T(8,128)(2,1)S(1)}, u32[]{:S(2)}, u32[]{:S(2)}) collective-permute-start(bf16[2048,512]{1,0:T(8,128)(2,1)} %get-tuple-element.238), channel_id=1, source_target_pairs={{0,1},{1,0},{2,3},{3,2},{4,5},{5,4},{6,7},{7,6},{8,9},{9,8},{10,11... | collective-permute-start | bytes 6291464 | tf_op jit(solution)/shard_map/ppermute | solution.py:474
  248.3 39.3 %collective-permute-start.24 = (bf16[4,8,16,512]{3,2,1,0:T(8,128)(2,1)}, bf16[4,8,16,512]{3,2,1,0:T(8,128)(2,1)S(1)}, u32[]{:S(2)}, u32[]{:S(2)}) collective-permute-start(bf16[4,8,16,512]{3,2,1,0:T(8,128)(2,1)} %get-tuple-element.208), channel_id=1, source_target_pairs={{0,6},{2,4},{4,2},{6,0},{8,14},{10,12},{12,10},{14,8},{16,22},{18,... | collective-permute-start | bytes 1572872 | tf_op jit(solution)/shard_map/ppermute | solution.py:288
  325.6 120.6 %collective-permute-start.60 = (bf16[2048,512]{1,0:T(8,128)(2,1)}, bf16[2048,512]{1,0:T(8,128)(2,1)S(1)}, u32[]{:S(2)}, u32[]{:S(2)}) collective-permute-start(bf16[2048,512]{1,0:T(8,128)(2,1)} %get-tuple-element.259), channel_id=1, source_target_pairs={{0,1},{1,0},{2,3},{3,2},{4,5},{5,4},{6,7},{7,6},{8,9},{9,8},{10,11... | collective-permute-start | bytes 6291464 | tf_op jit(solution)/shard_map/ppermute | solution.py:474
  326.2 45.3 %collective-permute-start.33 = (bf16[4,8,16,512]{3,2,1,0:T(8,128)(2,1)}, bf16[4,8,16,512]{3,2,1,0:T(8,128)(2,1)S(1)}, u32[]{:S(2)}, u32[]{:S(2)}) collective-permute-start(bf16[4,8,16,512]{3,2,1,0:T(8,128)(2,1)} %get-tuple-element.225), channel_id=1, source_target_pairs={{0,8},{2,10},{4,12},{6,14},{8,0},{10,2},{12,4},{14,6},{16,24},{18,... | collective-permute-start | bytes 1572872 | tf_op jit(solution)/shard_map/ppermute | solution.py:288
  447.3 53.3 %collective-permute-start.63 = (bf16[4,8,16,512]{3,2,1,0:T(8,128)(2,1)}, bf16[4,8,16,512]{3,2,1,0:T(8,128)(2,1)S(1)}, u32[]{:S(2)}, u32[]{:S(2)}) collective-permute-start(bf16[4,8,16,512]{3,2,1,0:T(8,128)(2,1)} %get-tuple-element.234.refs_7_), channel_id=1, source_target_pairs={{0,16},{2,18},{4,20},{6,22},{8,24},{10,26},{12,28},{14,30},{16,0},... | collective-permute-start | bytes 1572872 | tf_op jit(solution)/shard_map/ppermute | solution.py:288
  450.7 47.5 %collective-permute-start.30 = (bf16[4,8,16,512]{3,2,1,0:T(8,128)(2,1)}, bf16[4,8,16,512]{3,2,1,0:T(8,128)(2,1)S(1)}, u32[]{:S(2)}, u32[]{:S(2)}) collective-permute-start(bf16[4,8,16,512]{3,2,1,0:T(8,128)(2,1)} %get-tuple-element.220), channel_id=1, source_target_pairs={{0,8},{2,10},{4,12},{6,14},{8,0},{10,2},{12,4},{14,6},{16,24},{18,... | collective-permute-start | bytes 1572872 | tf_op jit(solution)/shard_map/ppermute | solution.py:288
  451.3 47.5 %collective-permute-start.62 = (bf16[4,8,16,512]{3,2,1,0:T(8,128)(2,1)}, bf16[4,8,16,512]{3,2,1,0:T(8,128)(2,1)S(1)}, u32[]{:S(2)}, u32[]{:S(2)}) collective-permute-start(bf16[4,8,16,512]{3,2,1,0:T(8,128)(2,1)} %get-tuple-element.263), channel_id=1, source_target_pairs={{0,8},{2,10},{4,12},{6,14},{8,0},{10,2},{12,4},{14,6},{16,24},{18,... | collective-permute-start | bytes 1572872 | tf_op jit(solution)/shard_map/ppermute | solution.py:288
  500.6 92.1 %collective-permute-start.71 = (bf16[2048,512]{1,0:T(8,128)(2,1)}, bf16[2048,512]{1,0:T(8,128)(2,1)S(1)}, u32[]{:S(2)}, u32[]{:S(2)}) collective-permute-start(bf16[2048,512]{1,0:T(8,128)(2,1)} %get-tuple-element.276), channel_id=1, source_target_pairs={{0,1},{1,0},{2,3},{3,2},{4,5},{5,4},{6,7},{7,6},{8,9},{9,8},{10,11... | collective-permute-start | bytes 6291464 | tf_op jit(solution)/shard_map/ppermute | solution.py:474
  511.8 56.2 %collective-permute-start.19 = (bf16[4,8,16,512]{3,2,1,0:T(8,128)(2,1)}, bf16[4,8,16,512]{3,2,1,0:T(8,128)(2,1)S(1)}, u32[]{:S(2)}, u32[]{:S(2)}) collective-permute-start(bf16[4,8,16,512]{3,2,1,0:T(8,128)(2,1)} %get-tuple-element.203), channel_id=1, source_target_pairs={{0,16},{2,18},{4,20},{6,22},{8,24},{10,26},{12,28},{14,30},{16,0},... | collective-permute-start | bytes 1572872 | tf_op jit(solution)/shard_map/ppermute | solution.py:288
  524.5 51.5 %collective-permute-start.61 = (bf16[1024,512]{1,0:T(8,128)(2,1)}, bf16[1024,512]{1,0:T(8,128)(2,1)}, u32[]{:S(2)}, u32[]{:S(2)}) collective-permute-start(bf16[1024,512]{1,0:T(8,128)(2,1)} %get-tuple-element.262), channel_id=1, source_target_pairs={{0,1},{1,0},{2,3},{3,2},{4,5},{5,4},{6,7},{7,6},{8,9},{9,8},{10,11... | collective-permute-start | bytes 3145736 | tf_op jit(solution)/shard_map/ppermute | solution.py:474
  568.0 65.9 %collective-permute-start.78 = (bf16[1024,512]{1,0:T(8,128)(2,1)}, bf16[1024,512]{1,0:T(8,128)(2,1)}, u32[]{:S(2)}, u32[]{:S(2)}) collective-permute-start(bf16[1024,512]{1,0:T(8,128)(2,1)} %get-tuple-element.284), channel_id=1, source_target_pairs={{0,1},{1,0},{2,3},{3,2},{4,5},{5,4},{6,7},{7,6},{8,9},{9,8},{10,11... | collective-permute-start | bytes 3145736 | tf_op jit(solution)/shard_map/ppermute | solution.py:474
  576.0 57.5 %collective-permute-start.77 = (bf16[4,8,16,512]{3,2,1,0:T(8,128)(2,1)}, bf16[4,8,16,512]{3,2,1,0:T(8,128)(2,1)S(1)}, u32[]{:S(2)}, u32[]{:S(2)}) collective-permute-start(bf16[4,8,16,512]{3,2,1,0:T(8,128)(2,1)} %get-tuple-element.283), channel_id=1, source_target_pairs={{0,8},{2,10},{4,12},{6,14},{8,0},{10,2},{12,4},{14,6},{16,24},{18,... | collective-permute-start | bytes 1572872 | tf_op jit(solution)/shard_map/ppermute | solution.py:288
  592.7 131.8 %collective-permute-start.105 = (bf16[2048,512]{1,0:T(8,128)(2,1)}, bf16[2048,512]{1,0:T(8,128)(2,1)S(1)}, u32[]{:S(2)}, u32[]{:S(2)}) collective-permute-start(bf16[2048,512]{1,0:T(8,128)(2,1)} %get-tuple-element.317), channel_id=1, source_target_pairs={{0,1},{1,0},{2,3},{3,2},{4,5},{5,4},{6,7},{7,6},{8,9},{9,8},{10,11... | collective-permute-start | bytes 6291464 | tf_op jit(solution)/shard_map/ppermute | solution.py:474
  609.9 43.4 %collective-permute-start.83 = (bf16[4,8,16,512]{3,2,1,0:T(8,128)(2,1)S(1)}, bf16[4,8,16,512]{3,2,1,0:T(8,128)(2,1)S(1)}, u32[]{:S(2)}, u32[]{:S(2)}) collective-permute-start(bf16[4,8,16,512]{3,2,1,0:T(8,128)(2,1)S(1)} %copy-done.134), channel_id=1, source_target_pairs={{0,24},{2,26},{4,28},{6,30},{8,16},{10,18},{12,20},{14,22},{16,8},... | collective-permute-start | bytes 1572872 | tf_op jit(solution)/shard_map/ppermute | solution.py:288
  612.0 53.4 %collective-permute-start.82 = (bf16[4,8,16,512]{3,2,1,0:T(8,128)(2,1)S(1)}, bf16[4,8,16,512]{3,2,1,0:T(8,128)(2,1)S(1)}, u32[]{:S(2)}, u32[]{:S(2)}) collective-permute-start(bf16[4,8,16,512]{3,2,1,0:T(8,128)(2,1)S(1)} %copy-done.112), channel_id=1, source_target_pairs={{0,16},{2,18},{4,20},{6,22},{8,24},{10,26},{12,28},{14,30},{16,0},... | collective-permute-start | bytes 1572872 | tf_op jit(solution)/shard_map/ppermute | solution.py:288
  667.6 45.3 %collective-permute-start.87 = (bf16[4,8,16,512]{3,2,1,0:T(8,128)(2,1)}, bf16[4,8,16,512]{3,2,1,0:T(8,128)(2,1)S(1)}, u32[]{:S(2)}, u32[]{:S(2)}) collective-permute-start(bf16[4,8,16,512]{3,2,1,0:T(8,128)(2,1)} %get-tuple-element.295), channel_id=1, source_target_pairs={{0,8},{2,10},{4,12},{6,14},{8,0},{10,2},{12,4},{14,6},{16,24},{18,... | collective-permute-start | bytes 1572872 | tf_op jit(solution)/shard_map/ppermute | solution.py:288
  733.0 53.2 %collective-permute-start.106 = (bf16[1024,512]{1,0:T(8,128)(2,1)}, bf16[1024,512]{1,0:T(8,128)(2,1)}, u32[]{:S(2)}, u32[]{:S(2)}) collective-permute-start(bf16[1024,512]{1,0:T(8,128)(2,1)} %get-tuple-element.275.refs_7_), channel_id=1, source_target_pairs={{0,1},{1,0},{2,3},{3,2},{4,5},{5,4},{6,7},{7,6},{8,9},{9,8},{10,11... | collective-permute-start | bytes 3145736 | tf_op jit(solution)/shard_map/ppermute | solution.py:474
  734.0 53.3 %collective-permute-start.104 = (bf16[1024,512]{1,0:T(8,128)(2,1)}, bf16[1024,512]{1,0:T(8,128)(2,1)}, u32[]{:S(2)}, u32[]{:S(2)}) collective-permute-start(bf16[1024,512]{1,0:T(8,128)(2,1)} %get-tuple-element.316), channel_id=1, source_target_pairs={{0,1},{1,0},{2,3},{3,2},{4,5},{5,4},{6,7},{7,6},{8,9},{9,8},{10,11... | collective-permute-start | bytes 3145736 | tf_op jit(solution)/shard_map/ppermute | solution.py:474
  761.0 74.3 %collective-permute-start.107 = (bf16[1024,512]{1,0:T(8,128)(2,1)}, bf16[1024,512]{1,0:T(8,128)(2,1)S(1)}, u32[]{:S(2)}, u32[]{:S(2)}) collective-permute-start(bf16[1024,512]{1,0:T(8,128)(2,1)} %get-tuple-element.286.refs_7_), channel_id=1, source_target_pairs={{0,1},{1,0},{2,3},{3,2},{4,5},{5,4},{6,7},{7,6},{8,9},{9,8},{10,11... | collective-permute-start | bytes 3145736 | tf_op jit(solution)/shard_map/ppermute | solution.py:474
  773.9 61.5 %collective-permute-start.100 = (bf16[1024,512]{1,0:T(8,128)(2,1)}, bf16[1024,512]{1,0:T(8,128)(2,1)S(1)}, u32[]{:S(2)}, u32[]{:S(2)}) collective-permute-start(bf16[1024,512]{1,0:T(8,128)(2,1)} %get-tuple-element.313), channel_id=1, source_target_pairs={{0,1},{1,0},{2,3},{3,2},{4,5},{5,4},{6,7},{7,6},{8,9},{9,8},{10,11... | collective-permute-start | bytes 3145736 | tf_op jit(solution)/shard_map/ppermute | solution.py:474
  787.4 47.9 %collective-permute-start.96 = (bf16[4,8,16,512]{3,2,1,0:T(8,128)(2,1)S(1)}, bf16[4,8,16,512]{3,2,1,0:T(8,128)(2,1)S(1)}, u32[]{:S(2)}, u32[]{:S(2)}) collective-permute-start(bf16[4,8,16,512]{3,2,1,0:T(8,128)(2,1)S(1)} %copy-done.93), channel_id=1, source_target_pairs={{0,16},{2,18},{4,20},{6,22},{8,24},{10,26},{12,28},{14,30},{16,0},... | collective-permute-start | bytes 1572872 | tf_op jit(solution)/shard_map/ppermute | solution.py:288
  809.0 48.4 %collective-permute-start.98 = (bf16[4,8,16,512]{3,2,1,0:T(8,128)(2,1)}, bf16[4,8,16,512]{3,2,1,0:T(8,128)(2,1)S(1)}, u32[]{:S(2)}, u32[]{:S(2)}) collective-permute-start(bf16[4,8,16,512]{3,2,1,0:T(8,128)(2,1)} %get-tuple-element.309), channel_id=1, source_target_pairs={{0,8},{2,10},{4,12},{6,14},{8,0},{10,2},{12,4},{14,6},{16,24},{18,... | collective-permute-start | bytes 1572872 | tf_op jit(solution)/shard_map/ppermute | solution.py:288
  818.2 40.2 %collective-permute-start.109 = (bf16[4,8,16,512]{3,2,1,0:T(8,128)(2,1)}, bf16[4,8,16,512]{3,2,1,0:T(8,128)(2,1)S(1)}, u32[]{:S(2)}, u32[]{:S(2)}) collective-permute-start(bf16[4,8,16,512]{3,2,1,0:T(8,128)(2,1)} %get-tuple-element.325), channel_id=1, source_target_pairs={{0,8},{2,10},{4,12},{6,14},{8,0},{10,2},{12,4},{14,6},{16,24},{18,... | collective-permute-start | bytes 1572872 | tf_op jit(solution)/shard_map/ppermute | solution.py:288
  835.3 43.9 %collective-permute-start.112 = (bf16[1024,512]{1,0:T(8,128)(2,1)}, bf16[1024,512]{1,0:T(8,128)(2,1)S(1)}, u32[]{:S(2)}, u32[]{:S(2)}) collective-permute-start(bf16[1024,512]{1,0:T(8,128)(2,1)} %get-tuple-element.327), channel_id=1, source_target_pairs={{0,1},{1,0},{2,3},{3,2},{4,5},{5,4},{6,7},{7,6},{8,9},{9,8},{10,11... | collective-permute-start | bytes 3145736 | tf_op jit(solution)/shard_map/ppermute | solution.py:474
  835.4 48.6 %collective-permute-start.113 = (bf16[1024,512]{1,0:T(8,128)(2,1)S(1)}, bf16[1024,512]{1,0:T(8,128)(2,1)S(1)}, u32[]{:S(2)}, u32[]{:S(2)}) collective-permute-start(bf16[1024,512]{1,0:T(8,128)(2,1)S(1)} %copy-done.90), channel_id=1, source_target_pairs={{0,1},{1,0},{2,3},{3,2},{4,5},{5,4},{6,7},{7,6},{8,9},{9,8},{10,11... | collective-permute-start | bytes 3145736 | tf_op jit(solution)/shard_map/ppermute | solution.py:474
  857.4 55.3 %collective-permute-start.114 = (bf16[1024,512]{1,0:T(8,128)(2,1)}, bf16[1024,512]{1,0:T(8,128)(2,1)S(1)}, u32[]{:S(2)}, u32[]{:S(2)}) collective-permute-start(bf16[1024,512]{1,0:T(8,128)(2,1)} %get-tuple-element.322.refs_12_), channel_id=1, source_target_pairs={{0,1},{1,0},{2,3},{3,2},{4,5},{5,4},{6,7},{7,6},{8,9},{9,8},{10,11... | collective-permute-start | bytes 3145736 | tf_op jit(solution)/shard_map/ppermute | solution.py:474
  866.5 62.5 %collective-permute-start.108 = (bf16[1024,512]{1,0:T(8,128)(2,1)}, bf16[1024,512]{1,0:T(8,128)(2,1)S(1)}, u32[]{:S(2)}, u32[]{:S(2)}) collective-permute-start(bf16[1024,512]{1,0:T(8,128)(2,1)} %get-tuple-element.324), channel_id=1, source_target_pairs={{0,1},{1,0},{2,3},{3,2},{4,5},{5,4},{6,7},{7,6},{8,9},{9,8},{10,11... | collective-permute-start | bytes 3145736 | tf_op jit(solution)/shard_map/ppermute | solution.py:474
  879.3 43.7 %collective-permute-start.93 = (bf16[4,8,16,512]{3,2,1,0:T(8,128)(2,1)}, bf16[4,8,16,512]{3,2,1,0:T(8,128)(2,1)S(1)}, u32[]{:S(2)}, u32[]{:S(2)}) collective-permute-start(bf16[4,8,16,512]{3,2,1,0:T(8,128)(2,1)} %get-tuple-element.304.refs_12_), channel_id=1, source_target_pairs={{0,16},{2,18},{4,20},{6,22},{8,24},{10,26},{12,28},{14,30},{16,0},... | collective-permute-start | bytes 1572872 | tf_op jit(solution)/shard_map/ppermute | solution.py:288
  884.1 61.3 %collective-permute-start.95 = (bf16[4,8,16,512]{3,2,1,0:T(8,128)(2,1)}, bf16[4,8,16,512]{3,2,1,0:T(8,128)(2,1)S(1)}, u32[]{:S(2)}, u32[]{:S(2)}) collective-permute-start(bf16[4,8,16,512]{3,2,1,0:T(8,128)(2,1)} %get-tuple-element.306), channel_id=1, source_target_pairs={{0,8},{2,10},{4,12},{6,14},{8,0},{10,2},{12,4},{14,6},{16,24},{18,... | collective-permute-start | bytes 1572872 | tf_op jit(solution)/shard_map/ppermute | solution.py:288
  912.7 43.5 %collective-permute-start.117 = (bf16[1024,512]{1,0:T(8,128)(2,1)S(1)}, bf16[1024,512]{1,0:T(8,128)(2,1)S(1)}, u32[]{:S(2)}, u32[]{:S(2)}) collective-permute-start(bf16[1024,512]{1,0:T(8,128)(2,1)S(1)} %copy-done.91), channel_id=1, source_target_pairs={{0,1},{1,0},{2,3},{3,2},{4,5},{5,4},{6,7},{7,6},{8,9},{9,8},{10,11... | collective-permute-start | bytes 3145736 | tf_op jit(solution)/shard_map/ppermute | solution.py:474
  917.8 56.2 %collective-permute-start.116 = (bf16[1024,512]{1,0:T(8,128)(2,1)S(1)}, bf16[1024,512]{1,0:T(8,128)(2,1)S(1)}, u32[]{:S(2)}, u32[]{:S(2)}) collective-permute-start(bf16[1024,512]{1,0:T(8,128)(2,1)S(1)} %copy-done.130), channel_id=1, source_target_pairs={{0,1},{1,0},{2,3},{3,2},{4,5},{5,4},{6,7},{7,6},{8,9},{9,8},{10,11... | collective-permute-start | bytes 3145736 | tf_op jit(solution)/shard_map/ppermute | solution.py:474
  945.3 51.1 %collective-permute-start.118 = (bf16[1024,512]{1,0:T(8,128)(2,1)}, bf16[1024,512]{1,0:T(8,128)(2,1)S(1)}, u32[]{:S(2)}, u32[]{:S(2)}) collective-permute-start(bf16[1024,512]{1,0:T(8,128)(2,1)} %get-tuple-element.332.refs_9_), channel_id=1, source_target_pairs={{0,1},{1,0},{2,3},{3,2},{4,5},{5,4},{6,7},{7,6},{8,9},{9,8},{10,11... | collective-permute-start | bytes 3145736 | tf_op jit(solution)/shard_map/ppermute | solution.py:474
  954.2 64.7 %collective-permute-start.115 = (bf16[1024,512]{1,0:T(8,128)(2,1)}, bf16[1024,512]{1,0:T(8,128)(2,1)S(1)}, u32[]{:S(2)}, u32[]{:S(2)}) collective-permute-start(bf16[1024,512]{1,0:T(8,128)(2,1)} %get-tuple-element.334), channel_id=1, source_target_pairs={{0,1},{1,0},{2,3},{3,2},{4,5},{5,4},{6,7},{7,6},{8,9},{9,8},{10,11... | collective-permute-start | bytes 3145736 | tf_op jit(solution)/shard_map/ppermute | solution.py:474
  990.3 51.1 %collective-permute-start.120 = (bf16[1024,512]{1,0:T(8,128)(2,1)}, bf16[1024,512]{1,0:T(8,128)(2,1)S(1)}, u32[]{:S(2)}, u32[]{:S(2)}) collective-permute-start(bf16[1024,512]{1,0:T(8,128)(2,1)} %get-tuple-element.337.rest_0_), channel_id=1, source_target_pairs={{0,1},{1,0},{2,3},{3,2},{4,5},{5,4},{6,7},{7,6},{8,9},{9,8},{10,11... | collective-permute-start | bytes 3145736 | tf_op jit(solution)/shard_map/ppermute | solution.py:474
  (219 other events, 4321.6 us)

commit v3 on v2

--- a/solution.py
+++ b/solution.py
@@ -34,7 +34,7 @@
 
 
 def mixer_front(extra, pos_ref, x_ref, sums_ref, rim_ref, gain_ref, proj_ref, taps_ref, fwd_ref, twid_ref, *rest):
-    query_ref, across_ref, tail_ref, *out_refs = rest[extra:-1]
+    query_ref, across_ref, tail_ref, out_ref = rest[extra:-1]
     hist = rest[-1]
     step = pl.program_id(0)
     blocks, width, triple = proj_ref.shape
@@ -68,45 +68,29 @@
     source = jnp.concatenate(parts, axis=1)
     first = jnp.dot(fwd_ref[...], source, preferred_element_type=f32)
     first = (first * wide(column(twid_ref[0]), blocks * width)).astype(bf16)
-    inner, _, cols, _ = out_refs[0].shape
-    for k, ref in enumerate(out_refs):
-        for j in range(inner):
-            at = (k * inner + j) * cols
-            ref[j, 0] = first[at : at + cols]
-
-
-def regroup(count, *refs):
-    ins = refs[:count]
-    outs = refs[-(ins[0].shape[0] - 1) :]
-    for q, out in enumerate(outs):
-        for p in range(count):
-            out[p] = ins[p][q + 1]
-
-
-def mixer_middle(outer, inner, into, outof, *refs):
-    count = outer * inner
-    per = outer + inner - 1
-    ins, refs = refs[: per * len(into)], refs[per * len(into) :]
+    out_ref[:, 0] = first.reshape(out_ref.shape[0], *out_ref.shape[2:])
+
+
+def mixer_middle(into, outof, *refs):
+    ins, refs = refs[: len(into)], refs[len(into) :]
     fwd_ref, kernel_ref, inv_ref, twid_ref = refs[:4]
-    outs = refs[-2 - inner * len(outof) : -2]
+    outs = refs[-2 - len(outof) : -2]
     held, done = refs[-2:]
     step = pl.program_id(0)
-    cols, width = ins[0].shape[-2:]
+    count, _, cols, width = ins[0].shape
     lanes = width // 128
     root = fwd_ref.shape[0]
     rows = root // count
 
     @pl.when(step == 0)
     def _():
-        for c, (start, size) in enumerate(into):
-            for k in range(outer):
-                for j in range(inner):
-                    ref = ins[c * per + k].at[0] if j == 0 else ins[c * per + outer + j - 1].at[k]
-                    at = ((k * inner + j) * rows + start) * cols
-                    for l in range(lanes):
-                        held[l, at : at + size * cols, :] = (
-                            ref[:, :, l * 128 : (l + 1) * 128].astype(f32).reshape(size * cols, 128)
-                        )
+        for (start, size), ref in zip(into, ins):
+            for k in range(count):
+                at = (k * rows + start) * cols
+                for l in range(lanes):
+                    held[l, at : at + size * cols, :] = (
+                        ref[k, :, :, l * 128 : (l + 1) * 128].astype(f32).reshape(size * cols, 128)
+                    )
 
     table = jnp.concatenate(
         [held[l, pl.ds(step, root, stride=cols), :] for l in range(lanes)], axis=1
@@ -120,25 +104,19 @@
 
     @pl.when(step == cols - 1)
     def _():
-        for c, (start, size) in enumerate(outof):
-            for k in range(outer):
-                for j in range(inner):
-                    at = ((k * inner + j) * rows + 2 * start) * cols
-                    for l in range(lanes):
-                        outs[c * inner + j][k, :, :, l * 128 : (l + 1) * 128] = (
-                            done[l, at : at + 2 * size * cols, :]
-                            .astype(bf16)
-                            .reshape(2 * size, cols, 128)
-                        )
-
-
-def mixer_back(outer, inner, half, pos_ref, *refs):
-    ins = refs[: outer + inner - 1]
-    inv_ref, query_ref = refs[outer + inner - 1 : outer + inner + 1]
-    send_ref, own_ref = refs[-2:]
+        for (start, size), ref in zip(outof, outs):
+            for k in range(count):
+                at = (k * rows + 2 * start) * cols
+                for l in range(lanes):
+                    ref[k, :, :, l * 128 : (l + 1) * 128] = (
+                        done[l, at : at + 2 * size * cols, :].astype(bf16).reshape(2 * size, cols, 128)
+                    )
+
+
+def mixer_back(half, pos_ref, in_ref, inv_ref, query_ref, *rest):
+    send_ref, own_ref = rest[-2:]
     step = pl.program_id(0)
-    table = [r[0, 0] for r in ins[:inner]] + [r[j, 0] for r in ins[inner:] for j in range(inner)]
-    table = jnp.concatenate(table, axis=0)
+    table = in_ref[:, 0].reshape(inv_ref.shape[1], in_ref.shape[3])
     conv = jnp.dot(inv_ref[...], table, preferred_element_type=f32)
     gated = (query_ref[0].astype(f32) * conv).astype(bf16)
 
@@ -174,6 +152,10 @@
             out_ref[0, :, p * span : (p + 1) * span] = res
         else:
             send_ref[:, p * span - width : (p + 1) * span - width] = res
+
+
+def hold(*refs):
+    pass
 
 
 def place(pos_ref, got_ref, *rest):
@@ -212,23 +194,12 @@
     pos = jnp.stack([me, mp]).astype(jnp.int32)
     swap = [(0, 1), (1, 0)]
 
-    inner = 4
-    outer = count // inner
-    legs = [0] + list(range(outer // 2, outer)) + list(range(1, outer // 2))
-    turns = [k * inner + j for k in legs for j in range(inner)]
-    order = me ^ jnp.array(turns, jnp.int32)
-
-    def relative(table):
-        return jnp.take(
-            table.reshape(count, root // count, -1), order, axis=0, mode="clip"
-        ).reshape(root, -1)
-
-    fwd_in = relative(fwd_inner.T)
-    twid_in = relative(twid_inner.T).T.reshape(rows, 1, root)
-    fwd_out = relative(fwd_outer).T
-    inv_out = relative(inv_outer.T)
-    twid_out = relative(backward_twiddle).T.reshape(cols, 1, root)
-    inv_in = relative(inv_inner).T
+    fwd_in = fwd_inner.T
+    twid_in = twid_inner.reshape(rows, 1, root)
+    fwd_out = fwd_outer.T
+    inv_out = inv_outer.T
+    twid_out = backward_twiddle.T.reshape(cols, 1, root)
+    inv_in = inv_inner.T
     kernel_t = jnp.transpose(kernel, (1, 0, 2))
 
     def sumsq(x):
@@ -236,11 +207,16 @@
         part = jnp.sum(x * x, axis=-1)
         return part + lax.ppermute(part, "mp", swap)
 
-    rim = lax.ppermute(stream[:, toks - 2 :], "ctx", [(i, i + 1) for i in range(count - 1)])
+    ends = stream[:, toks - 2 :]
+    rim = lax.ppermute(ends, "ctx", [(i, i + 1) for i in range(count - 1)])
+    rim_other = lax.ppermute(
+        ends, ("ctx", "mp"), [(2 * i + m, 2 * (i + 1) + 1 - m) for i in range(count - 1) for m in range(2)]
+    )
     early, later = sumsq(stream[:1]), sumsq(stream[1:])
     sums = [(early[0] if s == 0 else later[s - 1]).reshape(rows, 1, root) for s in range(seqs)]
+    rim_sums = jnp.sum(rim.astype(f32) ** 2, axis=-1) + jnp.sum(rim_other.astype(f32) ** 2, axis=-1)
     rim_norm = (
-        rim.astype(f32) * lax.rsqrt(sumsq(rim)[..., None] / D + epsilon) * gain_mix.astype(f32)
+        rim.astype(f32) * lax.rsqrt(rim_sums[..., None] / D + epsilon) * gain_mix.astype(f32)
     ).astype(bf16)
     rim_proj = jnp.einsum(
         "xtlc,lcd->xltd", rim_norm.reshape(seqs, 2, blocks, block), proj_in, preferred_element_type=f32
@@ -283,47 +259,28 @@
     hbm = pl.BlockSpec(memory_space=pltpu.HBM)
     line = []
 
-    def over(parts, shifts, note=False):
-        got = [
-            p if k == 0 else lax.ppermute(p, "ctx", [(i, i ^ k) for i in range(count)])
-            for p, k in zip(parts, shifts)
-        ]
-        if note:
-            line.extend(got[1:])
-        return got
-
-    def over_outer(parts):
-        return over(parts, [k * inner for k in legs], True)
-
-    def over_inner(parts):
-        return over(parts, range(inner))
-
-    def regrouped(parts, after):
-        size = parts[0].shape[1]
-        step = max(size // 4, 1)
-        many = parts[0].shape[0] - 1
-        shape = jax.ShapeDtypeStruct((len(parts),) + parts[0].shape[1:], bf16)
-
-        def spec(n):
-            return pl.BlockSpec((n, step, cols, width), lambda i: (0, i, 0, 0))
-
+    def held_back(array, after):
         return pl.pallas_call(
-            functools.partial(regroup, len(parts)),
-            grid=(size // step,),
-            in_specs=[spec(many + 1)] * len(parts) + [hbm] * len(after),
-            out_specs=[spec(len(parts))] * many,
-            out_shape=[shape] * many,
-            compiler_params=params(),
-            cost_estimate=cost(4),
-            name="regroup",
-        )(*parts, *after)
+            hold,
+            in_specs=[hbm] * (1 + len(after)),
+            out_specs=hbm,
+            out_shape=jax.ShapeDtypeStruct(array.shape, array.dtype),
+            input_output_aliases={0: 0},
+            name="hold",
+        )(array, *after)
+
+    def exchanged(part, after=()):
+        if after:
+            part = held_back(part, after)
+        line.append(lax.all_to_all(part, "ctx", 0, 0, tiled=True))
+        return line[-1]
 
     def front(s, start, size, rim, held, after):
-        piece = jax.ShapeDtypeStruct((inner, size, cols, width), bf16)
+        piece = jax.ShapeDtypeStruct((count, size, cols, width), bf16)
         extra = list(after) + list(held)
         args = [pos, stream, sums[s], rim, gain_in, proj_in, short_taps, fwd_in, twid_in] + extra
         first = len(args) - 2
-        query, across, tail, *parts = pl.pallas_call(
+        query, across, tail, part = pl.pallas_call(
             functools.partial(mixer_front, len(extra)),
             grid_spec=pltpu.PrefetchScalarGridSpec(
                 num_scalar_prefetch=1,
@@ -344,7 +301,7 @@
                     pl.BlockSpec((root, width), lambda i, pos: ((start + i) // 2, 0)),
                     whole(rim),
                 ]
-                + [pl.BlockSpec((inner, 1, cols, width), lambda i, pos: (0, i, 0, 0))] * outer,
+                + [pl.BlockSpec((count, 1, cols, width), lambda i, pos: (0, i, 0, 0))],
                 scratch_shapes=[pltpu.VMEM((blocks, root + 8, 3 * block), f32)],
             ),
             out_shape=[
@@ -352,26 +309,23 @@
                 jax.ShapeDtypeStruct((toks // 2, width), bf16),
                 jax.ShapeDtypeStruct(rim.shape, f32),
             ]
-            + [piece] * outer,
+            + [piece],
             input_output_aliases={first: 0, first + 1: 1} if held else {},
             compiler_params=params(),
             cost_estimate=cost(1.25 * size),
             name="mixer_front",
         )(*args)
-        return (query, across), tail, parts
+        return (query, across), tail, part
 
     def middle(pieces, into, outof, after):
-        def specs(first, sizes):
-            return [
-                pl.BlockSpec((n,) + p, lambda i: (0, 0, 0, 0)) for p in sizes for n in first
-            ]
-
-        flat = [p for piece in pieces for p in piece]
-        shapes = [(2 * n, cols, width) for _, n in outof]
-        res = pl.pallas_call(
-            functools.partial(mixer_middle, outer, inner, into, outof),
+        def fixed(n):
+            return pl.BlockSpec((count, n, cols, width), lambda i: (0, 0, 0, 0))
+
+        sizes = [2 * n for _, n in outof]
+        return pl.pallas_call(
+            functools.partial(mixer_middle, into, outof),
             grid=(cols,),
-            in_specs=specs([1] * outer + [outer] * (inner - 1), [(n, cols, width) for _, n in into])
+            in_specs=[fixed(n) for _, n in into]
             + [
                 whole(fwd_out),
                 pl.BlockSpec((1, root, width), lambda i: (i, 0, 0)),
@@ -379,16 +333,15 @@
                 pl.BlockSpec((1, 1, root), lambda i: (i, 0, 0)),
             ]
             + [hbm] * len(after),
-            out_specs=specs([outer] * inner, shapes),
-            out_shape=[jax.ShapeDtypeStruct((outer,) + p, bf16) for p in shapes for _ in range(inner)],
+            out_specs=[fixed(n) for n in sizes],
+            out_shape=[jax.ShapeDtypeStruct((count, n, cols, width), bf16) for n in sizes],
             scratch_shapes=[pltpu.VMEM((width // 128, root * cols, 128), f32)] * 2,
             compiler_params=params(),
             cost_estimate=cost(20),
             name="mixer_middle",
-        )(*flat, fwd_out, kernel_t, inv_out, twid_out, *after)
-        return [res[c * inner : (c + 1) * inner] for c in range(len(outof))]
-
-    def back(parts, query, start, size, after):
+        )(*pieces, fwd_out, kernel_t, inv_out, twid_out, *after)
+
+    def back(part, query, start, size, after):
         def local(i, pos):
             return jnp.where(i < size, 2 * i + 1 - pos[1], 2 * (i - size) + pos[1])
 
@@ -397,13 +350,11 @@
 
         shape = jax.ShapeDtypeStruct((size * root, width), bf16)
         return pl.pallas_call(
-            functools.partial(mixer_back, outer, inner, size),
+            functools.partial(mixer_back, size),
             grid_spec=pltpu.PrefetchScalarGridSpec(
                 num_scalar_prefetch=1,
                 grid=(2 * size,),
-                in_specs=[pl.BlockSpec((1, 1, cols, width), lambda i, pos: (0, local(i, pos), 0, 0))] * inner
-                + [pl.BlockSpec((inner, 1, cols, width), lambda i, pos: (0, local(i, pos), 0, 0))]
-                * (outer - 1)
+                in_specs=[pl.BlockSpec((count, 1, cols, width), lambda i, pos: (0, local(i, pos), 0, 0))]
                 + [
                     whole(inv_in),
                     pl.BlockSpec((1, root, width), lambda i, pos: (0, row(i, pos), 0)),
@@ -418,7 +369,7 @@
             compiler_params=params(),
             cost_estimate=cost(1.8 * size),
             name="mixer_back",
-        )(pos, *parts, inv_in, query, *after)
+        )(pos, part, inv_in, query, *after)
 
     out_shape = jax.ShapeDtypeStruct(stream.shape, bf16)
 
@@ -463,8 +414,8 @@
     def cut(sizes):
         return [(sum(sizes[:i]), n) for i, n in enumerate(sizes)]
 
-    into = [cut([half, half])] * seqs
-    outof = [cut([half // 2, half // 2])] * seqs
+    into = [cut([half, half])] + [cut([rows])] * (seqs - 1)
+    outof = [cut([half])] * (seqs - 2) + [cut([half // 2, half // 2])] * 2
 
     firsts, queries, thirds, x_gots, gates, sent = {}, {}, {}, {}, {}, {}
     out = None
@@ -474,58 +425,43 @@
         return lax.ppermute(a, "mp", swap)
 
     def upto(n):
-        return [] if n is None else line[max(n - 3, 0) : n]
-
-    def do_front(s, c=0, n=None, extra=()):
+        return line[n - 1 : n] if n else []
+
+    def do_front(s, c=0, n=0, extra=()):
         nonlocal last
         start, size = into[s][c]
         rim, held = (rim_proj[s], ()) if c == 0 else queries[s]
-        held, rim, parts = front(
+        held, rim, part = front(
             s, start, size, rim, held, [*upto(n), *extra, *([] if last is None else [last])]
         )
         last = rim
         queries[s] = rim, held
-        firsts[s, c] = parts
+        firsts[s, c] = part
         if c + 1 == len(into[s]):
             x_gots[s] = swap_x(held[1])
 
-    def do_go(s, c):
-        firsts[s, c] = over_outer(firsts[s, c])
-
-    def do_turn(s, c=0, n=None, extra=()):
-        nonlocal last
-        parts = firsts[s, c]
-        res = regrouped(parts, [*upto(n), last, *extra])
-        last = res[0]
-        firsts[s, c] = parts + over_inner([None] + list(res))[1:]
-
-    def do_middle(s, n=None, extra=()):
+    def do_go(s, c=0, after=()):
+        firsts[s, c] = exchanged(firsts[s, c], after)
+
+    def do_middle(s, n=0, extra=()):
         nonlocal last
         pieces = [firsts[s, c] for c in range(len(into[s]))]
         res = middle(pieces, into[s], outof[s], [*upto(n), last, *extra])
-        last = res[0][0]
-        for c, parts in enumerate(res):
-            thirds[s, c] = over_inner(parts)
-
-    def do_return(s, c=0, n=None):
-        nonlocal last
-        parts = thirds[s, c]
-        res = regrouped(parts, [*upto(n), last])
         last = res[0]
-        thirds[s, c] = parts, res
-
-    def do_send(s, c=0):
-        parts, res = thirds[s, c]
-        thirds[s, c] = parts + over_outer([None] + list(res))[1:]
-
-    def do_back(s, c=0, n=None, extra=()):
+        for c, part in enumerate(res):
+            thirds[s, c] = part
+
+    def do_send(s, c=0, after=()):
+        thirds[s, c] = exchanged(thirds[s, c], after)
+
+    def do_back(s, c=0, n=0, extra=()):
         nonlocal last
         start, size = outof[s][c]
         send, own = back(thirds[s, c], queries[s][1][0], start, size, [*upto(n), last, *extra])
         last = own
         gates[s, c] = own, swap_x(send)
 
-    def do_mlp(s, c=0, n=None, extra=()):
+    def do_mlp(s, c=0, n=0, extra=()):
         nonlocal last, out
         start, size = outof[s][c]
         out, send = channels(s, start, size, *gates[s, c], x_gots[s], out, [*upto(n), last, *extra])
@@ -536,73 +472,40 @@
         nonlocal out
         out = placed(s, *outof[s][c], sent[s, c], out)
 
-    def at(groups):
-        return int(groups * (outer - 1))
-
     do_front(0, 0)
     do_go(0, 0)
-    do_front(0, 1)
+    do_front(0, 1, extra=[sums[1]])
     do_go(0, 1)
-    do_front(1, 0, n=1)
-    do_go(1, 0)
-    do_front(1, 1, n=2)
-    do_go(1, 1)
-    do_turn(0, 0, n=3)
-    do_front(2, 0, n=4)
-    do_go(2, 0)
-    do_front(2, 1, n=5)
-    do_go(2, 1)
-    do_turn(0, 1, n=6)
-    do_middle(0, n=7, extra=[packed_got])
-    do_front(3, 0, n=8)
-    do_turn(1, 0, n=9)
-    do_front(3, 1, n=10)
-    do_return(0, 0, n=11)
-    do_send(0, 0)
-    do_return(0, 1, n=11)
-    do_send(0, 1)
-    do_go(3, 0)
-    do_go(3, 1)
-    do_turn(1, 1, n=12)
-    do_middle(1, n=14, extra=[x_gots[0]])
-    do_turn(2, 0, n=15)
-    do_return(1, 0, n=16)
-    do_send(1, 0)
-    do_return(1, 1, n=17)
-    do_send(1, 1)
-    do_turn(2, 1, n=18)
-    do_middle(2, n=20, extra=[x_gots[1]])
-    do_back(0, 0, n=21)
-    do_return(2, 0, n=22)
-    do_send(2, 0)
-    do_return(2, 1, n=23)
-    do_send(2, 1)
-    do_back(0, 1, n=24)
-    do_mlp(0, 0, n=26)
-    do_turn(3, 0, n=27, extra=[x_gots[2]])
-    do_mlp(0, 1, n=29)
-    do_turn(3, 1, n=30)
-    do_middle(3, n=32)
-    do_back(1, 0, n=33)
-    do_place(0, 0)
-    do_return(3, 0, n=34)
-    do_send(3, 0)
-    do_return(3, 1, n=35)
-    do_send(3, 1)
-    do_back(1, 1, n=36)
-    do_mlp(1, 0, n=38, extra=[x_gots[3]])
-    do_place(0, 1)
-    do_back(2, 0, n=39)
-    do_mlp(1, 1, n=41)
-    do_place(1, 0)
-    do_back(2, 1, n=42)
-    do_mlp(2, 0, n=44)
-    do_place(1, 1)
-    do_back(3, 0, n=45)
-    do_mlp(2, 1, n=47)
+    do_front(1, n=1)
+    do_go(1, 0, [x_gots[0]])
+    do_middle(0, n=2)
+    do_front(2, n=2)
+    do_send(0, 0, [last, x_gots[1]])
+    do_middle(1, n=3)
+    do_front(3, n=3)
+    do_send(1, 0, [last, x_gots[2]])
+    do_back(0, n=4)
+    do_go(2, 0, [last, x_gots[3], packed_got])
+    do_back(1, n=5)
+    do_mlp(0, n=5)
+    do_go(3, 0, [last, gates[1, 0][1]])
+    do_middle(2, n=6)
+    do_mlp(1, n=6)
+    do_send(2, 0, [last, sent[0, 0]])
+    do_middle(3, n=7)
+    do_send(2, 1, [last, sent[1, 0]])
+    do_back(2, 0, n=8)
+    do_place(0)
+    do_send(3, 0, [last, gates[2, 0][1]])
+    do_back(2, 1, n=9)
+    do_mlp(2, 0, n=9)
+    do_send(3, 1, [last, gates[2, 1][1]])
+    do_back(3, 0, n=10)
+    do_mlp(2, 1, n=10)
+    do_place(1)
     do_back(3, 1)
+    do_mlp(3, 0)
     do_place(2, 0)
-    do_mlp(3, 0)
     do_place(2, 1)
     do_mlp(3, 1)
     do_place(3, 0)

time: 1070 us -> 961 us (0.90)
  Pallas kernels: 462 us -> 370 us
  starting transfers between devices: 201 us -> 167 us
  waiting for transfers between devices: 328 us -> 345 us
    ppermute x97 -> x2, waiting for transfers between devices: 262 us -> 0.01 us  [the longest x1 0.01 us: body(): lax.ppermute(ends, ('ctx', 'mp'), [(2 * i + m, 2 * (i + 1) + 1 - m) for i...]
    ppermute x97 -> x2, starting transfers between devices: 177 us -> 7.95 us  [the longest x1 4.41 us: body(): lax.ppermute(ends, ('ctx', 'mp'), [(2 * i + m, 2 * (i + 1) + 1 - m) for i...]
    all_to_all x0 -> x11, starting transfers between devices: none -> 136 us  [exchanged(): line.append(lax.all_to_all(part, 'ctx', 0, 0, tiled=True))]
    all_to_all x0 -> x11, waiting for transfers between devices: none -> 128 us  [exchanged(): line.append(lax.all_to_all(part, 'ctx', 0, 0, tiled=True))]
    ppermute x20 -> x16, waiting for transfers between devices: 63.9 us -> 160 us  [swap_x(): return lax.ppermute(a, 'mp', swap)]
    pallas_call x28 -> x19, Pallas kernels: 208 us -> 139 us  [the longest x4 80.9 us: middle(): pl.pallas_call(functools.partial(mixer_middle, into, outof), grid=(cols,)...]
    ppermute x1, waiting for transfers between devices: 0.01 us -> 54.7 us  [body(): packed_got = lax.ppermute(packed, 'mp', swap)]
    pallas_call x8 -> x5, Pallas kernels: 98.3 us -> 88.7 us  [front(): pl.pallas_call(functools.partial(mixer_front, len(extra)), grid_spec=pltp...]
  transfers between devices with their start and end apart: 121 -> 32, of which waited for: 40 -> 23; matrix products, arithmetic and copies ran while one was open for 5% -> 5% of each run, Pallas kernels for 43% -> 37%
where the time goes in v3:
time: 961 us; the launch traced here: 951 us
  Pallas kernels  370 us (39%)
  waiting for transfers between devices  345 us (36%)
  starting transfers between devices  167 us (17%)
  local copies, waits for them, and re-layouts  45.7 us (5%)
  other arithmetic  21.4 us (2%)
    ppermute x16, waiting for transfers between devices, swap_x(): return lax.ppermute(a, 'mp', swap)  160 us
    all_to_all x11, starting transfers between devices, exchanged(): line.append(lax.all_to_all(part, 'ctx', 0, 0, tiled=True))  136 us
    all_to_all x11, waiting for transfers between devices, exchanged(): line.append(lax.all_to_all(part, 'ctx', 0, 0, tiled=True))  128 us
    pallas_call x6, Pallas kernels, channels(): pl.pallas_call(mlp, grid_spec=pltpu.PrefetchScalarGridSpec(num_scalar_pre...  114 us
    pallas_call x5, Pallas kernels, front(): pl.pallas_call(functools.partial(mixer_front, len(extra)), grid_spec=pltp...  88.7 us
    pallas_call x4, Pallas kernels, middle(): pl.pallas_call(functools.partial(mixer_middle, into, outof), grid=(cols,)...  80.9 us
    pallas_call x6, Pallas kernels, back(): pl.pallas_call(functools.partial(mixer_back, size), grid_spec=pltpu.Prefe...  57.8 us
    ppermute x1, waiting for transfers between devices, body(): packed_got = lax.ppermute(packed, 'mp', swap)  54.7 us
  transfers between devices with their start and end apart: 32, of which 23 were waited for; matrix products, arithmetic and copies ran while one was open for 5% of the time, Pallas kernels for 37%

profile of v3, /device:TPU:0, one launch (start us, length us, event | category | flops | bytes accessed | tf_op | source)
XLA Modules:
  0.0 950.6 jit_solution(7931624130099167354)
XLA Ops:
  16.3 12.0 %mixer_front.5 = (bf16[1,4096,512]{2,1,0:T(8,128)(2,1)}, bf16[2048,512]{1,0:T(8,128)(2,1)}, f32[4,8,384]{2,1,0:T(8,128)}, bf16[16,8,16,512]{3,2,1,0:T(8,128)(2,1)}) custom-call(s32[2]{0:T(128)} %pad_add_fusion.pos_ref, bf16[4,4096,512]{2,1,0:T(8,128)(2,1)} %x_own_ref.11, f32[16,1,256]{2,1,0:T(1,128)} %bitcast.101, f32[4,8,384]{2,1,0:T(8,128)} %get-tuple-element.110.rim_ref, ...), custom_call_target="tpu_custom_call" | custom-call | bytes 36000000 | tf_op jit(solution)/shard_map/mixer_front/pallas_call | solution.py:283
  33.3 7.2 multiply_reduce_fusion
  45.7 12.1 %mixer_front.6 = (bf16[1,4096,512]{2,1,0:T(8,128)(2,1)}, bf16[2048,512]{1,0:T(8,128)(2,1)}, f32[4,8,384]{2,1,0:T(8,128)}, bf16[16,8,16,512]{3,2,1,0:T(8,128)(2,1)}) custom-call(s32[2]{0:T(128)} %pad_add_fusion.pos_ref, bf16[4,4096,512]{2,1,0:T(8,128)(2,1)} %x_own_ref.11, f32[16,1,256]{2,1,0:T(1,128)} %bitcast.102, ...), custom_call_target="tpu_custom_call", output_to_operand_aliasing={{0}: (11, {}), {1}: (12, {})} | custom-call | bytes 36000000 | tf_op jit(solution)/shard_map/mixer_front/pallas_call | solution.py:283
  57.7 16.7 %all-to-all-done.rest_0_.refs_0_ = bf16[16,8,16,512]{3,2,1,0:T(8,128)(2,1)S(1)} async-done(((bf16[16,8,16,512]{3,2,1,0:T(8,128)(2,1)}), bf16[16,8,16,512]{3,2,1,0:T(8,128)(2,1)S(1)}, u32[]{:S(2)}, u32[]{:S(2)}) %all-to-all-start) | async-done | bytes 2097184 | tf_op jit(solution)/shard_map/all_to_all | solution.py:275
  75.8 11.2 %all-to-all-start.2 = ((bf16[16,8,16,512]{3,2,1,0:T(8,128)(2,1)}), bf16[16,8,16,512]{3,2,1,0:T(8,128)(2,1)S(1)}, u32[]{:S(2)}, u32[]{:S(2)}) async-start(bf16[16,8,16,512]{3,2,1,0:T(8,128)(2,1)} %get-tuple-element.60), calls=%async_computation.2 | async-start | bytes 4194304 | tf_op jit(solution)/shard_map/all_to_all | solution.py:275
  88.5 21.5 %mixer_front.7 = (bf16[1,4096,512]{2,1,0:T(8,128)(2,1)}, bf16[2048,512]{1,0:T(8,128)(2,1)}, f32[4,8,384]{2,1,0:T(8,128)}, bf16[16,16,16,512]{3,2,1,0:T(8,128)(2,1)}) custom-call(s32[2]{0:T(128)} %pad_add_fusion.pos_ref, bf16[4,4096,512]{2,1,0:T(8,128)(2,1)} %x_own_ref.11, f32[16,1,256]{2,1,0:T(1,128)} %bitcast.104, f32[4,8,384]{2,1,0:T(8,128)} %get-tuple-element.111.rim_ref, ...), custom_call_target="tpu_custom_call" | custom-call | bytes 72000000 | tf_op jit(solution)/shard_map/mixer_front/pallas_call | solution.py:283
  110.0 25.2 %collective-permute-done.4.refs_1_.x_got_ref = bf16[2048,512]{1,0:T(8,128)(2,1)} collective-permute-done((bf16[2048,512]{1,0:T(8,128)(2,1)}, bf16[2048,512]{1,0:T(8,128)(2,1)}, u32[]{:S(2)}, u32[]{:S(2)}) %collective-permute-start.4) | collective-permute-done | bytes 2097184 | tf_op jit(solution)/shard_map/ppermute | solution.py:425
  136.6 6.1 all-to-all-start.1
  146.3 6.6 copy.73
  152.9 20.1 %mixer_middle.4.rest_1_.refs_0_ = bf16[16,16,16,512]{3,2,1,0:T(8,128)(2,1)} custom-call(bf16[16,8,16,512]{3,2,1,0:T(8,128)(2,1)} %copy-done.5, bf16[16,8,16,512]{3,2,1,0:T(8,128)(2,1)} %copy-done.2, bf16[256,256]{1,0:T(8,128)(2,1)} %bitcast.86, bf16[16,256,512]{2,1,0:T(8,128)(2,1)} %bitcast.58, bf16[256,256]{1,0:T(8,128)(2,1)} %bitcast.90, ...), custom_call_target="tpu_custom_call" | custom-call | bytes 72000000 | tf_op jit(solution)/shard_map/mixer_middle/pallas_call | solution.py:325
  173.0 21.5 %mixer_front.8 = (bf16[1,4096,512]{2,1,0:T(8,128)(2,1)}, bf16[2048,512]{1,0:T(8,128)(2,1)}, f32[4,8,384]{2,1,0:T(8,128)}, bf16[16,16,16,512]{3,2,1,0:T(8,128)(2,1)}) custom-call(s32[2]{0:T(128)} %pad_add_fusion.pos_ref, bf16[4,4096,512]{2,1,0:T(8,128)(2,1)} %x_own_ref.11, f32[16,1,256]{2,1,0:T(1,128)} %bitcast.113, f32[4,8,384]{2,1,0:T(8,128)} %get-tuple-element.109.rim_ref, ...), custom_call_target="tpu_custom_call" | custom-call | bytes 72000000 | tf_op jit(solution)/shard_map/mixer_front/pallas_call | solution.py:283
  195.9 24.5 %all-to-all-done.1.refs_0_.refs_5_.rest_0_ = bf16[16,16,16,512]{3,2,1,0:T(8,128)(2,1)} async-done(((bf16[16,16,16,512]{3,2,1,0:T(8,128)(2,1)}), bf16[16,16,16,512]{3,2,1,0:T(8,128)(2,1)}, u32[]{:S(2)}, u32[]{:S(2)}) %all-to-all-start.1) | async-done | bytes 4194336 | tf_op jit(solution)/shard_map/all_to_all | solution.py:275
  220.3 19.7 %all-to-all-start.3 = ((bf16[16,16,16,512]{3,2,1,0:T(8,128)(2,1)}), bf16[16,16,16,512]{3,2,1,0:T(8,128)(2,1)}, u32[]{:S(2)}, u32[]{:S(2)}) async-start(bf16[16,16,16,512]{3,2,1,0:T(8,128)(2,1)} %hold.10), calls=%async_computation.3 | async-start | bytes 8388608 | tf_op jit(solution)/shard_map/all_to_all | solution.py:275
  241.5 20.2 %mixer_middle.5.rest_1_.refs_0_ = bf16[16,16,16,512]{3,2,1,0:T(8,128)(2,1)} custom-call(bf16[16,16,16,512]{3,2,1,0:T(8,128)(2,1)} %all-to-all-done.1.refs_0_.refs_5_.rest_0_, bf16[256,256]{1,0:T(8,128)(2,1)} %bitcast.87, bf16[16,256,512]{2,1,0:T(8,128)(2,1)} %bitcast.59, bf16[256,256]{1,0:T(8,128)(2,1)} %bitcast.91, f32[16,1,256]{2,1,0:T(1,128)} %reshape.95.refs_5_.refs_4_, ...), custom_call_target="tpu_custom_call" | custom-call | bytes 72000000 | tf_op jit(solution)/shard_map/mixer_middle/pallas_call | solution.py:325
  261.8 21.5 %mixer_front.9 = (bf16[1,4096,512]{2,1,0:T(8,128)(2,1)}, bf16[2048,512]{1,0:T(8,128)(2,1)}, f32[4,8,384]{2,1,0:T(8,128)}, bf16[16,16,16,512]{3,2,1,0:T(8,128)(2,1)}) custom-call(s32[2]{0:T(128)} %pad_add_fusion.pos_ref, bf16[4,4096,512]{2,1,0:T(8,128)(2,1)} %x_own_ref.11, f32[16,1,256]{2,1,0:T(1,128)} %bitcast.112, f32[4,8,384]{2,1,0:T(8,128)} %get-tuple-element.112.rim_ref, ...), custom_call_target="tpu_custom_call" | custom-call | bytes 72000000 | tf_op jit(solution)/shard_map/mixer_front/pallas_call | solution.py:283
  289.4 28.3 %all-to-all-done.3.in_ref.rest_0_ = bf16[16,16,16,512]{3,2,1,0:T(8,128)(2,1)} async-done(((bf16[16,16,16,512]{3,2,1,0:T(8,128)(2,1)}), bf16[16,16,16,512]{3,2,1,0:T(8,128)(2,1)}, u32[]{:S(2)}, u32[]{:S(2)}) %all-to-all-start.3) | async-done | bytes 4194336 | tf_op jit(solution)/shard_map/all_to_all | solution.py:275
  317.7 19.7 %all-to-all-start.4 = ((bf16[16,16,16,512]{3,2,1,0:T(8,128)(2,1)}), bf16[16,16,16,512]{3,2,1,0:T(8,128)(2,1)}, u32[]{:S(2)}, u32[]{:S(2)}) async-start(bf16[16,16,16,512]{3,2,1,0:T(8,128)(2,1)} %hold.11), calls=%async_computation.4 | async-start | bytes 8388608 | tf_op jit(solution)/shard_map/all_to_all | solution.py:275
  342.7 13.4 %mixer_back.6 = (bf16[2048,512]{1,0:T(8,128)(2,1)}, bf16[2048,512]{1,0:T(8,128)(2,1)}) custom-call(s32[2]{0:T(128)} %pad_add_fusion.pos_ref, bf16[16,16,16,512]{3,2,1,0:T(8,128)(2,1)} %all-to-all-done.3.in_ref.rest_0_, bf16[256,256]{1,0:T(8,128)(2,1)} %bitcast.69, bf16[1,4096,512]{2,1,0:T(8,128)(2,1)} %get-tuple-element.65.query_ref, ...), custom_call_target="tpu_custom_call" | custom-call | bytes 51840000 | tf_op jit(solution)/shard_map/mixer_back/pallas_call | solution.py:352
  356.2 54.7 %collective-permute-done.7.refs_3_ = bf16[4612,128]{1,0:T(8,128)(2,1)S(1)} collective-permute-done((bf16[4612,128]{1,0:T(8,128)(2,1)}, bf16[4612,128]{1,0:T(8,128)(2,1)S(1)}, u32[]{:S(2)}, u32[]{:S(2)}) %collective-permute-start.7) | collective-permute-done | bytes 1180704 | tf_op jit(solution)/shard_map/ppermute | solution.py:229
  415.1 20.2 %all-to-all-start.6 = ((bf16[16,16,16,512]{3,2,1,0:T(8,128)(2,1)}), bf16[16,16,16,512]{3,2,1,0:T(8,128)(2,1)}, u32[]{:S(2)}, u32[]{:S(2)}) async-start(bf16[16,16,16,512]{3,2,1,0:T(8,128)(2,1)} %hold.13), calls=%async_computation.6 | async-start | bytes 8388608 | tf_op jit(solution)/shard_map/all_to_all | solution.py:275
  440.0 13.4 %mixer_back.7 = (bf16[2048,512]{1,0:T(8,128)(2,1)}, bf16[2048,512]{1,0:T(8,128)(2,1)}) custom-call(s32[2]{0:T(128)} %pad_add_fusion.pos_ref, bf16[16,16,16,512]{3,2,1,0:T(8,128)(2,1)} %all-to-all-done.4.in_ref.rest_0_, bf16[256,256]{1,0:T(8,128)(2,1)} %bitcast.70, bf16[1,4096,512]{2,1,0:T(8,128)(2,1)} %get-tuple-element.70.query_ref, ...), custom_call_target="tpu_custom_call" | custom-call | bytes 51840000 | tf_op jit(solution)/shard_map/mixer_back/pallas_call | solution.py:352
  470.6 16.8 %collective-permute-done.6.got_ref = bf16[2048,512]{1,0:T(8,128)(2,1)} collective-permute-done((bf16[2048,512]{1,0:T(8,128)(2,1)}, bf16[2048,512]{1,0:T(8,128)(2,1)}, u32[]{:S(2)}, u32[]{:S(2)}) %collective-permute-start.6) | collective-permute-done | bytes 2097184 | tf_op jit(solution)/shard_map/ppermute | solution.py:425
  487.4 26.3 %mlp.6 = (bf16[4,4096,512]{2,1,0:T(8,128)(2,1)}, bf16[2048,512]{1,0:T(8,128)(2,1)}) custom-call(s32[2]{0:T(128)} %pad_add_fusion.pos_ref, bf16[2048,512]{1,0:T(8,128)(2,1)} %get-tuple-element.67.rest_1_.own_ref.refs_1_, bf16[2048,512]{1,0:T(8,128)(2,1)} %collective-permute-done.6.got_ref, bf16[4,4096,512]{2,1,0:T(8,128)(2,1)} %x_own_ref.11, ...), custom_call_target="tpu_custom_call" | custom-call | bytes 92160000 | tf_op jit(solution)/shard_map/mlp/pallas_call | solution.py:384
  513.7 18.1 %collective-permute-done.9.refs_2_.got_ref = bf16[2048,512]{1,0:T(8,128)(2,1)S(1)} collective-permute-done((bf16[2048,512]{1,0:T(8,128)(2,1)}, bf16[2048,512]{1,0:T(8,128)(2,1)S(1)}, u32[]{:S(2)}, u32[]{:S(2)}) %collective-permute-start.9) | collective-permute-done | bytes 2097184 | tf_op jit(solution)/shard_map/ppermute | solution.py:425
  540.6 20.3 %mixer_middle.6 = (bf16[16,8,16,512]{3,2,1,0:T(8,128)(2,1)}, bf16[16,8,16,512]{3,2,1,0:T(8,128)(2,1)}) custom-call(bf16[16,16,16,512]{3,2,1,0:T(8,128)(2,1)} %all-to-all-done.6.refs_0_.refs_5_.rest_0_, bf16[256,256]{1,0:T(8,128)(2,1)} %bitcast.88, bf16[16,256,512]{2,1,0:T(8,128)(2,1)} %bitcast.60, bf16[256,256]{1,0:T(8,128)(2,1)} %bitcast.92, ...), custom_call_target="tpu_custom_call" | custom-call | bytes 72000000 | tf_op jit(solution)/shard_map/mixer_middle/pallas_call | solution.py:325
  560.9 26.3 %mlp.7 = (bf16[4,4096,512]{2,1,0:T(8,128)(2,1)}, bf16[2048,512]{1,0:T(8,128)(2,1)}) custom-call(s32[2]{0:T(128)} %pad_add_fusion.pos_ref, bf16[2048,512]{1,0:T(8,128)(2,1)} %get-tuple-element.71.rest_1_.own_ref, bf16[2048,512]{1,0:T(8,128)(2,1)} %copy-done.10, bf16[4,4096,512]{2,1,0:T(8,128)(2,1)} %x_own_ref.11, ...), custom_call_target="tpu_custom_call", output_to_operand_aliasing={{0}: (11, {})} | custom-call | bytes 92160000 | tf_op jit(solution)/shard_map/mlp/pallas_call | solution.py:384
  588.8 28.0 %all-to-all-done.5.refs_0_.refs_5_ = bf16[16,16,16,512]{3,2,1,0:T(8,128)(2,1)} async-done(((bf16[16,16,16,512]{3,2,1,0:T(8,128)(2,1)}), bf16[16,16,16,512]{3,2,1,0:T(8,128)(2,1)}, u32[]{:S(2)}, u32[]{:S(2)}) %all-to-all-start.5) | async-done | bytes 4194336 | tf_op jit(solution)/shard_map/all_to_all | solution.py:275
  616.8 19.6 %all-to-all-start.7 = ((bf16[16,8,16,512]{3,2,1,0:T(8,128)(2,1)}), bf16[16,8,16,512]{3,2,1,0:T(8,128)(2,1)S(1)}, u32[]{:S(2)}, u32[]{:S(2)}) async-start(bf16[16,8,16,512]{3,2,1,0:T(8,128)(2,1)} %hold.14), calls=%async_computation.7 | async-start | bytes 4194304 | tf_op jit(solution)/shard_map/all_to_all | solution.py:275
  637.9 20.2 %mixer_middle.7 = (bf16[16,8,16,512]{3,2,1,0:T(8,128)(2,1)}, bf16[16,8,16,512]{3,2,1,0:T(8,128)(2,1)}) custom-call(bf16[16,16,16,512]{3,2,1,0:T(8,128)(2,1)} %all-to-all-done.5.refs_0_.refs_5_, bf16[256,256]{1,0:T(8,128)(2,1)} %bitcast.89, bf16[16,256,512]{2,1,0:T(8,128)(2,1)} %bitcast.61, bf16[256,256]{1,0:T(8,128)(2,1)} %bitcast.93, ...), custom_call_target="tpu_custom_call" | custom-call | bytes 72000000 | tf_op jit(solution)/shard_map/mixer_middle/pallas_call | solution.py:325
  658.1 26.5 %collective-permute-done.13.refs_2_.got_ref = bf16[2048,512]{1,0:T(8,128)(2,1)} collective-permute-done((bf16[2048,512]{1,0:T(8,128)(2,1)}, bf16[2048,512]{1,0:T(8,128)(2,1)}, u32[]{:S(2)}, u32[]{:S(2)}) %collective-permute-start.13) | collective-permute-done | bytes 2097184 | tf_op jit(solution)/shard_map/ppermute | solution.py:425
  691.7 7.7 mixer_back.8
  700.9 24.3 %collective-permute-done.12.got_ref.refs_2_ = bf16[1024,512]{1,0:T(8,128)(2,1)S(1)} collective-permute-done((bf16[1024,512]{1,0:T(8,128)(2,1)}, bf16[1024,512]{1,0:T(8,128)(2,1)S(1)}, u32[]{:S(2)}, u32[]{:S(2)}) %collective-permute-start.12) | collective-permute-done | bytes 1048608 | tf_op jit(solution)/shard_map/ppermute | solution.py:425
  726.1 6.7 all-to-all-done.8.in_ref.rest_0_
  734.1 11.2 %all-to-all-start.10 = ((bf16[16,8,16,512]{3,2,1,0:T(8,128)(2,1)}), bf16[16,8,16,512]{3,2,1,0:T(8,128)(2,1)S(1)}, u32[]{:S(2)}, u32[]{:S(2)}) async-start(bf16[16,8,16,512]{3,2,1,0:T(8,128)(2,1)} %hold.17), calls=%async_computation.10 | async-start | bytes 4194304 | tf_op jit(solution)/shard_map/all_to_all | solution.py:275
  745.4 7.7 mixer_back.9
  754.5 6.3 place.6.rest_2_
  760.8 15.3 %mlp.8 = (bf16[4,4096,512]{2,1,0:T(8,128)(2,1)}, bf16[1024,512]{1,0:T(8,128)(2,1)}) custom-call(s32[2]{0:T(128)} %pad_add_fusion.pos_ref, bf16[1024,512]{1,0:T(8,128)(2,1)} %get-tuple-element.82.rest_1_.own_ref.refs_1_, bf16[1024,512]{1,0:T(8,128)(2,1)} %copy-done.18, bf16[4,4096,512]{2,1,0:T(8,128)(2,1)} %x_own_ref.11, ...), custom_call_target="tpu_custom_call", output_to_operand_aliasing={{0}: (11, {})} | custom-call | bytes 46080000 | tf_op jit(solution)/shard_map/mlp/pallas_call | solution.py:384
  779.8 6.7 all-to-all-done.10.in_ref.rest_0_
  787.9 11.5 %all-to-all-start.9 = ((bf16[16,8,16,512]{3,2,1,0:T(8,128)(2,1)}), bf16[16,8,16,512]{3,2,1,0:T(8,128)(2,1)}, u32[]{:S(2)}, u32[]{:S(2)}) async-start(bf16[16,8,16,512]{3,2,1,0:T(8,128)(2,1)} %hold.16), calls=%async_computation.9 | async-start | bytes 4194304 | tf_op jit(solution)/shard_map/all_to_all | solution.py:275
  799.4 7.8 mixer_back.10
  809.2 15.3 %mlp.9 = (bf16[4,4096,512]{2,1,0:T(8,128)(2,1)}, bf16[1024,512]{1,0:T(8,128)(2,1)}) custom-call(s32[2]{0:T(128)} %pad_add_fusion.pos_ref, bf16[1024,512]{1,0:T(8,128)(2,1)} %get-tuple-element.85.rest_1_.own_ref, bf16[1024,512]{1,0:T(8,128)(2,1)} %copy-done.17, bf16[4,4096,512]{2,1,0:T(8,128)(2,1)} %x_own_ref.11, ...), custom_call_target="tpu_custom_call", output_to_operand_aliasing={{0}: (11, {})} | custom-call | bytes 46080000 | tf_op jit(solution)/shard_map/mlp/pallas_call | solution.py:384
  826.0 14.5 %all-to-all-done.9.in_ref = bf16[16,8,16,512]{3,2,1,0:T(8,128)(2,1)} async-done(((bf16[16,8,16,512]{3,2,1,0:T(8,128)(2,1)}), bf16[16,8,16,512]{3,2,1,0:T(8,128)(2,1)}, u32[]{:S(2)}, u32[]{:S(2)}) %all-to-all-start.9) | async-done | bytes 2097184 | tf_op jit(solution)/shard_map/all_to_all | solution.py:275
  840.5 7.7 mixer_back.11
  849.6 6.3 place.7.rest_1_
  855.9 15.3 %mlp.10 = (bf16[4,4096,512]{2,1,0:T(8,128)(2,1)}, bf16[1024,512]{1,0:T(8,128)(2,1)}) custom-call(s32[2]{0:T(128)} %pad_add_fusion.pos_ref, bf16[1024,512]{1,0:T(8,128)(2,1)} %get-tuple-element.90.rest_1_.own_ref, bf16[1024,512]{1,0:T(8,128)(2,1)} %collective-permute-done.16.got_ref, ...), custom_call_target="tpu_custom_call", output_to_operand_aliasing={{0}: (10, {})} | custom-call | bytes 46080000 | tf_op jit(solution)/shard_map/mlp/pallas_call | solution.py:384
  883.4 17.4 %collective-permute-done.15.got_ref = bf16[1024,512]{1,0:T(8,128)(2,1)S(1)} collective-permute-done((bf16[1024,512]{1,0:T(8,128)(2,1)}, bf16[1024,512]{1,0:T(8,128)(2,1)S(1)}, u32[]{:S(2)}, u32[]{:S(2)}) %collective-permute-start.15) | collective-permute-done | bytes 1048608 | tf_op jit(solution)/shard_map/ppermute | solution.py:425
  901.8 15.3 %mlp.11 = (bf16[4,4096,512]{2,1,0:T(8,128)(2,1)}, bf16[1024,512]{1,0:T(8,128)(2,1)}) custom-call(s32[2]{0:T(128)} %pad_add_fusion.pos_ref, bf16[1024,512]{1,0:T(8,128)(2,1)} %get-tuple-element.93.rest_0_.own_ref, bf16[1024,512]{1,0:T(8,128)(2,1)} %copy-done.24, bf16[4,4096,512]{2,1,0:T(8,128)(2,1)} %x_own_ref.11, ...), custom_call_target="tpu_custom_call", output_to_operand_aliasing={{0}: (10, {})} | custom-call | bytes 46080000 | tf_op jit(solution)/shard_map/mlp/pallas_call | solution.py:384
  928.3 17.1 %collective-permute-done.19.got_ref = bf16[1024,512]{1,0:T(8,128)(2,1)S(1)} collective-permute-done((bf16[1024,512]{1,0:T(8,128)(2,1)}, bf16[1024,512]{1,0:T(8,128)(2,1)S(1)}, u32[]{:S(2)}, u32[]{:S(2)}) %collective-permute-start.19) | collective-permute-done | bytes 1048608 | tf_op jit(solution)/shard_map/ppermute | solution.py:425
  (172 shorter events, 137.4 us)
Async XLA Ops:
  0.8 12.3 %copy-start.35 = (bf16[512]{0:T(512)(128)(2,1)S(1)}, bf16[512]{0:T(512)(128)(2,1)}, u32[]{:S(2)}) copy-start(bf16[512]{0:T(512)(128)(2,1)} %param.16) | copy-start | bytes 3076
  0.8 12.3 %copy-start.32 = (f32[16,256]{1,0:T(8,128)S(1)}, f32[16,256]{1,0:T(8,128)}, u32[]{:S(2)}) copy-start(f32[16,256]{1,0:T(8,128)} %param.20) | copy-start | bytes 49156
  0.8 12.9 %copy-start.27 = (bf16[256,256]{1,0:T(8,128)(2,1)S(1)}, bf16[256,256]{1,0:T(8,128)(2,1)}, u32[]{:S(2)}) copy-start(bf16[256,256]{1,0:T(8,128)(2,1)} %param.19) | copy-start | bytes 393220
  0.8 13.8 %copy-start.7 = (bf16[4,128,384]{2,1,0:T(8,128)(2,1)S(1)}, bf16[4,128,384]{2,1,0:T(8,128)(2,1)}, u32[]{:S(2)}) copy-start(bf16[4,128,384]{2,1,0:T(8,128)(2,1)} %proj_ref.9) | copy-start | bytes 1179652
  0.8 13.6 %collective-permute-start.2 = (bf16[4,2,512]{2,1,0:T(2,128)(2,1)S(1)}, bf16[4,2,512]{2,1,0:T(2,128)(2,1)S(1)}, u32[]{:S(2)}, u32[]{:S(2)}) collective-permute-start(bf16[4,2,512]{2,1,0:T(2,128)(2,1)S(1)} %slice.76), channel_id=1, source_target_pairs={{0,3},{1,2},{2,5},{3,4},{4,7},{5,6},{6,9},{7,8},{8,11},{9,10},{10,... | collective-permute-start | bytes 24584 | tf_op jit(solution)/shard_map/ppermute | solution.py:212
  5.2 9.3 collective-permute-start.1
  11.9 3.8 collective-permute-start.3
  13.1 3.2 copy-start.31
  28.3 46.1 %all-to-all-start = ((bf16[16,8,16,512]{3,2,1,0:T(8,128)(2,1)}), bf16[16,8,16,512]{3,2,1,0:T(8,128)(2,1)S(1)}, u32[]{:S(2)}, u32[]{:S(2)}) async-start(bf16[16,8,16,512]{3,2,1,0:T(8,128)(2,1)} %get-tuple-element.53), calls=%async_computation | async-start | bytes 4194304 | tf_op jit(solution)/shard_map/all_to_all | solution.py:275
  40.5 4.5 collective-permute-start
  75.8 59.5 %all-to-all-start.2 = ((bf16[16,8,16,512]{3,2,1,0:T(8,128)(2,1)}), bf16[16,8,16,512]{3,2,1,0:T(8,128)(2,1)S(1)}, u32[]{:S(2)}, u32[]{:S(2)}) async-start(bf16[16,8,16,512]{3,2,1,0:T(8,128)(2,1)} %get-tuple-element.60), calls=%async_computation.2 | async-start | bytes 4194304 | tf_op jit(solution)/shard_map/all_to_all | solution.py:275
  87.0 48.3 %collective-permute-start.4 = (bf16[2048,512]{1,0:T(8,128)(2,1)}, bf16[2048,512]{1,0:T(8,128)(2,1)}, u32[]{:S(2)}, u32[]{:S(2)}) collective-permute-start(bf16[2048,512]{1,0:T(8,128)(2,1)} %get-tuple-element.59), channel_id=1, source_target_pairs={{0,1},{1,0},{2,3},{3,2},{4,5},{5,4},{6,7},{7,6},{8,9},{9,8},{10,11... | collective-permute-start | bytes 6291464 | tf_op jit(solution)/shard_map/ppermute | solution.py:425
  135.3 8.9 copy-start.33
  135.3 9.5 %copy-start.28 = (bf16[256,256]{1,0:T(8,128)(2,1)S(1)}, bf16[256,256]{1,0:T(8,128)(2,1)}, u32[]{:S(2)}) copy-start(bf16[256,256]{1,0:T(8,128)(2,1)} %param.21) | copy-start | bytes 393220
  135.3 10.3 %copy-start.29 = (bf16[256,256]{1,0:T(8,128)(2,1)S(1)}, bf16[256,256]{1,0:T(8,128)(2,1)}, u32[]{:S(2)}) copy-start(bf16[256,256]{1,0:T(8,128)(2,1)} %param.23) | copy-start | bytes 393220
  136.6 83.8 %all-to-all-start.1 = ((bf16[16,16,16,512]{3,2,1,0:T(8,128)(2,1)}), bf16[16,16,16,512]{3,2,1,0:T(8,128)(2,1)}, u32[]{:S(2)}, u32[]{:S(2)}) async-start(bf16[16,16,16,512]{3,2,1,0:T(8,128)(2,1)} %hold.9), calls=%async_computation.1 | async-start | bytes 8388608 | tf_op jit(solution)/shard_map/all_to_all | solution.py:275
  142.7 51.9 %collective-permute-start.5 = (bf16[2048,512]{1,0:T(8,128)(2,1)}, bf16[2048,512]{1,0:T(8,128)(2,1)S(1)}, u32[]{:S(2)}, u32[]{:S(2)}) collective-permute-start(bf16[2048,512]{1,0:T(8,128)(2,1)} %get-tuple-element.64), channel_id=1, source_target_pairs={{0,1},{1,0},{2,3},{3,2},{4,5},{5,4},{6,7},{7,6},{8,9},{9,8},{10,11... | collective-permute-start | bytes 6291464 | tf_op jit(solution)/shard_map/ppermute | solution.py:425
  220.3 97.4 %all-to-all-start.3 = ((bf16[16,16,16,512]{3,2,1,0:T(8,128)(2,1)}), bf16[16,16,16,512]{3,2,1,0:T(8,128)(2,1)}, u32[]{:S(2)}, u32[]{:S(2)}) async-start(bf16[16,16,16,512]{3,2,1,0:T(8,128)(2,1)} %hold.10), calls=%async_computation.3 | async-start | bytes 8388608 | tf_op jit(solution)/shard_map/all_to_all | solution.py:275
  240.0 48.1 %collective-permute-start.8 = (bf16[2048,512]{1,0:T(8,128)(2,1)}, bf16[2048,512]{1,0:T(8,128)(2,1)S(1)}, u32[]{:S(2)}, u32[]{:S(2)}) collective-permute-start(bf16[2048,512]{1,0:T(8,128)(2,1)} %get-tuple-element.69), channel_id=1, source_target_pairs={{0,1},{1,0},{2,3},{3,2},{4,5},{5,4},{6,7},{7,6},{8,9},{9,8},{10,11... | collective-permute-start | bytes 6291464 | tf_op jit(solution)/shard_map/ppermute | solution.py:425
  289.4 50.9 %copy-start.13 = (bf16[4,512,128]{2,1,0:T(8,128)(2,1)S(1)}, bf16[4,512,128]{2,1,0:T(8,128)(2,1)}, u32[]{:S(2)}) copy-start(bf16[4,512,128]{2,1,0:T(8,128)(2,1)} %param.29) | copy-start | bytes 1572868
  289.4 50.9 %copy-start.21 = (bf16[4,128,128]{2,1,0:T(8,128)(2,1)S(1)}, bf16[4,128,128]{2,1,0:T(8,128)(2,1)}, u32[]{:S(2)}) copy-start(bf16[4,128,128]{2,1,0:T(8,128)(2,1)} %param.26) | copy-start | bytes 393220
  289.4 50.9 %copy-start.34 = (bf16[512]{0:T(512)(128)(2,1)S(1)}, bf16[512]{0:T(512)(128)(2,1)}, u32[]{:S(2)}) copy-start(bf16[512]{0:T(512)(128)(2,1)} %param.27) | copy-start | bytes 3076
  317.7 97.4 %all-to-all-start.4 = ((bf16[16,16,16,512]{3,2,1,0:T(8,128)(2,1)}), bf16[16,16,16,512]{3,2,1,0:T(8,128)(2,1)}, u32[]{:S(2)}, u32[]{:S(2)}) async-start(bf16[16,16,16,512]{3,2,1,0:T(8,128)(2,1)} %hold.11), calls=%async_computation.4 | async-start | bytes 8388608 | tf_op jit(solution)/shard_map/all_to_all | solution.py:275
  337.4 4.6 copy-start.30
  337.4 73.5 %collective-permute-start.10 = (bf16[2048,512]{1,0:T(8,128)(2,1)}, bf16[2048,512]{1,0:T(8,128)(2,1)S(1)}, u32[]{:S(2)}, u32[]{:S(2)}) collective-permute-start(bf16[2048,512]{1,0:T(8,128)(2,1)} %get-tuple-element.75), channel_id=1, source_target_pairs={{0,1},{1,0},{2,3},{3,2},{4,5},{5,4},{6,7},{7,6},{8,9},{9,8},{10,11... | collective-permute-start | bytes 6291464 | tf_op jit(solution)/shard_map/ppermute | solution.py:425
  341.4 69.5 %collective-permute-start.7 = (bf16[4612,128]{1,0:T(8,128)(2,1)}, bf16[4612,128]{1,0:T(8,128)(2,1)S(1)}, u32[]{:S(2)}, u32[]{:S(2)}) collective-permute-start(bf16[4612,128]{1,0:T(8,128)(2,1)} %pad_maximum_fusion.1), channel_id=1, source_target_pairs={{0,1},{1,0},{2,3},{3,2},{4,5},{5,4},{6,7},{7,6},{8,9},{9,8},{10,11... | collective-permute-start | bytes 3542024 | tf_op jit(solution)/shard_map/ppermute | solution.py:229
  412.6 23.9 %copy-start.12 = (bf16[4612,128]{1,0:T(8,128)(2,1)S(1)}, bf16[4612,128]{1,0:T(8,128)(2,1)}, u32[]{:S(2)}) copy-start(bf16[4612,128]{1,0:T(8,128)(2,1)} %copy-done.11) | copy-start | bytes 3542020
  415.1 118.0 %all-to-all-start.6 = ((bf16[16,16,16,512]{3,2,1,0:T(8,128)(2,1)}), bf16[16,16,16,512]{3,2,1,0:T(8,128)(2,1)}, u32[]{:S(2)}, u32[]{:S(2)}) async-start(bf16[16,16,16,512]{3,2,1,0:T(8,128)(2,1)} %hold.13), calls=%async_computation.6 | async-start | bytes 8388608 | tf_op jit(solution)/shard_map/all_to_all | solution.py:275
  435.3 2.2 copy-start.14
  438.6 48.7 %collective-permute-start.6 = (bf16[2048,512]{1,0:T(8,128)(2,1)}, bf16[2048,512]{1,0:T(8,128)(2,1)}, u32[]{:S(2)}, u32[]{:S(2)}) collective-permute-start(bf16[2048,512]{1,0:T(8,128)(2,1)} %get-tuple-element.68), channel_id=1, source_target_pairs={{0,1},{1,0},{2,3},{3,2},{4,5},{5,4},{6,7},{7,6},{8,9},{9,8},{10,11... | collective-permute-start | bytes 6291464 | tf_op jit(solution)/shard_map/ppermute | solution.py:425
  453.5 78.3 %collective-permute-start.9 = (bf16[2048,512]{1,0:T(8,128)(2,1)}, bf16[2048,512]{1,0:T(8,128)(2,1)S(1)}, u32[]{:S(2)}, u32[]{:S(2)}) collective-permute-start(bf16[2048,512]{1,0:T(8,128)(2,1)} %get-tuple-element.73), channel_id=1, source_target_pairs={{0,1},{1,0},{2,3},{3,2},{4,5},{5,4},{6,7},{7,6},{8,9},{9,8},{10,11... | collective-permute-start | bytes 6291464 | tf_op jit(solution)/shard_map/ppermute | solution.py:425
  466.5 2.6 copy-start.20
  533.1 83.6 %all-to-all-start.5 = ((bf16[16,16,16,512]{3,2,1,0:T(8,128)(2,1)}), bf16[16,16,16,512]{3,2,1,0:T(8,128)(2,1)}, u32[]{:S(2)}, u32[]{:S(2)}) async-start(bf16[16,16,16,512]{3,2,1,0:T(8,128)(2,1)} %hold.12), calls=%async_computation.5 | async-start | bytes 8388608 | tf_op jit(solution)/shard_map/all_to_all | solution.py:275
  539.1 48.3 %collective-permute-start.11 = (bf16[2048,512]{1,0:T(8,128)(2,1)}, bf16[2048,512]{1,0:T(8,128)(2,1)S(1)}, u32[]{:S(2)}, u32[]{:S(2)}) collective-permute-start(bf16[2048,512]{1,0:T(8,128)(2,1)} %get-tuple-element.72.refs_1_.refs_6_), channel_id=1, source_target_pairs={{0,1},{1,0},{2,3},{3,2},{4,5},{5,4},{6,7},{7,6},{8,9},{9,8},{10,11... | collective-permute-start | bytes 6291464 | tf_op jit(solution)/shard_map/ppermute | solution.py:425
  616.8 67.9 %all-to-all-start.7 = ((bf16[16,8,16,512]{3,2,1,0:T(8,128)(2,1)}), bf16[16,8,16,512]{3,2,1,0:T(8,128)(2,1)S(1)}, u32[]{:S(2)}, u32[]{:S(2)}) async-start(bf16[16,8,16,512]{3,2,1,0:T(8,128)(2,1)} %hold.14), calls=%async_computation.7 | async-start | bytes 4194304 | tf_op jit(solution)/shard_map/all_to_all | solution.py:275
  636.4 48.3 %collective-permute-start.13 = (bf16[2048,512]{1,0:T(8,128)(2,1)}, bf16[2048,512]{1,0:T(8,128)(2,1)}, u32[]{:S(2)}, u32[]{:S(2)}) collective-permute-start(bf16[2048,512]{1,0:T(8,128)(2,1)} %get-tuple-element.78.refs_6_.refs_1_), channel_id=1, source_target_pairs={{0,1},{1,0},{2,3},{3,2},{4,5},{5,4},{6,7},{7,6},{8,9},{9,8},{10,11... | collective-permute-start | bytes 6291464 | tf_op jit(solution)/shard_map/ppermute | solution.py:425
  686.0 46.9 %all-to-all-start.8 = ((bf16[16,8,16,512]{3,2,1,0:T(8,128)(2,1)}), bf16[16,8,16,512]{3,2,1,0:T(8,128)(2,1)S(1)}, u32[]{:S(2)}, u32[]{:S(2)}) async-start(bf16[16,8,16,512]{3,2,1,0:T(8,128)(2,1)} %hold.15), calls=%async_computation.8 | async-start | bytes 4194304 | tf_op jit(solution)/shard_map/all_to_all | solution.py:275
  699.4 25.7 %collective-permute-start.12 = (bf16[1024,512]{1,0:T(8,128)(2,1)}, bf16[1024,512]{1,0:T(8,128)(2,1)S(1)}, u32[]{:S(2)}, u32[]{:S(2)}) collective-permute-start(bf16[1024,512]{1,0:T(8,128)(2,1)} %get-tuple-element.83), channel_id=1, source_target_pairs={{0,1},{1,0},{2,3},{3,2},{4,5},{5,4},{6,7},{7,6},{8,9},{9,8},{10,11... | collective-permute-start | bytes 3145736 | tf_op jit(solution)/shard_map/ppermute | solution.py:425
  734.1 52.3 %all-to-all-start.10 = ((bf16[16,8,16,512]{3,2,1,0:T(8,128)(2,1)}), bf16[16,8,16,512]{3,2,1,0:T(8,128)(2,1)S(1)}, u32[]{:S(2)}, u32[]{:S(2)}) async-start(bf16[16,8,16,512]{3,2,1,0:T(8,128)(2,1)} %hold.17), calls=%async_computation.10 | async-start | bytes 4194304 | tf_op jit(solution)/shard_map/all_to_all | solution.py:275
  753.1 25.7 %collective-permute-start.14 = (bf16[1024,512]{1,0:T(8,128)(2,1)}, bf16[1024,512]{1,0:T(8,128)(2,1)S(1)}, u32[]{:S(2)}, u32[]{:S(2)}) collective-permute-start(bf16[1024,512]{1,0:T(8,128)(2,1)} %get-tuple-element.88), channel_id=1, source_target_pairs={{0,1},{1,0},{2,3},{3,2},{4,5},{5,4},{6,7},{7,6},{8,9},{9,8},{10,11... | collective-permute-start | bytes 3145736 | tf_op jit(solution)/shard_map/ppermute | solution.py:425
  787.9 52.6 %all-to-all-start.9 = ((bf16[16,8,16,512]{3,2,1,0:T(8,128)(2,1)}), bf16[16,8,16,512]{3,2,1,0:T(8,128)(2,1)}, u32[]{:S(2)}, u32[]{:S(2)}) async-start(bf16[16,8,16,512]{3,2,1,0:T(8,128)(2,1)} %hold.16), calls=%async_computation.9 | async-start | bytes 4194304 | tf_op jit(solution)/shard_map/all_to_all | solution.py:275
  799.4 9.3 copy-start.16
  807.2 48.7 %collective-permute-start.16 = (bf16[1024,512]{1,0:T(8,128)(2,1)}, bf16[1024,512]{1,0:T(8,128)(2,1)}, u32[]{:S(2)}, u32[]{:S(2)}) collective-permute-start(bf16[1024,512]{1,0:T(8,128)(2,1)} %get-tuple-element.95), channel_id=1, source_target_pairs={{0,1},{1,0},{2,3},{3,2},{4,5},{5,4},{6,7},{7,6},{8,9},{9,8},{10,11... | collective-permute-start | bytes 3145736 | tf_op jit(solution)/shard_map/ppermute | solution.py:425
  808.6 63.2 %collective-permute-start.18 = (bf16[1024,512]{1,0:T(8,128)(2,1)S(1)}, bf16[1024,512]{1,0:T(8,128)(2,1)S(1)}, u32[]{:S(2)}, u32[]{:S(2)}) collective-permute-start(bf16[1024,512]{1,0:T(8,128)(2,1)S(1)} %copy-done.16), channel_id=1, source_target_pairs={{0,1},{1,0},{2,3},{3,2},{4,5},{5,4},{6,7},{7,6},{8,9},{9,8},{10,11... | collective-permute-start | bytes 3145736 | tf_op jit(solution)/shard_map/ppermute | solution.py:425
  824.6 53.7 %collective-permute-start.17 = (bf16[1024,512]{1,0:T(8,128)(2,1)}, bf16[1024,512]{1,0:T(8,128)(2,1)S(1)}, u32[]{:S(2)}, u32[]{:S(2)}) collective-permute-start(bf16[1024,512]{1,0:T(8,128)(2,1)} %get-tuple-element.92.rest_0_), channel_id=1, source_target_pairs={{0,1},{1,0},{2,3},{3,2},{4,5},{5,4},{6,7},{7,6},{8,9},{9,8},{10,11... | collective-permute-start | bytes 3145736 | tf_op jit(solution)/shard_map/ppermute | solution.py:425
  848.2 52.6 %collective-permute-start.15 = (bf16[1024,512]{1,0:T(8,128)(2,1)}, bf16[1024,512]{1,0:T(8,128)(2,1)S(1)}, u32[]{:S(2)}, u32[]{:S(2)}) collective-permute-start(bf16[1024,512]{1,0:T(8,128)(2,1)} %get-tuple-element.94), channel_id=1, source_target_pairs={{0,1},{1,0},{2,3},{3,2},{4,5},{5,4},{6,7},{7,6},{8,9},{9,8},{10,11... | collective-permute-start | bytes 3145736 | tf_op jit(solution)/shard_map/ppermute | solution.py:425
  871.2 52.0 %collective-permute-start.20 = (bf16[1024,512]{1,0:T(8,128)(2,1)}, bf16[1024,512]{1,0:T(8,128)(2,1)S(1)}, u32[]{:S(2)}, u32[]{:S(2)}) collective-permute-start(bf16[1024,512]{1,0:T(8,128)(2,1)} %get-tuple-element.97.rest_0_), channel_id=1, source_target_pairs={{0,1},{1,0},{2,3},{3,2},{4,5},{5,4},{6,7},{7,6},{8,9},{9,8},{10,11... | collective-permute-start | bytes 3145736 | tf_op jit(solution)/shard_map/ppermute | solution.py:425
  917.1 28.3 %collective-permute-start.19 = (bf16[1024,512]{1,0:T(8,128)(2,1)}, bf16[1024,512]{1,0:T(8,128)(2,1)S(1)}, u32[]{:S(2)}, u32[]{:S(2)}) collective-permute-start(bf16[1024,512]{1,0:T(8,128)(2,1)} %get-tuple-element.99), channel_id=1, source_target_pairs={{0,1},{1,0},{2,3},{3,2},{4,5},{5,4},{6,7},{7,6},{8,9},{9,8},{10,11... | collective-permute-start | bytes 3145736 | tf_op jit(solution)/shard_map/ppermute | solution.py:425
  (20 other events, 24.0 us)

commit v4 on v3

--- a/solution.py
+++ b/solution.py
@@ -376,7 +376,8 @@
     def channels(s, start, size, own, got, x_got, out, after):
         flat = pl.BlockSpec((root, width), lambda i, pos: (i, 0))
         mine = pl.BlockSpec((1, root, width), lambda i, pos: (s, 2 * (start + i) + pos[1], 0))
-        theirs = pl.BlockSpec((root, width), lambda i, pos: (start + i, 0))
+        first = 0 if x_got.shape[0] == size * root else start
+        theirs = pl.BlockSpec((root, width), lambda i, pos: (first + i, 0))
         args = [pos, own, got, stream, x_got, mix_tab, gain_out, up_tab, down_tab]
         specs = [flat, flat, mine, theirs, whole(mix_tab), whole(gain_out), whole(up_tab), whole(down_tab)]
         extra = list(after) + ([] if out is None else [out])
@@ -414,7 +415,7 @@
     def cut(sizes):
         return [(sum(sizes[:i]), n) for i, n in enumerate(sizes)]
 
-    into = [cut([half, half])] + [cut([rows])] * (seqs - 1)
+    into = [cut([rows // 4, rows - rows // 4])] + [cut([rows])] * (seqs - 1)
     outof = [cut([half])] * (seqs - 2) + [cut([half // 2, half // 2])] * 2
 
     firsts, queries, thirds, x_gots, gates, sent = {}, {}, {}, {}, {}, {}
@@ -438,7 +439,8 @@
         queries[s] = rim, held
         firsts[s, c] = part
         if c + 1 == len(into[s]):
-            x_gots[s] = swap_x(held[1])
+            pieces = outof[s] if s == seqs - 1 else [(0, half)]
+            x_gots[s] = [swap_x(held[1][a * root : (a + n) * root]) for a, n in pieces]
 
     def do_go(s, c=0, after=()):
         firsts[s, c] = exchanged(firsts[s, c], after)
@@ -464,7 +466,7 @@
     def do_mlp(s, c=0, n=0, extra=()):
         nonlocal last, out
         start, size = outof[s][c]
-        out, send = channels(s, start, size, *gates[s, c], x_gots[s], out, [*upto(n), last, *extra])
+        out, send = channels(s, start, size, *gates[s, c], x_gots[s][c] if s == seqs - 1 else x_gots[s][0], out, [*upto(n), last, *extra])
         last = send
         sent[s, c] = swap_x(send)
 
@@ -477,37 +479,37 @@
     do_front(0, 1, extra=[sums[1]])
     do_go(0, 1)
     do_front(1, n=1)
-    do_go(1, 0, [x_gots[0]])
+    do_go(1, 0, x_gots[0])
     do_middle(0, n=2)
     do_front(2, n=2)
-    do_send(0, 0, [last, x_gots[1]])
+    do_send(0, 0, [last, *x_gots[1], packed_got])
     do_middle(1, n=3)
     do_front(3, n=3)
-    do_send(1, 0, [last, x_gots[2]])
+    do_send(1, 0, [last, *x_gots[2], x_gots[3][0]])
     do_back(0, n=4)
-    do_go(2, 0, [last, x_gots[3], packed_got])
+    do_go(2, 0, [last, gates[0, 0][1]])
     do_back(1, n=5)
     do_mlp(0, n=5)
     do_go(3, 0, [last, gates[1, 0][1]])
     do_middle(2, n=6)
     do_mlp(1, n=6)
-    do_send(2, 0, [last, sent[0, 0]])
+    do_send(2, 0, [last, sent[0, 0], x_gots[3][1]])
     do_middle(3, n=7)
     do_send(2, 1, [last, sent[1, 0]])
     do_back(2, 0, n=8)
     do_place(0)
-    do_send(3, 0, [last, gates[2, 0][1]])
+    do_mlp(2, 0, n=8)
+    do_send(3, 0, [last])
     do_back(2, 1, n=9)
-    do_mlp(2, 0, n=9)
-    do_send(3, 1, [last, gates[2, 1][1]])
+    do_send(3, 1, [last, gates[2, 1][1], sent[2, 0]])
     do_back(3, 0, n=10)
     do_mlp(2, 1, n=10)
-    do_place(1)
     do_back(3, 1)
     do_mlp(3, 0)
+    do_mlp(3, 1, extra=[sent[2, 1]])
+    do_place(1)
     do_place(2, 0)
     do_place(2, 1)
-    do_mlp(3, 1)
     do_place(3, 0)
     do_place(3, 1)
     return out

time: 961 us -> 936 us (0.974)
  waiting for transfers between devices: 345 us -> 309 us
    ppermute x16 -> x17, waiting for transfers between devices: 160 us -> 224 us  [swap_x(): return lax.ppermute(a, 'mp', swap)]
    all_to_all x11, waiting for transfers between devices: 128 us -> 65.9 us  [exchanged(): line.append(lax.all_to_all(part, 'ctx', 0, 0, tiled=True))]
    ppermute x1, waiting for transfers between devices: 54.7 us -> 16.1 us  [body(): packed_got = lax.ppermute(packed, 'mp', swap)]
    unnamed x81 -> x75, local copies, waits for them, and re-layouts: 33.2 us -> 30.9 us
    ppermute x16 -> x17, starting transfers between devices: 20.7 us -> 20.7 us  [swap_x(): return lax.ppermute(a, 'mp', swap)]
  transfers between devices with their start and end apart: 32 -> 33, of which waited for: 23 -> 21; matrix products, arithmetic and copies ran while one was open for 5% -> 5% of each run, Pallas kernels for 37% -> 39%
where the time goes in v4:
time: 936 us; the launch traced here: 924 us
  Pallas kernels  370 us (40%)
  waiting for transfers between devices  309 us (33%)
  starting transfers between devices  175 us (19%)
  local copies, waits for them, and re-layouts  46.7 us (5%)
  other arithmetic  22.5 us (2%)
    ppermute x17, waiting for transfers between devices, swap_x(): return lax.ppermute(a, 'mp', swap)  224 us
    all_to_all x11, starting transfers between devices, exchanged(): line.append(lax.all_to_all(part, 'ctx', 0, 0, tiled=True))  143 us
    pallas_call x6, Pallas kernels, channels(): pl.pallas_call(mlp, grid_spec=pltpu.PrefetchScalarGridSpec(num_scalar_pre...  114 us
    pallas_call x5, Pallas kernels, front(): pl.pallas_call(functools.partial(mixer_front, len(extra)), grid_spec=pltp...  88.8 us
    pallas_call x4, Pallas kernels, middle(): pl.pallas_call(functools.partial(mixer_middle, into, outof), grid=(cols,)...  80.8 us
    all_to_all x11, waiting for transfers between devices, exchanged(): line.append(lax.all_to_all(part, 'ctx', 0, 0, tiled=True))  65.9 us
    pallas_call x6, Pallas kernels, back(): pl.pallas_call(functools.partial(mixer_back, size), grid_spec=pltpu.Prefe...  57.5 us
    unnamed x75, local copies, waits for them, and re-layouts  30.9 us
  transfers between devices with their start and end apart: 33, of which 21 were waited for; matrix products, arithmetic and copies ran while one was open for 5% of the time, Pallas kernels for 39%

profile of v4, /device:TPU:0, one launch (start us, length us, event | category | flops | bytes accessed | tf_op | source)
XLA Modules:
  0.0 923.9 jit_solution(2697779860650102673)
XLA Ops:
  16.3 7.3 mixer_front.5
  28.6 7.2 multiply_reduce_fusion
  41.0 16.8 %mixer_front.6 = (bf16[1,4096,512]{2,1,0:T(8,128)(2,1)}, bf16[2048,512]{1,0:T(8,128)(2,1)}, f32[4,8,384]{2,1,0:T(8,128)}, bf16[16,12,16,512]{3,2,1,0:T(8,128)(2,1)}) custom-call(s32[2]{0:T(128)} %pad_add_fusion.pos_ref, bf16[4,4096,512]{2,1,0:T(8,128)(2,1)} %x_own_ref.11, f32[16,1,256]{2,1,0:T(1,128)} %bitcast.104, ...), custom_call_target="tpu_custom_call", output_to_operand_aliasing={{0}: (11, {}), {1}: (12, {})} | custom-call | bytes 54000000 | tf_op jit(solution)/shard_map/mixer_front/pallas_call | solution.py:283
  58.8 5.8 all-to-all-start.2
  66.2 21.5 %mixer_front.7 = (bf16[1,4096,512]{2,1,0:T(8,128)(2,1)}, bf16[2048,512]{1,0:T(8,128)(2,1)}, f32[4,8,384]{2,1,0:T(8,128)}, bf16[16,16,16,512]{3,2,1,0:T(8,128)(2,1)}) custom-call(s32[2]{0:T(128)} %pad_add_fusion.pos_ref, bf16[4,4096,512]{2,1,0:T(8,128)(2,1)} %x_own_ref.11, f32[16,1,256]{2,1,0:T(1,128)} %bitcast.102, f32[4,8,384]{2,1,0:T(8,128)} %get-tuple-element.113.rim_ref, ...), custom_call_target="tpu_custom_call" | custom-call | bytes 72000000 | tf_op jit(solution)/shard_map/mixer_front/pallas_call | solution.py:283
  87.7 25.2 %collective-permute-done.4.refs_1_.x_got_ref = bf16[2048,512]{1,0:T(8,128)(2,1)} collective-permute-done((bf16[2048,512]{1,0:T(8,128)(2,1)}, bf16[2048,512]{1,0:T(8,128)(2,1)}, u32[]{:S(2)}, u32[]{:S(2)}) %collective-permute-start.4) | collective-permute-done | bytes 2097184 | tf_op jit(solution)/shard_map/ppermute | solution.py:426
  112.9 11.1 %all-to-all-done.2.refs_1_.refs_6_.rest_0_ = bf16[16,12,16,512]{3,2,1,0:T(8,128)(2,1)S(1)} async-done(((bf16[16,12,16,512]{3,2,1,0:T(8,128)(2,1)}), bf16[16,12,16,512]{3,2,1,0:T(8,128)(2,1)S(1)}, u32[]{:S(2)}, u32[]{:S(2)}) %all-to-all-start.2) | async-done | bytes 3145760 | tf_op jit(solution)/shard_map/all_to_all | solution.py:275
  125.7 15.8 %all-to-all-start.1 = ((bf16[16,16,16,512]{3,2,1,0:T(8,128)(2,1)}), bf16[16,16,16,512]{3,2,1,0:T(8,128)(2,1)}, u32[]{:S(2)}, u32[]{:S(2)}) async-start(bf16[16,16,16,512]{3,2,1,0:T(8,128)(2,1)} %hold.9), calls=%async_computation.1 | async-start | bytes 8388608 | tf_op jit(solution)/shard_map/all_to_all | solution.py:275
  150.9 6.5 copy.73
  157.3 20.1 %mixer_middle.4.rest_1_.refs_0_ = bf16[16,16,16,512]{3,2,1,0:T(8,128)(2,1)} custom-call(bf16[16,4,16,512]{3,2,1,0:T(8,128)(2,1)} %copy-done.5, bf16[16,12,16,512]{3,2,1,0:T(8,128)(2,1)} %copy-done, bf16[256,256]{1,0:T(8,128)(2,1)} %bitcast.86, bf16[16,256,512]{2,1,0:T(8,128)(2,1)} %bitcast.58, bf16[256,256]{1,0:T(8,128)(2,1)} %bitcast.90, ...), custom_call_target="tpu_custom_call" | custom-call | bytes 72000000 | tf_op jit(solution)/shard_map/mixer_middle/pallas_call | solution.py:325
  177.4 21.6 %mixer_front.8 = (bf16[1,4096,512]{2,1,0:T(8,128)(2,1)}, bf16[2048,512]{1,0:T(8,128)(2,1)}, f32[4,8,384]{2,1,0:T(8,128)}, bf16[16,16,16,512]{3,2,1,0:T(8,128)(2,1)}) custom-call(s32[2]{0:T(128)} %pad_add_fusion.pos_ref, bf16[4,4096,512]{2,1,0:T(8,128)(2,1)} %x_own_ref.11, f32[16,1,256]{2,1,0:T(1,128)} %bitcast.113, f32[4,8,384]{2,1,0:T(8,128)} %get-tuple-element.111.rim_ref, ...), custom_call_target="tpu_custom_call" | custom-call | bytes 72000000 | tf_op jit(solution)/shard_map/mixer_front/pallas_call | solution.py:283
  199.0 16.1 %collective-permute-done.6.refs_3_ = bf16[4612,128]{1,0:T(8,128)(2,1)S(1)} collective-permute-done((bf16[4612,128]{1,0:T(8,128)(2,1)}, bf16[4612,128]{1,0:T(8,128)(2,1)S(1)}, u32[]{:S(2)}, u32[]{:S(2)}) %collective-permute-start.6) | collective-permute-done | bytes 1180704 | tf_op jit(solution)/shard_map/ppermute | solution.py:229
  219.1 19.7 %all-to-all-start.3 = ((bf16[16,16,16,512]{3,2,1,0:T(8,128)(2,1)}), bf16[16,16,16,512]{3,2,1,0:T(8,128)(2,1)}, u32[]{:S(2)}, u32[]{:S(2)}) async-start(bf16[16,16,16,512]{3,2,1,0:T(8,128)(2,1)} %hold.10), calls=%async_computation.3 | async-start | bytes 8388608 | tf_op jit(solution)/shard_map/all_to_all | solution.py:275
  240.3 20.2 %mixer_middle.5.rest_1_.refs_0_ = bf16[16,16,16,512]{3,2,1,0:T(8,128)(2,1)} custom-call(bf16[16,16,16,512]{3,2,1,0:T(8,128)(2,1)} %all-to-all-done.1.refs_0_.refs_5_.rest_0_, bf16[256,256]{1,0:T(8,128)(2,1)} %bitcast.87, bf16[16,256,512]{2,1,0:T(8,128)(2,1)} %bitcast.59, bf16[256,256]{1,0:T(8,128)(2,1)} %bitcast.91, f32[16,1,256]{2,1,0:T(1,128)} %reshape.95.refs_5_.refs_4_, ...), custom_call_target="tpu_custom_call" | custom-call | bytes 72000000 | tf_op jit(solution)/shard_map/mixer_middle/pallas_call | solution.py:325
  260.5 21.5 %mixer_front.9 = (bf16[1,4096,512]{2,1,0:T(8,128)(2,1)}, bf16[2048,512]{1,0:T(8,128)(2,1)}, f32[4,8,384]{2,1,0:T(8,128)}, bf16[16,16,16,512]{3,2,1,0:T(8,128)(2,1)}) custom-call(s32[2]{0:T(128)} %pad_add_fusion.pos_ref, bf16[4,4096,512]{2,1,0:T(8,128)(2,1)} %x_own_ref.11, f32[16,1,256]{2,1,0:T(1,128)} %bitcast.112, f32[4,8,384]{2,1,0:T(8,128)} %get-tuple-element.114.rim_ref, ...), custom_call_target="tpu_custom_call" | custom-call | bytes 72000000 | tf_op jit(solution)/shard_map/mixer_front/pallas_call | solution.py:283
  286.9 22.9 %collective-permute-done.9.refs_3_.x_got_ref = bf16[1024,512]{1,0:T(8,128)(2,1)S(1)} collective-permute-done((bf16[1024,512]{1,0:T(8,128)(2,1)S(1)}, bf16[1024,512]{1,0:T(8,128)(2,1)S(1)}, u32[]{:S(2)}, u32[]{:S(2)}) %collective-permute-start.9) | collective-permute-done | bytes 1048608 | tf_op jit(solution)/shard_map/ppermute | solution.py:426
  316.5 19.7 %all-to-all-start.4 = ((bf16[16,16,16,512]{3,2,1,0:T(8,128)(2,1)}), bf16[16,16,16,512]{3,2,1,0:T(8,128)(2,1)}, u32[]{:S(2)}, u32[]{:S(2)}) async-start(bf16[16,16,16,512]{3,2,1,0:T(8,128)(2,1)} %hold.11), calls=%async_computation.4 | async-start | bytes 8388608 | tf_op jit(solution)/shard_map/all_to_all | solution.py:275
  336.9 13.4 %mixer_back.6 = (bf16[2048,512]{1,0:T(8,128)(2,1)}, bf16[2048,512]{1,0:T(8,128)(2,1)}) custom-call(s32[2]{0:T(128)} %pad_add_fusion.pos_ref, bf16[16,16,16,512]{3,2,1,0:T(8,128)(2,1)} %all-to-all-done.3.in_ref.rest_0_, bf16[256,256]{1,0:T(8,128)(2,1)} %bitcast.69, bf16[1,4096,512]{2,1,0:T(8,128)(2,1)} %get-tuple-element.65.query_ref, ...), custom_call_target="tpu_custom_call" | custom-call | bytes 51840000 | tf_op jit(solution)/shard_map/mixer_back/pallas_call | solution.py:352
  351.8 46.6 %collective-permute-done.7.got_ref.refs_2_ = bf16[2048,512]{1,0:T(8,128)(2,1)S(1)} collective-permute-done((bf16[2048,512]{1,0:T(8,128)(2,1)}, bf16[2048,512]{1,0:T(8,128)(2,1)S(1)}, u32[]{:S(2)}, u32[]{:S(2)}) %collective-permute-start.7) | collective-permute-done | bytes 2097184 | tf_op jit(solution)/shard_map/ppermute | solution.py:426
  399.7 14.1 %all-to-all-done.4.in_ref.rest_0_ = bf16[16,16,16,512]{3,2,1,0:T(8,128)(2,1)} async-done(((bf16[16,16,16,512]{3,2,1,0:T(8,128)(2,1)}), bf16[16,16,16,512]{3,2,1,0:T(8,128)(2,1)}, u32[]{:S(2)}, u32[]{:S(2)}) %all-to-all-start.4) | async-done | bytes 4194336 | tf_op jit(solution)/shard_map/all_to_all | solution.py:275
  413.8 20.2 %all-to-all-start.6 = ((bf16[16,16,16,512]{3,2,1,0:T(8,128)(2,1)}), bf16[16,16,16,512]{3,2,1,0:T(8,128)(2,1)}, u32[]{:S(2)}, u32[]{:S(2)}) async-start(bf16[16,16,16,512]{3,2,1,0:T(8,128)(2,1)} %hold.13), calls=%async_computation.6 | async-start | bytes 8388608 | tf_op jit(solution)/shard_map/all_to_all | solution.py:275
  437.3 13.4 %mixer_back.7 = (bf16[2048,512]{1,0:T(8,128)(2,1)}, bf16[2048,512]{1,0:T(8,128)(2,1)}) custom-call(s32[2]{0:T(128)} %pad_add_fusion.pos_ref, bf16[16,16,16,512]{3,2,1,0:T(8,128)(2,1)} %all-to-all-done.4.in_ref.rest_0_, bf16[256,256]{1,0:T(8,128)(2,1)} %bitcast.70, bf16[1,4096,512]{2,1,0:T(8,128)(2,1)} %get-tuple-element.71.query_ref, ...), custom_call_target="tpu_custom_call" | custom-call | bytes 51840000 | tf_op jit(solution)/shard_map/mixer_back/pallas_call | solution.py:352
  468.7 26.3 %mlp.6 = (bf16[4,4096,512]{2,1,0:T(8,128)(2,1)}, bf16[2048,512]{1,0:T(8,128)(2,1)}) custom-call(s32[2]{0:T(128)} %pad_add_fusion.pos_ref, bf16[2048,512]{1,0:T(8,128)(2,1)} %get-tuple-element.67.rest_1_.own_ref.refs_1_, bf16[2048,512]{1,0:T(8,128)(2,1)} %copy-done.7, bf16[4,4096,512]{2,1,0:T(8,128)(2,1)} %x_own_ref.11, ...), custom_call_target="tpu_custom_call" | custom-call | bytes 92160000 | tf_op jit(solution)/shard_map/mlp/pallas_call | solution.py:385
  500.3 11.4 %all-to-all-done.6.refs_0_.refs_5_.rest_0_ = bf16[16,16,16,512]{3,2,1,0:T(8,128)(2,1)} async-done(((bf16[16,16,16,512]{3,2,1,0:T(8,128)(2,1)}), bf16[16,16,16,512]{3,2,1,0:T(8,128)(2,1)}, u32[]{:S(2)}, u32[]{:S(2)}) %all-to-all-start.6) | async-done | bytes 4194336 | tf_op jit(solution)/shard_map/all_to_all | solution.py:275
  511.7 19.9 %all-to-all-start.5 = ((bf16[16,16,16,512]{3,2,1,0:T(8,128)(2,1)}), bf16[16,16,16,512]{3,2,1,0:T(8,128)(2,1)}, u32[]{:S(2)}, u32[]{:S(2)}) async-start(bf16[16,16,16,512]{3,2,1,0:T(8,128)(2,1)} %hold.12), calls=%async_computation.5 | async-start | bytes 8388608 | tf_op jit(solution)/shard_map/all_to_all | solution.py:275
  533.7 20.3 %mixer_middle.6 = (bf16[16,8,16,512]{3,2,1,0:T(8,128)(2,1)}, bf16[16,8,16,512]{3,2,1,0:T(8,128)(2,1)}) custom-call(bf16[16,16,16,512]{3,2,1,0:T(8,128)(2,1)} %all-to-all-done.6.refs_0_.refs_5_.rest_0_, bf16[256,256]{1,0:T(8,128)(2,1)} %bitcast.88, bf16[16,256,512]{2,1,0:T(8,128)(2,1)} %bitcast.60, bf16[256,256]{1,0:T(8,128)(2,1)} %bitcast.92, ...), custom_call_target="tpu_custom_call" | custom-call | bytes 72000000 | tf_op jit(solution)/shard_map/mixer_middle/pallas_call | solution.py:325
  554.0 26.3 %mlp.7 = (bf16[4,4096,512]{2,1,0:T(8,128)(2,1)}, bf16[2048,512]{1,0:T(8,128)(2,1)}) custom-call(s32[2]{0:T(128)} %pad_add_fusion.pos_ref, bf16[2048,512]{1,0:T(8,128)(2,1)} %get-tuple-element.72.rest_1_.own_ref, bf16[2048,512]{1,0:T(8,128)(2,1)} %copy-done.8, bf16[4,4096,512]{2,1,0:T(8,128)(2,1)} %x_own_ref.11, ...), custom_call_target="tpu_custom_call", output_to_operand_aliasing={{0}: (11, {})} | custom-call | bytes 92160000 | tf_op jit(solution)/shard_map/mlp/pallas_call | solution.py:385
  580.3 22.1 %collective-permute-done.13.refs_3_.x_got_ref = bf16[1024,512]{1,0:T(8,128)(2,1)S(1)} collective-permute-done((bf16[1024,512]{1,0:T(8,128)(2,1)}, bf16[1024,512]{1,0:T(8,128)(2,1)S(1)}, u32[]{:S(2)}, u32[]{:S(2)}) %collective-permute-start.13) | collective-permute-done | bytes 1048608 | tf_op jit(solution)/shard_map/ppermute | solution.py:426
  609.3 19.6 %all-to-all-start.8 = ((bf16[16,8,16,512]{3,2,1,0:T(8,128)(2,1)}), bf16[16,8,16,512]{3,2,1,0:T(8,128)(2,1)S(1)}, u32[]{:S(2)}, u32[]{:S(2)}) async-start(bf16[16,8,16,512]{3,2,1,0:T(8,128)(2,1)} %hold.15), calls=%async_computation.8 | async-start | bytes 4194304 | tf_op jit(solution)/shard_map/all_to_all | solution.py:275
  630.4 20.2 %mixer_middle.7 = (bf16[16,8,16,512]{3,2,1,0:T(8,128)(2,1)}, bf16[16,8,16,512]{3,2,1,0:T(8,128)(2,1)}) custom-call(bf16[16,16,16,512]{3,2,1,0:T(8,128)(2,1)} %all-to-all-done.5.refs_0_.refs_5_, bf16[256,256]{1,0:T(8,128)(2,1)} %bitcast.89, bf16[16,256,512]{2,1,0:T(8,128)(2,1)} %bitcast.61, bf16[256,256]{1,0:T(8,128)(2,1)} %bitcast.93, ...), custom_call_target="tpu_custom_call" | custom-call | bytes 72000000 | tf_op jit(solution)/shard_map/mixer_middle/pallas_call | solution.py:325
  650.6 26.5 %collective-permute-done.11.refs_2_.got_ref = bf16[2048,512]{1,0:T(8,128)(2,1)} collective-permute-done((bf16[2048,512]{1,0:T(8,128)(2,1)}, bf16[2048,512]{1,0:T(8,128)(2,1)}, u32[]{:S(2)}, u32[]{:S(2)}) %collective-permute-start.11) | collective-permute-done | bytes 2097184 | tf_op jit(solution)/shard_map/ppermute | solution.py:426
  684.3 7.7 mixer_back.8
  693.4 6.3 place.6.rest_2_
  699.7 17.9 %collective-permute-done.14.got_ref = bf16[1024,512]{1,0:T(8,128)(2,1)S(1)} collective-permute-done((bf16[1024,512]{1,0:T(8,128)(2,1)}, bf16[1024,512]{1,0:T(8,128)(2,1)S(1)}, u32[]{:S(2)}, u32[]{:S(2)}) %collective-permute-start.14) | collective-permute-done | bytes 1048608 | tf_op jit(solution)/shard_map/ppermute | solution.py:426
  718.6 15.3 %mlp.8 = (bf16[4,4096,512]{2,1,0:T(8,128)(2,1)}, bf16[1024,512]{1,0:T(8,128)(2,1)}) custom-call(s32[2]{0:T(128)} %pad_add_fusion.pos_ref, bf16[1024,512]{1,0:T(8,128)(2,1)} %get-tuple-element.83.own_ref.rest_1_, bf16[1024,512]{1,0:T(8,128)(2,1)} %copy-done.25, bf16[4,4096,512]{2,1,0:T(8,128)(2,1)} %x_own_ref.11, ...), custom_call_target="tpu_custom_call", output_to_operand_aliasing={{0}: (11, {})} | custom-call | bytes 46080000 | tf_op jit(solution)/shard_map/mlp/pallas_call | solution.py:385
  741.2 7.7 mixer_back.9
  749.4 16.5 %collective-permute-done.16.refs_3_.got_ref = bf16[1024,512]{1,0:T(8,128)(2,1)S(1)} collective-permute-done((bf16[1024,512]{1,0:T(8,128)(2,1)}, bf16[1024,512]{1,0:T(8,128)(2,1)S(1)}, u32[]{:S(2)}, u32[]{:S(2)}) %collective-permute-start.16) | collective-permute-done | bytes 1048608 | tf_op jit(solution)/shard_map/ppermute | solution.py:426
  765.9 22.0 %collective-permute-done.15.refs_2_.got_ref = bf16[1024,512]{1,0:T(8,128)(2,1)} collective-permute-done((bf16[1024,512]{1,0:T(8,128)(2,1)}, bf16[1024,512]{1,0:T(8,128)(2,1)}, u32[]{:S(2)}, u32[]{:S(2)}) %collective-permute-start.15) | collective-permute-done | bytes 1048608 | tf_op jit(solution)/shard_map/ppermute | solution.py:426
  789.4 6.0 all-to-all-start.9
  795.4 7.7 mixer_back.10
  804.5 15.3 %mlp.9 = (bf16[4,4096,512]{2,1,0:T(8,128)(2,1)}, bf16[1024,512]{1,0:T(8,128)(2,1)}) custom-call(s32[2]{0:T(128)} %pad_add_fusion.pos_ref, bf16[1024,512]{1,0:T(8,128)(2,1)} %get-tuple-element.87.refs_1_.rest_1_.own_ref, bf16[1024,512]{1,0:T(8,128)(2,1)} %collective-permute-done.15.refs_2_.got_ref, ...), custom_call_target="tpu_custom_call", output_to_operand_aliasing={{0}: (11, {})} | custom-call | bytes 46080000 | tf_op jit(solution)/shard_map/mlp/pallas_call | solution.py:385
  820.4 16.1 %all-to-all-done.9.in_ref = bf16[16,8,16,512]{3,2,1,0:T(8,128)(2,1)} async-done(((bf16[16,8,16,512]{3,2,1,0:T(8,128)(2,1)}), bf16[16,8,16,512]{3,2,1,0:T(8,128)(2,1)}, u32[]{:S(2)}, u32[]{:S(2)}) %all-to-all-start.9) | async-done | bytes 2097184 | tf_op jit(solution)/shard_map/all_to_all | solution.py:275
  836.5 7.7 mixer_back.11
  846.6 15.4 %mlp.10 = (bf16[4,4096,512]{2,1,0:T(8,128)(2,1)}, bf16[1024,512]{1,0:T(8,128)(2,1)}) custom-call(s32[2]{0:T(128)} %pad_add_fusion.pos_ref, bf16[1024,512]{1,0:T(8,128)(2,1)} %get-tuple-element.90.rest_1_.own_ref, bf16[1024,512]{1,0:T(8,128)(2,1)} %copy-done.21, bf16[4,4096,512]{2,1,0:T(8,128)(2,1)} %x_own_ref.11, ...), custom_call_target="tpu_custom_call", output_to_operand_aliasing={{0}: (10, {})} | custom-call | bytes 46080000 | tf_op jit(solution)/shard_map/mlp/pallas_call | solution.py:385
  862.5 11.6 %collective-permute-done.17.got_ref = bf16[1024,512]{1,0:T(8,128)(2,1)S(1)} collective-permute-done((bf16[1024,512]{1,0:T(8,128)(2,1)}, bf16[1024,512]{1,0:T(8,128)(2,1)S(1)}, u32[]{:S(2)}, u32[]{:S(2)}) %collective-permute-start.17) | collective-permute-done | bytes 1048608 | tf_op jit(solution)/shard_map/ppermute | solution.py:426
  875.2 15.3 %mlp.11 = (bf16[4,4096,512]{2,1,0:T(8,128)(2,1)}, bf16[1024,512]{1,0:T(8,128)(2,1)}) custom-call(s32[2]{0:T(128)} %pad_add_fusion.pos_ref, bf16[1024,512]{1,0:T(8,128)(2,1)} %get-tuple-element.93.rest_0_.own_ref, bf16[1024,512]{1,0:T(8,128)(2,1)} %copy-done.23, bf16[4,4096,512]{2,1,0:T(8,128)(2,1)} %x_own_ref.11, ...), custom_call_target="tpu_custom_call", output_to_operand_aliasing={{0}: (11, {})} | custom-call | bytes 46080000 | tf_op jit(solution)/shard_map/mlp/pallas_call | solution.py:385
  891.9 6.3 place.7.rest_0_
  911.3 7.4 collective-permute-done.20.got_ref
  (169 shorter events, 141.8 us)
Async XLA Ops:
  0.8 12.3 %copy-start.32 = (bf16[512]{0:T(512)(128)(2,1)S(1)}, bf16[512]{0:T(512)(128)(2,1)}, u32[]{:S(2)}) copy-start(bf16[512]{0:T(512)(128)(2,1)} %param.16) | copy-start | bytes 3076
  0.8 12.3 %copy-start.30 = (f32[16,256]{1,0:T(8,128)S(1)}, f32[16,256]{1,0:T(8,128)}, u32[]{:S(2)}) copy-start(f32[16,256]{1,0:T(8,128)} %param.20) | copy-start | bytes 49156
  0.8 12.9 %copy-start.26 = (bf16[256,256]{1,0:T(8,128)(2,1)S(1)}, bf16[256,256]{1,0:T(8,128)(2,1)}, u32[]{:S(2)}) copy-start(bf16[256,256]{1,0:T(8,128)(2,1)} %param.19) | copy-start | bytes 393220
  0.8 13.9 %copy-start.4 = (bf16[4,128,384]{2,1,0:T(8,128)(2,1)S(1)}, bf16[4,128,384]{2,1,0:T(8,128)(2,1)}, u32[]{:S(2)}) copy-start(bf16[4,128,384]{2,1,0:T(8,128)(2,1)} %proj_ref.9) | copy-start | bytes 1179652
  0.8 13.7 %collective-permute-start.2 = (bf16[4,2,512]{2,1,0:T(2,128)(2,1)S(1)}, bf16[4,2,512]{2,1,0:T(2,128)(2,1)S(1)}, u32[]{:S(2)}, u32[]{:S(2)}) collective-permute-start(bf16[4,2,512]{2,1,0:T(2,128)(2,1)S(1)} %slice.82), channel_id=1, source_target_pairs={{0,3},{1,2},{2,5},{3,4},{4,7},{5,6},{6,9},{7,8},{8,11},{9,10},{10,... | collective-permute-start | bytes 24584 | tf_op jit(solution)/shard_map/ppermute | solution.py:212
  5.2 9.3 %collective-permute-start.1 = (bf16[4,2,512]{2,1,0:T(2,128)(2,1)S(1)}, bf16[4,2,512]{2,1,0:T(2,128)(2,1)S(1)}, u32[]{:S(2)}, u32[]{:S(2)}) collective-permute-start(bf16[4,2,512]{2,1,0:T(2,128)(2,1)S(1)} %slice.82), channel_id=1, source_target_pairs={{0,2},{2,4},{4,6},{6,8},{8,10},{10,12},{12,14},{14,16},{16,18},{18... | collective-permute-start | bytes 24584 | tf_op jit(solution)/shard_map/ppermute | solution.py:211
  11.9 3.8 collective-permute-start.3
  13.1 3.2 copy-start.29
  23.6 34.2 %all-to-all-start = ((bf16[16,4,16,512]{3,2,1,0:T(8,128)(2,1)}), bf16[16,4,16,512]{3,2,1,0:T(8,128)(2,1)S(1)}, u32[]{:S(2)}, u32[]{:S(2)}) async-start(bf16[16,4,16,512]{3,2,1,0:T(8,128)(2,1)} %get-tuple-element.53), calls=%async_computation | async-start | bytes 2097152 | tf_op jit(solution)/shard_map/all_to_all | solution.py:275
  35.8 4.5 collective-permute-start
  58.8 65.2 %all-to-all-start.2 = ((bf16[16,12,16,512]{3,2,1,0:T(8,128)(2,1)}), bf16[16,12,16,512]{3,2,1,0:T(8,128)(2,1)S(1)}, u32[]{:S(2)}, u32[]{:S(2)}) async-start(bf16[16,12,16,512]{3,2,1,0:T(8,128)(2,1)} %get-tuple-element.60), calls=%async_computation.2 | async-start | bytes 6291456 | tf_op jit(solution)/shard_map/all_to_all | solution.py:275
  64.7 48.3 %collective-permute-start.4 = (bf16[2048,512]{1,0:T(8,128)(2,1)}, bf16[2048,512]{1,0:T(8,128)(2,1)}, u32[]{:S(2)}, u32[]{:S(2)}) collective-permute-start(bf16[2048,512]{1,0:T(8,128)(2,1)} %get-tuple-element.59), channel_id=1, source_target_pairs={{0,1},{1,0},{2,3},{3,2},{4,5},{5,4},{6,7},{7,6},{8,9},{9,8},{10,11... | collective-permute-start | bytes 6291464 | tf_op jit(solution)/shard_map/ppermute | solution.py:426
  112.9 31.4 %copy-start.20 = (bf16[4,128,128]{2,1,0:T(8,128)(2,1)S(1)}, bf16[4,128,128]{2,1,0:T(8,128)(2,1)}, u32[]{:S(2)}) copy-start(bf16[4,128,128]{2,1,0:T(8,128)(2,1)} %param.26) | copy-start | bytes 393220
  112.9 31.4 %copy-start.31 = (bf16[512]{0:T(512)(128)(2,1)S(1)}, bf16[512]{0:T(512)(128)(2,1)}, u32[]{:S(2)}) copy-start(bf16[512]{0:T(512)(128)(2,1)} %param.27) | copy-start | bytes 3076
  125.7 93.4 %all-to-all-start.1 = ((bf16[16,16,16,512]{3,2,1,0:T(8,128)(2,1)}), bf16[16,16,16,512]{3,2,1,0:T(8,128)(2,1)}, u32[]{:S(2)}, u32[]{:S(2)}) async-start(bf16[16,16,16,512]{3,2,1,0:T(8,128)(2,1)} %hold.9), calls=%async_computation.1 | async-start | bytes 8388608 | tf_op jit(solution)/shard_map/all_to_all | solution.py:275
  141.4 7.0 copy-start.27
  141.5 73.6 %collective-permute-start.5 = (bf16[2048,512]{1,0:T(8,128)(2,1)}, bf16[2048,512]{1,0:T(8,128)(2,1)S(1)}, u32[]{:S(2)}, u32[]{:S(2)}) collective-permute-start(bf16[2048,512]{1,0:T(8,128)(2,1)} %get-tuple-element.64), channel_id=1, source_target_pairs={{0,1},{1,0},{2,3},{3,2},{4,5},{5,4},{6,7},{7,6},{8,9},{9,8},{10,11... | collective-permute-start | bytes 6291464 | tf_op jit(solution)/shard_map/ppermute | solution.py:426
  146.6 68.5 %collective-permute-start.6 = (bf16[4612,128]{1,0:T(8,128)(2,1)}, bf16[4612,128]{1,0:T(8,128)(2,1)S(1)}, u32[]{:S(2)}, u32[]{:S(2)}) collective-permute-start(bf16[4612,128]{1,0:T(8,128)(2,1)} %pad_maximum_fusion.1), channel_id=1, source_target_pairs={{0,1},{1,0},{2,3},{3,2},{4,5},{5,4},{6,7},{7,6},{8,9},{9,8},{10,11... | collective-permute-start | bytes 3542024 | tf_op jit(solution)/shard_map/ppermute | solution.py:229
  219.1 97.4 %all-to-all-start.3 = ((bf16[16,16,16,512]{3,2,1,0:T(8,128)(2,1)}), bf16[16,16,16,512]{3,2,1,0:T(8,128)(2,1)}, u32[]{:S(2)}, u32[]{:S(2)}) async-start(bf16[16,16,16,512]{3,2,1,0:T(8,128)(2,1)} %hold.10), calls=%async_computation.3 | async-start | bytes 8388608 | tf_op jit(solution)/shard_map/all_to_all | solution.py:275
  238.8 48.1 %collective-permute-start.8 = (bf16[2048,512]{1,0:T(8,128)(2,1)}, bf16[2048,512]{1,0:T(8,128)(2,1)S(1)}, u32[]{:S(2)}, u32[]{:S(2)}) collective-permute-start(bf16[2048,512]{1,0:T(8,128)(2,1)} %get-tuple-element.69), channel_id=1, source_target_pairs={{0,1},{1,0},{2,3},{3,2},{4,5},{5,4},{6,7},{7,6},{8,9},{9,8},{10,11... | collective-permute-start | bytes 6291464 | tf_op jit(solution)/shard_map/ppermute | solution.py:426
  284.7 25.1 %collective-permute-start.9 = (bf16[1024,512]{1,0:T(8,128)(2,1)S(1)}, bf16[1024,512]{1,0:T(8,128)(2,1)S(1)}, u32[]{:S(2)}, u32[]{:S(2)}) collective-permute-start(bf16[1024,512]{1,0:T(8,128)(2,1)S(1)} %get-tuple-element.102), channel_id=1, source_target_pairs={{0,1},{1,0},{2,3},{3,2},{4,5},{5,4},{6,7},{7,6},{8,9},{9,8},{10,11... | collective-permute-start | bytes 3145736 | tf_op jit(solution)/shard_map/ppermute | solution.py:426
  286.9 22.9 %copy-start.3 = (bf16[2048,512]{1,0:T(8,128)(2,1)}, bf16[2048,512]{1,0:T(8,128)(2,1)S(1)}, u32[]{:S(2)}) copy-start(bf16[2048,512]{1,0:T(8,128)(2,1)S(1)} %collective-permute-done.8.refs_2_.x_got_ref) | copy-start | bytes 6291460
  310.8 25.4 %copy-start.28 = (bf16[256,256]{1,0:T(8,128)(2,1)S(1)}, bf16[256,256]{1,0:T(8,128)(2,1)}, u32[]{:S(2)}) copy-start(bf16[256,256]{1,0:T(8,128)(2,1)} %param.25) | copy-start | bytes 393220
  316.5 97.4 %all-to-all-start.4 = ((bf16[16,16,16,512]{3,2,1,0:T(8,128)(2,1)}), bf16[16,16,16,512]{3,2,1,0:T(8,128)(2,1)}, u32[]{:S(2)}, u32[]{:S(2)}) async-start(bf16[16,16,16,512]{3,2,1,0:T(8,128)(2,1)} %hold.11), calls=%async_computation.4 | async-start | bytes 8388608 | tf_op jit(solution)/shard_map/all_to_all | solution.py:275
  350.3 48.1 %collective-permute-start.7 = (bf16[2048,512]{1,0:T(8,128)(2,1)}, bf16[2048,512]{1,0:T(8,128)(2,1)S(1)}, u32[]{:S(2)}, u32[]{:S(2)}) collective-permute-start(bf16[2048,512]{1,0:T(8,128)(2,1)} %get-tuple-element.68), channel_id=1, source_target_pairs={{0,1},{1,0},{2,3},{3,2},{4,5},{5,4},{6,7},{7,6},{8,9},{9,8},{10,11... | collective-permute-start | bytes 6291464 | tf_op jit(solution)/shard_map/ppermute | solution.py:426
  399.7 35.6 %copy-start.11 = (bf16[4612,128]{1,0:T(8,128)(2,1)S(1)}, bf16[4612,128]{1,0:T(8,128)(2,1)}, u32[]{:S(2)}) copy-start(bf16[4612,128]{1,0:T(8,128)(2,1)} %copy-done.10) | copy-start | bytes 3542020
  413.8 97.9 %all-to-all-start.6 = ((bf16[16,16,16,512]{3,2,1,0:T(8,128)(2,1)}), bf16[16,16,16,512]{3,2,1,0:T(8,128)(2,1)}, u32[]{:S(2)}, u32[]{:S(2)}) async-start(bf16[16,16,16,512]{3,2,1,0:T(8,128)(2,1)} %hold.13), calls=%async_computation.6 | async-start | bytes 8388608 | tf_op jit(solution)/shard_map/all_to_all | solution.py:275
  434.1 2.1 copy-start.12
  450.8 48.2 %collective-permute-start.10 = (bf16[2048,512]{1,0:T(8,128)(2,1)}, bf16[2048,512]{1,0:T(8,128)(2,1)S(1)}, u32[]{:S(2)}, u32[]{:S(2)}) collective-permute-start(bf16[2048,512]{1,0:T(8,128)(2,1)} %get-tuple-element.74), channel_id=1, source_target_pairs={{0,1},{1,0},{2,3},{3,2},{4,5},{5,4},{6,7},{7,6},{8,9},{9,8},{10,11... | collective-permute-start | bytes 6291464 | tf_op jit(solution)/shard_map/ppermute | solution.py:426
  464.7 2.6 copy-start.19
  511.7 97.5 %all-to-all-start.5 = ((bf16[16,16,16,512]{3,2,1,0:T(8,128)(2,1)}), bf16[16,16,16,512]{3,2,1,0:T(8,128)(2,1)}, u32[]{:S(2)}, u32[]{:S(2)}) async-start(bf16[16,16,16,512]{3,2,1,0:T(8,128)(2,1)} %hold.12), calls=%async_computation.5 | async-start | bytes 8388608 | tf_op jit(solution)/shard_map/all_to_all | solution.py:275
  531.6 70.8 %collective-permute-start.12 = (bf16[2048,512]{1,0:T(8,128)(2,1)}, bf16[2048,512]{1,0:T(8,128)(2,1)S(1)}, u32[]{:S(2)}, u32[]{:S(2)}) collective-permute-start(bf16[2048,512]{1,0:T(8,128)(2,1)} %get-tuple-element.73.refs_1_.refs_6_), channel_id=1, source_target_pairs={{0,1},{1,0},{2,3},{3,2},{4,5},{5,4},{6,7},{7,6},{8,9},{9,8},{10,11... | collective-permute-start | bytes 6291464 | tf_op jit(solution)/shard_map/ppermute | solution.py:426
  533.1 69.3 %collective-permute-start.13 = (bf16[1024,512]{1,0:T(8,128)(2,1)}, bf16[1024,512]{1,0:T(8,128)(2,1)S(1)}, u32[]{:S(2)}, u32[]{:S(2)}) collective-permute-start(bf16[1024,512]{1,0:T(8,128)(2,1)} %get-tuple-element.101), channel_id=1, source_target_pairs={{0,1},{1,0},{2,3},{3,2},{4,5},{5,4},{6,7},{7,6},{8,9},{9,8},{10,11... | collective-permute-start | bytes 3145736 | tf_op jit(solution)/shard_map/ppermute | solution.py:426
  609.3 67.9 %all-to-all-start.8 = ((bf16[16,8,16,512]{3,2,1,0:T(8,128)(2,1)}), bf16[16,8,16,512]{3,2,1,0:T(8,128)(2,1)S(1)}, u32[]{:S(2)}, u32[]{:S(2)}) async-start(bf16[16,8,16,512]{3,2,1,0:T(8,128)(2,1)} %hold.15), calls=%async_computation.8 | async-start | bytes 4194304 | tf_op jit(solution)/shard_map/all_to_all | solution.py:275
  628.9 48.3 %collective-permute-start.11 = (bf16[2048,512]{1,0:T(8,128)(2,1)}, bf16[2048,512]{1,0:T(8,128)(2,1)}, u32[]{:S(2)}, u32[]{:S(2)}) collective-permute-start(bf16[2048,512]{1,0:T(8,128)(2,1)} %get-tuple-element.78.refs_6_.refs_1_), channel_id=1, source_target_pairs={{0,1},{1,0},{2,3},{3,2},{4,5},{5,4},{6,7},{7,6},{8,9},{9,8},{10,11... | collective-permute-start | bytes 6291464 | tf_op jit(solution)/shard_map/ppermute | solution.py:426
  678.5 55.4 %all-to-all-start.7 = ((bf16[16,8,16,512]{3,2,1,0:T(8,128)(2,1)}), bf16[16,8,16,512]{3,2,1,0:T(8,128)(2,1)}, u32[]{:S(2)}, u32[]{:S(2)}) async-start(bf16[16,8,16,512]{3,2,1,0:T(8,128)(2,1)} %hold.14), calls=%async_computation.7 | async-start | bytes 4194304 | tf_op jit(solution)/shard_map/all_to_all | solution.py:275
  691.9 25.6 %collective-permute-start.14 = (bf16[1024,512]{1,0:T(8,128)(2,1)}, bf16[1024,512]{1,0:T(8,128)(2,1)S(1)}, u32[]{:S(2)}, u32[]{:S(2)}) collective-permute-start(bf16[1024,512]{1,0:T(8,128)(2,1)} %get-tuple-element.84), channel_id=1, source_target_pairs={{0,1},{1,0},{2,3},{3,2},{4,5},{5,4},{6,7},{7,6},{8,9},{9,8},{10,11... | collective-permute-start | bytes 3145736 | tf_op jit(solution)/shard_map/ppermute | solution.py:426
  733.9 54.1 %all-to-all-start.10 = ((bf16[16,8,16,512]{3,2,1,0:T(8,128)(2,1)}), bf16[16,8,16,512]{3,2,1,0:T(8,128)(2,1)S(1)}, u32[]{:S(2)}, u32[]{:S(2)}) async-start(bf16[16,8,16,512]{3,2,1,0:T(8,128)(2,1)} %hold.17), calls=%async_computation.10 | async-start | bytes 4194304 | tf_op jit(solution)/shard_map/all_to_all | solution.py:275
  739.7 26.2 %collective-permute-start.16 = (bf16[1024,512]{1,0:T(8,128)(2,1)}, bf16[1024,512]{1,0:T(8,128)(2,1)S(1)}, u32[]{:S(2)}, u32[]{:S(2)}) collective-permute-start(bf16[1024,512]{1,0:T(8,128)(2,1)} %get-tuple-element.86.rest_1_.refs_1_), channel_id=1, source_target_pairs={{0,1},{1,0},{2,3},{3,2},{4,5},{5,4},{6,7},{7,6},{8,9},{9,8},{10,11... | collective-permute-start | bytes 3145736 | tf_op jit(solution)/shard_map/ppermute | solution.py:426
  748.8 39.1 %collective-permute-start.15 = (bf16[1024,512]{1,0:T(8,128)(2,1)}, bf16[1024,512]{1,0:T(8,128)(2,1)}, u32[]{:S(2)}, u32[]{:S(2)}) collective-permute-start(bf16[1024,512]{1,0:T(8,128)(2,1)} %get-tuple-element.88), channel_id=1, source_target_pairs={{0,1},{1,0},{2,3},{3,2},{4,5},{5,4},{6,7},{7,6},{8,9},{9,8},{10,11... | collective-permute-start | bytes 3145736 | tf_op jit(solution)/shard_map/ppermute | solution.py:426
  765.9 22.0 %copy-start.15 = (bf16[1024,512]{1,0:T(8,128)(2,1)}, bf16[1024,512]{1,0:T(8,128)(2,1)S(1)}, u32[]{:S(2)}) copy-start(bf16[1024,512]{1,0:T(8,128)(2,1)S(1)} %collective-permute-done.16.refs_3_.got_ref) | copy-start | bytes 3145732
  789.4 47.2 %all-to-all-start.9 = ((bf16[16,8,16,512]{3,2,1,0:T(8,128)(2,1)}), bf16[16,8,16,512]{3,2,1,0:T(8,128)(2,1)}, u32[]{:S(2)}, u32[]{:S(2)}) async-start(bf16[16,8,16,512]{3,2,1,0:T(8,128)(2,1)} %hold.16), calls=%async_computation.9 | async-start | bytes 4194304 | tf_op jit(solution)/shard_map/all_to_all | solution.py:275
  803.1 42.6 %collective-permute-start.18 = (bf16[1024,512]{1,0:T(8,128)(2,1)}, bf16[1024,512]{1,0:T(8,128)(2,1)S(1)}, u32[]{:S(2)}, u32[]{:S(2)}) collective-permute-start(bf16[1024,512]{1,0:T(8,128)(2,1)} %get-tuple-element.95), channel_id=1, source_target_pairs={{0,1},{1,0},{2,3},{3,2},{4,5},{5,4},{6,7},{7,6},{8,9},{9,8},{10,11... | collective-permute-start | bytes 3145736 | tf_op jit(solution)/shard_map/ppermute | solution.py:426
  819.8 42.7 %collective-permute-start.19 = (bf16[1024,512]{1,0:T(8,128)(2,1)}, bf16[1024,512]{1,0:T(8,128)(2,1)S(1)}, u32[]{:S(2)}, u32[]{:S(2)}) collective-permute-start(bf16[1024,512]{1,0:T(8,128)(2,1)} %get-tuple-element.92.rest_0_), channel_id=1, source_target_pairs={{0,1},{1,0},{2,3},{3,2},{4,5},{5,4},{6,7},{7,6},{8,9},{9,8},{10,11... | collective-permute-start | bytes 3145736 | tf_op jit(solution)/shard_map/ppermute | solution.py:426
  844.2 30.0 %collective-permute-start.17 = (bf16[1024,512]{1,0:T(8,128)(2,1)}, bf16[1024,512]{1,0:T(8,128)(2,1)S(1)}, u32[]{:S(2)}, u32[]{:S(2)}) collective-permute-start(bf16[1024,512]{1,0:T(8,128)(2,1)} %get-tuple-element.94), channel_id=1, source_target_pairs={{0,1},{1,0},{2,3},{3,2},{4,5},{5,4},{6,7},{7,6},{8,9},{9,8},{10,11... | collective-permute-start | bytes 3145736 | tf_op jit(solution)/shard_map/ppermute | solution.py:426
  861.9 44.4 %collective-permute-start.21 = (bf16[1024,512]{1,0:T(8,128)(2,1)}, bf16[1024,512]{1,0:T(8,128)(2,1)S(1)}, u32[]{:S(2)}, u32[]{:S(2)}) collective-permute-start(bf16[1024,512]{1,0:T(8,128)(2,1)} %get-tuple-element.97.rest_0_), channel_id=1, source_target_pairs={{0,1},{1,0},{2,3},{3,2},{4,5},{5,4},{6,7},{7,6},{8,9},{9,8},{10,11... | collective-permute-start | bytes 3145736 | tf_op jit(solution)/shard_map/ppermute | solution.py:426
  862.5 11.7 %copy-start.16 = (bf16[1024,512]{1,0:T(8,128)(2,1)}, bf16[1024,512]{1,0:T(8,128)(2,1)S(1)}, u32[]{:S(2)}) copy-start(bf16[1024,512]{1,0:T(8,128)(2,1)S(1)} %collective-permute-done.19.rest_1_.got_ref) | copy-start | bytes 3145732
  890.5 28.2 %collective-permute-start.20 = (bf16[1024,512]{1,0:T(8,128)(2,1)}, bf16[1024,512]{1,0:T(8,128)(2,1)S(1)}, u32[]{:S(2)}, u32[]{:S(2)}) collective-permute-start(bf16[1024,512]{1,0:T(8,128)(2,1)} %get-tuple-element.99), channel_id=1, source_target_pairs={{0,1},{1,0},{2,3},{3,2},{4,5},{5,4},{6,7},{7,6},{8,9},{9,8},{10,11... | collective-permute-start | bytes 3145736 | tf_op jit(solution)/shard_map/ppermute | solution.py:426
  (18 other events, 22.0 us)
